TPU v7x, 256 devices: a whole 4x4x8 slice. The times are simulated.
256 devices in a mesh: link: 32 (over z, x), intv: 8 (over y, core).
Axes of the slice: x: 4, y: 4, z: 8, core: 2. Of those that a mesh axis runs over, the one named last changes fastest.
Arguments:
- slab: bfloat16 [256, 16, 262144], P('intv', None, 'link'), may hold values from -6 to 6
- interval_factor: float32 [256, 64], P('intv'), may hold values from -6 to 6
- day_factor: float32 [16, 64], replicated, may hold values from -6 to 6
Outputs:
- link_new: float32 [262144, 64], P(('link', 'intv'))
- interval_new: float32 [256, 64], P('intv')
- day_new: float32 [16, 64], replicated
All inputs are finite; a program needn't handle non-finite values.
Results may differ from a plain program's by a relative error of at most 0.0024.
The roundings to bfloat16 on the way count: a program that leaves them out, or rounds other values in their place, can miss the bound.
Values may be sent and summed in bfloat16 or wider, within the bound.
No kernel may reach another device: no remote copies, remote signals or barrier semaphores. Data moves between devices by JAX's collectives and lax.ppermute only.
A program may use at most 64 MiB of HBM per device.

v0:
```python
import jax
import jax.numpy as jnp
from jax import lax
from jax.sharding import PartitionSpec as P


def solve_rows(system, rhs):
    rank = system.shape[0]
    shifted = system + 0.01 * jnp.trace(system) / rank * jnp.eye(rank, dtype=system.dtype)
    factor = jnp.linalg.cholesky(shifted)
    return jax.scipy.linalg.cho_solve((factor, True), rhs.T).T


def gram_of(matrix):
    return jnp.dot(matrix.T, matrix, precision=lax.Precision.HIGHEST)


def body(slab, interval_factor, day_factor):
    intervals, days, links = slab.shape
    rank = day_factor.shape[1]
    flat = slab.reshape(intervals * days, links)
    gram_day = gram_of(day_factor)
    gram_interval = lax.psum(gram_of(interval_factor), "intv")
    khatri = (
        (interval_factor[:, None, :] * day_factor[None, :, :])
        .reshape(intervals * days, rank)
        .astype(jnp.bfloat16)
    )
    system_link = gram_interval * gram_day
    owned_sums = lax.psum_scatter(
        lax.dot_general(flat, khatri, (((0,), (0,)), ((), ())), preferred_element_type=jnp.float32),
        "intv",
        scatter_dimension=0,
        tiled=True,
    )
    link_new = solve_rows(system_link, owned_sums)
    gram_link = lax.psum(gram_of(link_new), ("link", "intv"))
    link_block = lax.all_gather(link_new.astype(jnp.bfloat16), "intv", axis=0, tiled=True)
    partial_sums = jnp.dot(flat, link_block, preferred_element_type=jnp.float32).reshape(
        intervals, days, rank
    )
    interval_part = jnp.sum(partial_sums * day_factor[None, :, :], axis=1)
    interval_sums = lax.psum(interval_part, "link")
    interval_new = solve_rows(gram_link * gram_day, interval_sums)
    gram_new = lax.psum(gram_of(interval_new), "intv")
    day_part = jnp.sum(partial_sums * interval_new[:, None, :], axis=0)
    day_sums = lax.psum(day_part, ("link", "intv"))
    day_new = solve_rows(gram_link * gram_new, day_sums)
    return (link_new, interval_new, day_new)


def solution(mesh):
    placed = (P("intv", None, "link"), P("intv", None), P())
    return jax.shard_map(
        body,
        mesh=mesh,
        in_specs=placed,
        out_specs=(P(("link", "intv"), None), P("intv", None), P()),
        check_vma=False,
    )
```

profile of v0, /device:TPU:1, one launch (start us, length us, event | category | flops | bytes accessed | tf_op | source)
XLA Modules:
  0.0 411.1 jit_solution(11994552276993962413)
XLA Ops:
  7.2 0.0 reduce-scatter.2.cloned.1.call-start
  7.2 6.4 %convolution_bitcast_fusion = f32[8192,64]{0,1:T(8,128)} fusion(bf16[32,16,8192]{2,1,0:T(8,128)(2,1)} %param.4, f32[16,64]{1,0:T(8,128)} %param.6, f32[32,64]{1,0:T(8,128)} %param.5), kind=kOutput, calls=%fused_computation | convolution fusion | flops 536936448 | bytes 10498048 | tf_op jit(solution)/shard_map/dot_general | solution.py:31
  13.6 0.0 reduce-scatter.2.cloned.1.call-update
  13.6 0.0 all-gather.2.cloned.1.call-start
  13.7 0.2 fusion.32
  13.9 23.8 %psum.35 = f32[64,64]{1,0:T(8,128)S(1)} all-reduce(f32[64,64]{1,0:T(8,128)S(1)} %fusion.32), channel_id=1, replica_groups=mesh['link'=32,'intv'=8] {'intv'}, use_global_device_ids=true, to_apply=%region_0.0 | all-reduce | flops 4096 | bytes 32768 | tf_op jit(solution)/shard_map/psum | solution.py:23
  37.8 0.8 fusion.26
  39.3 0.1 copy.15
  39.4 0.1 copy.16
  39.5 5.9 %cholesky.59 = f32[64,64]{1,0:T(8,128)S(1)} custom-call(f32[64,64]{1,0:T(8,128)S(1)} %copy.16), custom_call_target="Cholesky" | custom-call | tf_op jit(solution)/shard_map/jit(cholesky)/cholesky | solution.py:10
  45.4 0.6 compare_reduce_fusion.2
  46.0 0.7 fusion.2
  46.7 4.9 %custom-call.23 = f32[1,64,64]{1,2,0:T(8,128)S(1)} custom-call(f32[1,64,64]{2,1,0:T(8,128)S(1)} %fusion.2), custom_call_target="InvertDiagBlocksLowerTriangular" | custom-call | tf_op jit(solution)/shard_map/jit(_cho_solve)/triangular_solve | solution.py:11
  51.6 0.0 reduce-scatter.2.cloned.1.call-done
  51.6 1.4 fusion.17
  53.0 0.4 fusion.15
  53.3 0.0 copy-start
  53.3 0.7 bitcast_convert_fusion
  54.1 0.0 all-gather.2.cloned.1.call-update
  54.1 0.4 fusion.33
  54.5 81.6 %psum.36 = f32[64,64]{1,0:T(8,128)S(1)} all-reduce(f32[64,64]{1,0:T(8,128)S(1)} %fusion.33), channel_id=1, replica_groups=mesh['link'=32,'intv'=8] {'link','intv'}, use_global_device_ids=true, to_apply=%region_5.7 | all-reduce | flops 4096 | bytes 32768 | tf_op jit(solution)/shard_map/psum | solution.py:37
  136.1 0.6 fusion.28
  137.4 0.1 copy.17
  137.5 0.1 copy.18
  137.5 5.9 %cholesky.70 = f32[64,64]{1,0:T(8,128)S(1)} custom-call(f32[64,64]{1,0:T(8,128)S(1)} %copy.18), custom_call_target="Cholesky" | custom-call | tf_op jit(solution)/shard_map/jit(cholesky)/cholesky | solution.py:10
  143.4 0.6 compare_reduce_fusion.1
  144.1 0.7 fusion.3
  144.7 4.9 %custom-call.24 = f32[1,64,64]{1,2,0:T(8,128)S(1)} custom-call(f32[1,64,64]{2,1,0:T(8,128)S(1)} %fusion.3), custom_call_target="InvertDiagBlocksLowerTriangular" | custom-call | tf_op jit(solution)/shard_map/jit(_cho_solve)/triangular_solve | solution.py:11
  149.6 0.0 all-gather.2.cloned.1.call-done
  149.7 6.4 %convolution_bitcast_fusion.1 = f32[512,64]{0,1:T(8,128)S(1)} fusion(bf16[8192,64]{0,1:T(8,128)(2,1)} %all-gather.2.cloned.1.call-done, bf16[512,8192]{1,0:T(8,128)(2,1)} %bitcast.62), kind=kOutput, calls=%fused_computation.1 | convolution fusion | flops 536870912 | bytes 9568256 | tf_op jit(solution)/shard_map/dot_general | solution.py:39
  156.0 0.1 copy.19
  156.2 0.1 multiply_reduce_fusion.1
  156.2 111.4 %psum.37 = f32[32,64]{1,0:T(8,128)S(1)} all-reduce(f32[32,64]{1,0:T(8,128)S(1)} %multiply_reduce_fusion.1), channel_id=1, replica_groups=mesh['link'=32,'intv'=8] {'link'}, use_global_device_ids=true, to_apply=%region_8.10 | all-reduce | flops 2048 | bytes 16384 | tf_op jit(solution)/shard_map/psum | solution.py:43
  267.7 0.2 fusion.12
  267.9 0.2 fusion.10
  268.1 0.0 copy-start.2
  268.1 0.2 fusion.34
  268.4 100.3 %psum.39 = f32[16,64]{1,0:T(8,128)S(1)} all-reduce(f32[16,64]{1,0:T(8,128)S(1)} %multiply_reduce_fusion), channel_id=1, replica_groups=mesh['link'=32,'intv'=8] {'link','intv'}, use_global_device_ids=true, to_apply=%region_12.14 | all-reduce | flops 1024 | bytes 8192 | tf_op jit(solution)/shard_map/psum | solution.py:47
  368.7 20.9 %psum.38 = f32[64,64]{1,0:T(8,128)S(1)} all-reduce(f32[64,64]{1,0:T(8,128)S(1)} %fusion.34), channel_id=1, replica_groups=mesh['link'=32,'intv'=8] {'intv'}, use_global_device_ids=true, to_apply=%region_9.11 | all-reduce | flops 4096 | bytes 32768 | tf_op jit(solution)/shard_map/psum | solution.py:45
  389.6 0.6 fusion.30
  390.9 0.1 copy.20
  391.0 0.1 copy.21
  391.1 5.9 %cholesky.81 = f32[64,64]{1,0:T(8,128)S(1)} custom-call(f32[64,64]{1,0:T(8,128)S(1)} %copy.21), custom_call_target="Cholesky" | custom-call | tf_op jit(solution)/shard_map/jit(cholesky)/cholesky | solution.py:10
  397.0 0.6 compare_reduce_fusion
  397.6 0.7 fusion.4
  398.3 4.9 %custom-call.25 = f32[1,64,64]{1,2,0:T(8,128)S(1)} custom-call(f32[1,64,64]{2,1,0:T(8,128)S(1)} %fusion.4), custom_call_target="InvertDiagBlocksLowerTriangular" | custom-call | tf_op jit(solution)/shard_map/jit(_cho_solve)/triangular_solve | solution.py:11
  403.2 0.3 fusion.7
  403.5 0.8 fusion.5
  (16 shorter events, 0.2 us)
Async XLA Ops:
  7.2 30.6 %copy-start.3 = (f32[16,64]{1,0:T(8,128)S(1)}, f32[16,64]{1,0:T(8,128)}, u32[]{:S(2)}) copy-start(f32[16,64]{1,0:T(8,128)} %param.6) | copy-start | bytes 12292
  7.2 6.5 %copy-start.1 = (f32[32,64]{1,0:T(8,128)S(1)}, f32[32,64]{1,0:T(8,128)}, u32[]{:S(2)}) copy-start(f32[32,64]{1,0:T(8,128)} %param.5) | copy-start | bytes 24580
  7.2 44.4 %reduce-scatter.2.cloned.1.call-start = ((), (), s32[]{:S(2)}) async-start(), calls=%async_computation.1 | async-start | bytes 2359296 | tf_op jit(solution)/shard_map/reduce_scatter | solution.py:30
  13.6 136.0 %all-gather.2.cloned.1.call-start = ((), (), s32[]{:S(2)}) async-start(), calls=%async_computation.2 | async-start | bytes 1179648 | tf_op jit(solution)/shard_map/all_gather | solution.py:38
  53.3 350.9 %copy-start = (f32[64,1024]{1,0:T(8,128)}, f32[64,1024]{1,0:T(8,128)S(1)}, u32[]{:S(2)}) copy-start(f32[64,1024]{1,0:T(8,128)S(1)} %fusion.15) | copy-start | bytes 786436
  268.1 136.2 %copy-start.2 = (f32[64,32]{0,1:T(8,128)}, f32[64,32]{0,1:T(8,128)S(1)}, u32[]{:S(2)}) copy-start(f32[64,32]{0,1:T(8,128)S(1)} %fusion.10) | copy-start | bytes 24580
Sparse Core Ops, SparseCore 0:
  13.8 37.5 reduce-scatter.1
  54.2 29.5 all-gather.1
where the time goes:
time: 414 us; the launch traced here: 411 us
  blocking collectives  338 us (82%)
  other arithmetic  38.4 us (9%)
  matrix products  17.7 us (4%)
  between operations  16.2 us (4%)
    psum x1, blocking collectives, body(): interval_sums = lax.psum(interval_part, 'link')  111 us
    psum x1, blocking collectives, body(): day_sums = lax.psum(day_part, ('link', 'intv'))  100 us
    psum x1, blocking collectives, body(): gram_link = lax.psum(gram_of(link_new), ('link', 'intv'))  81.6 us
    psum x1, blocking collectives, body(): gram_interval = lax.psum(gram_of(interval_factor), 'intv')  23.8 us
    psum x1, blocking collectives, body(): gram_new = lax.psum(gram_of(interval_new), 'intv')  20.9 us
    another operation x9, other arithmetic, solve_rows(): factor = jnp.linalg.cholesky(shifted)  19.6 us
    another operation x6, other arithmetic, solve_rows(): return jax.scipy.linalg.cho_solve((factor, True), rhs.T).T  16.6 us
  transfers between devices with their start and end apart: 2, of which 0 were waited for; matrix products, arithmetic and copies ran while one was open for 6% of the time, Pallas kernels for 0%

commit v1 on v0

v1 whole, which is shorter than its diff:
```python
import functools

import jax
import jax.numpy as jnp
from jax import lax
from jax.experimental import pallas as pl
from jax.experimental.pallas import tpu as pltpu
from jax.sharding import Mesh, PartitionSpec as P

RANK = 64
HIGH = lax.Precision.HIGHEST
F32 = jnp.float32
BF16 = jnp.bfloat16
VMEM = pl.BlockSpec(memory_space=pltpu.VMEM)


def shifts(n, d):
    return [(i, (i + d) % n) for i in range(n)]


def iota(shape, dim):
    return lax.broadcasted_iota(jnp.int32, shape, dim)


def dot(a, b, contract=((1,), (0,)), precision=HIGH):
    return lax.dot_general(a, b, (contract, ((), ())), precision=precision, preferred_element_type=F32)


def shifted(system):
    eye = iota((RANK, RANK), 0) == iota((RANK, RANK), 1)
    trace = jnp.sum(jnp.sum(jnp.where(eye, system, 0.0), axis=1, keepdims=True), axis=0, keepdims=True)
    return system + jnp.where(eye, 0.01 * trace / RANK, 0.0)


def eliminate(system, rhs):
    work = jnp.concatenate([system, rhs], axis=1)
    row = iota((RANK, 1), 0)
    for k in range(RANK):
        column = work[:, k : k + 1]
        pivot_row = work[k : k + 1, :] / work[k : k + 1, k : k + 1]
        work = jnp.where(row == k, pivot_row, work - column * pivot_row)
    return work


def first_sums_kernel(blocks, slab_ref, interval_ref, day_ref, sums_ref, khatri_ref, gram_ref):
    @pl.when(pl.program_id(0) == 0)
    def _():
        factor = interval_ref[...]
        product = factor[:, None, :] * day_ref[...][None, :, :]
        khatri_ref[...] = product.reshape(product.shape[0] * product.shape[1], RANK).T.astype(BF16)
        gram_ref[...] = dot(factor, factor, ((0,), (0,)))

    sums_ref[0] = dot(khatri_ref[...], slab_ref[...], precision=None)


def second_sums_kernel(blocks, slab_ref, khatri_ref, sums_ref):
    sums_ref[0] = dot(khatri_ref[...], slab_ref[...], precision=None)


def inverse_kernel(gram0, gram1, gram2, gram3, day_ref, out_ref):
    gram = (gram0[...] + gram1[...]) + (gram2[...] + gram3[...])
    gram_day = dot(day_ref[...], day_ref[...], ((0,), (0,)))
    eye = jnp.where(iota((RANK, RANK), 0) == iota((RANK, RANK), 1), 1.0, 0.0).astype(F32)
    out_ref[...] = eliminate(shifted(gram * gram_day), eye)[:, RANK:]


def link_kernel(sum0, sum1, sum2, sum3, inverse_ref, link_ref, low_ref, gram_ref):
    sums = (sum0[...] + sum1[...]) + (sum2[...] + sum3[...])
    link = dot(inverse_ref[...], sums)
    link_ref[...] = link
    low_ref[...] = link.astype(BF16)
    gram_ref[...] = dot(link, link, ((1,), (1,)))


def add_block(lows, slab_ref, acc):
    for i, low in enumerate(lows):

        @pl.when(pl.program_id(0) == i)
        def _():
            acc[...] += dot(low[...], slab_ref[...], ((1,), (1,)), None)


def first_partial_kernel(blocks, low0, low1, low2, low3, slab_ref, acc):
    @pl.when(pl.program_id(0) == 0)
    def _():
        acc[...] = jnp.zeros_like(acc)

    add_block((low0, low1, low2, low3), slab_ref, acc)


def second_partial_kernel(blocks, low0, low1, low2, low3, slab_ref, before, gram0, gram1, out_ref, acc):
    @pl.when(pl.program_id(0) == 0)
    def _():
        acc[...] = before[...]

    add_block((low0, low1, low2, low3), slab_ref, acc)

    @pl.when(pl.program_id(0) == 3)
    def _():
        gram = gram0[...] + gram1[...]
        packed = jnp.concatenate([gram[: RANK // 2], gram[RANK // 2 :]], axis=1)
        for d in range(4):
            at = pl.multiple_of(lax.rem(blocks[4] + d, 4) * 128, 128)
            out_ref[d, :RANK] = acc[:, pl.ds(at, 128)]
            out_ref[d, RANK:] = packed


def interval_kernel(recv_ref, day_ref, out_ref, gram_ref):
    total = recv_ref[0]
    for i in range(1, recv_ref.shape[0]):
        total = total + recv_ref[i]
    partial = total[:RANK]
    packed = total[RANK:]
    gram = jnp.concatenate([packed[:, :RANK], packed[:, RANK:]], axis=0)
    gram_ref[...] = gram
    day = day_ref[...]
    gram_day = dot(day, day, ((0,), (0,)))
    of_day = jnp.where(lax.rem(iota((16, 128), 1), 16) == iota((16, 128), 0), 1.0, 0.0).astype(F32)
    of_interval = jnp.where(lax.div(iota((8, 128), 1), 16) == iota((8, 128), 0), 1.0, 0.0).astype(F32)
    day_lanes = dot(day, of_day, ((0,), (0,)))
    interval_sums = dot(partial * day_lanes, of_interval, ((1,), (1,)))
    rhs = jnp.concatenate([interval_sums, jnp.zeros((RANK, 56), F32)], axis=1)
    solved = eliminate(shifted(gram * gram_day), rhs)
    interval_new = solved[:, RANK : RANK + 8]
    day_part = dot(of_day, partial * dot(interval_new, of_interval), ((1,), (1,)))
    rows = jnp.transpose(solved)[RANK : RANK + 8]
    payload = jnp.concatenate(
        [
            jnp.concatenate([day_part[:8], day_part[8:]], axis=1),
            jnp.concatenate([rows, jnp.zeros((8, RANK), F32)], axis=1),
        ],
        axis=0,
    )
    for i in range(out_ref.shape[0]):
        out_ref[i] = payload


def day_kernel(place, recv_ref, gram_ref, interval_ref, day_ref):
    total = recv_ref[0, :8]
    for i in range(1, 32):
        total = total + recv_ref[i, :8]
    rows = recv_ref[:, 8:, :RANK].reshape(256, RANK)
    gram_new = dot(rows, rows, ((0,), (0,)))
    for i in range(4):
        interval_ref[i * 8 : i * 8 + 8] = recv_ref[i * 8 + place[0], 8:, :RANK]
    turned = jnp.transpose(total)
    rhs = jnp.concatenate([turned[:RANK], turned[RANK:], jnp.zeros((RANK, 48), F32)], axis=1)
    solved = eliminate(shifted(gram_ref[...] * gram_new), rhs)
    day_ref[...] = jnp.transpose(solved)[RANK : RANK + 16]


def shape(dims, dtype=F32):
    return jax.ShapeDtypeStruct(dims, dtype)


def slab_call(kernel, blocks, args, in_specs, out_shape, out_specs, name, scratch=()):
    return pl.pallas_call(
        kernel,
        out_shape=out_shape,
        grid_spec=pltpu.PrefetchScalarGridSpec(
            num_scalar_prefetch=1, grid=(4,), in_specs=in_specs, out_specs=out_specs, scratch_shapes=scratch
        ),
        compiler_params=pltpu.CompilerParams(vmem_limit_bytes=32 * 2**20),
        cost_estimate=pl.CostEstimate(flops=2 * 512 * 4096 * 64, bytes_accessed=6 * 2**20, transcendentals=0),
        name=name,
    )(blocks, *args)


def small_call(kernel, out_shape, args, name):
    return pl.pallas_call(
        kernel,
        out_shape=out_shape,
        in_specs=[VMEM] * len(args),
        out_specs=jax.tree.map(lambda _: VMEM, out_shape),
        cost_estimate=pl.CostEstimate(flops=2**26, bytes_accessed=2**20, transcendentals=0),
        name=name,
    )(*args)


def body(slab, interval_factor, day_factor):
    intervals, days, links = slab.shape
    flat = slab.reshape(intervals * days, links)
    y, c, x = lax.axis_index("y"), lax.axis_index("core"), lax.axis_index("x")
    ahead = lax.rem(y + jnp.arange(4, dtype=jnp.int32), 4)
    behind = lax.rem(y + 4 - jnp.arange(4, dtype=jnp.int32), 4)

    def blocks(of_y, of_c):
        return jnp.concatenate([2 * of_y + of_c, x[None]]).astype(jnp.int32)

    def whole(dims):
        return pl.BlockSpec(dims, lambda i, b: (0,) * len(dims))

    slab_spec = pl.BlockSpec((512, 1024), lambda i, b: (0, b[i]))
    sums_spec = pl.BlockSpec((1, RANK, 1024), lambda i, b: (i, 0, 0))
    send, khatri, gram_part = slab_call(
        first_sums_kernel,
        blocks(ahead, 1 - c),
        (flat, interval_factor, day_factor),
        [slab_spec, whole((32, RANK)), whole((16, RANK))],
        (shape((4, RANK, 1024)), shape((RANK, 512), BF16), shape((RANK, RANK))),
        (sums_spec, whole((RANK, 512)), whole((RANK, RANK))),
        "sums_to_send",
    )
    got = lax.ppermute(send, "core", shifts(2, 1))
    gram_pair = gram_part + lax.ppermute(gram_part, "core", shifts(2, 1))
    gram_parts = [gram_pair] + [lax.ppermute(gram_pair, "y", shifts(4, d)) for d in (1, 2, 3)]
    keep = slab_call(
        second_sums_kernel,
        blocks(ahead, c),
        (flat, khatri),
        [slab_spec, whole((RANK, 512))],
        shape((4, RANK, 1024)),
        sums_spec,
        "sums_to_keep",
    )
    sums = [keep[d] + got[d] for d in range(4)]
    sums = [sums[0]] + [lax.ppermute(sums[d], "y", shifts(4, d)) for d in (1, 2, 3)]
    inverse = small_call(inverse_kernel, shape((RANK, RANK)), (*gram_parts, day_factor), "link_inverse")
    link, low, gram_link = small_call(
        link_kernel,
        (shape((RANK, 1024)), shape((RANK, 1024), BF16), shape((RANK, RANK))),
        (*sums, inverse),
        "link_rows",
    )
    lows = [low] + [lax.ppermute(low, "y", shifts(4, d)) for d in (1, 2, 3)]
    gram_link = sum([lax.ppermute(gram_link, "y", shifts(4, d)) for d in (1, 2, 3)], gram_link)
    gram_other = lax.ppermute(gram_link, "core", shifts(2, 1))
    lows_other = [lax.ppermute(one, "core", shifts(2, 1)) for one in lows]
    acc_spec = whole((RANK, 512))
    low_specs = [whole((RANK, 1024))] * 4
    before = slab_call(
        first_partial_kernel,
        blocks(behind, c),
        (*lows, flat),
        low_specs + [slab_spec],
        shape((RANK, 512)),
        acc_spec,
        "partial_own_core",
    )
    outgoing = slab_call(
        second_partial_kernel,
        blocks(behind, 1 - c),
        (*lows_other, flat, before, gram_link, gram_other),
        low_specs + [slab_spec, acc_spec, whole((RANK, RANK)), whole((RANK, RANK))],
        shape((4, 96, 128)),
        whole((4, 96, 128)),
        "partial_other_core",
        [pltpu.VMEM((RANK, 512), F32)],
    )
    over_x = sum([lax.ppermute(outgoing[d], "x", shifts(4, d)) for d in (1, 2, 3)], outgoing[0])
    over_z = lax.all_to_all(jnp.broadcast_to(over_x[None], (8, 96, 128)), "z", 0, 0)
    outgoing, gram_link = small_call(
        interval_kernel, (shape((32, 16, 128)), shape((RANK, RANK))), (over_z, day_factor), "interval_rows"
    )
    everyone = lax.all_to_all(outgoing, ("x", "y", "core"), 0, 0)
    interval_new, day_new = pl.pallas_call(
        day_kernel,
        out_shape=(shape((32, RANK)), shape((16, RANK))),
        in_specs=[pl.BlockSpec(memory_space=pltpu.SMEM), VMEM, VMEM],
        out_specs=(VMEM, VMEM),
        name="day_rows",
    )((2 * y + c).astype(jnp.int32)[None], everyone, gram_link)
    return link.T, interval_new, day_new


def solution(mesh):
    split = Mesh(mesh.devices.reshape(8, 4, 4, 2), ("z", "x", "y", "core"))
    link, intv = ("z", "x"), ("y", "core")
    return jax.shard_map(
        body,
        mesh=split,
        in_specs=(P(intv, None, link), P(intv, None), P()),
        out_specs=(P(link + intv, None), P(intv, None), P()),
        check_vma=False,
    )
```

time: 414 us -> 132 us (0.32)
  blocking collectives: 338 us -> 21.5 us
  other arithmetic: 38.4 us -> 1.98 us
  Pallas kernels: 0 us -> 35.1 us
  starting transfers between devices: 0.08 us -> 32.9 us
  waiting for transfers between devices: 0.09 us -> 28 us
  matrix products: 17.7 us -> 0 us
  between operations: 16.2 us -> 0.84 us
  local copies, waits for them, and re-layouts: 0.59 us -> 11.3 us
    psum x5 -> x0, blocking collectives: 338 us -> none  [the longest x1 111 us: body(): interval_sums = lax.psum(interval_part, 'link')]
    another operation x15 -> x0, other arithmetic: 36.2 us -> none  [the longest x9 19.6 us: solve_rows(): factor = jnp.linalg.cholesky(shifted)]
    pallas_call x0 -> x8, Pallas kernels: none -> 35.1 us  [the longest x3 17.9 us: small_call(): pl.pallas_call(kernel, out_shape=out_shape, in_specs=[VMEM] * len(args),...]
    ppermute x0 -> x22, starting transfers between devices: none -> 27.1 us  [the longest x4 4.45 us: body(): lows_other = [lax.ppermute(one, 'core', shifts(2, 1)) for one in lows]]
    all_to_all x0 -> x1, blocking collectives: none -> 21.5 us  [body(): lax.all_to_all(jnp.broadcast_to(over_x[None], (8, 96, 128)), 'z', 0, 0)]
    ppermute x0 -> x22, waiting for transfers between devices: none -> 18.9 us  [the longest x3 10.6 us: body(): lax.ppermute(gram_pair, 'y', shifts(4, d))]
    dot_general x6 -> x0, matrix products: 14.4 us -> none  [the longest x1 6.38 us: body(): lax.dot_general(flat, khatri, (((0,), (0,)), ((), ())), preferred_element...]
    unnamed x8 -> x28, local copies, waits for them, and re-layouts: 0.02 us -> 11.3 us
  transfers between devices with their start and end apart: 2 -> 23, of which waited for: 0 -> 10; matrix products, arithmetic and copies ran while one was open for 6% -> 1% of each run, Pallas kernels for 0% -> 9%
where the time goes in v1:
time: 132 us
  Pallas kernels  35.1 us (27%)
  starting transfers between devices  32.9 us (25%)
  waiting for transfers between devices  28 us (21%)
  blocking collectives  21.5 us (16%)
  local copies, waits for them, and re-layouts  11.3 us (9%)
  other arithmetic  1.98 us (2%)
    all_to_all x1, blocking collectives, body(): lax.all_to_all(jnp.broadcast_to(over_x[None], (8, 96, 128)), 'z', 0, 0)  21.5 us
    pallas_call x3, Pallas kernels, small_call(): pl.pallas_call(kernel, out_shape=out_shape, in_specs=[VMEM] * len(args),...  17.9 us
    unnamed x28, local copies, waits for them, and re-layouts  11.3 us
    ppermute x3, waiting for transfers between devices, body(): lax.ppermute(gram_pair, 'y', shifts(4, d))  10.6 us
    pallas_call x4, Pallas kernels, slab_call(): pl.pallas_call(kernel, out_shape=out_shape, grid_spec=pltpu.PrefetchScala...  9.86 us
    all_to_all x1, waiting for transfers between devices, body(): everyone = lax.all_to_all(outgoing, ('x', 'y', 'core'), 0, 0)  9.09 us
    pallas_call x1, Pallas kernels, body(): pl.pallas_call(day_kernel, out_shape=(shape((32, RANK)), shape((16, RANK)...  7.4 us
    all_to_all x1, starting transfers between devices, body(): everyone = lax.all_to_all(outgoing, ('x', 'y', 'core'), 0, 0)  5.74 us
  transfers between devices with their start and end apart: 23, of which 10 were waited for; matrix products, arithmetic and copies ran while one was open for 1% of the time, Pallas kernels for 9%

profile of v1, /device:TPU:1, one launch (start us, length us, event | category | flops | bytes accessed | tf_op | source)
XLA Modules:
  0.0 131.6 jit_solution(15263638847954446198)
XLA Ops:
  0.7 3.4 %copy-done = bf16[32,16,8192]{2,1,0:T(8,128)(2,1)S(1)} copy-done((bf16[32,16,8192]{2,1,0:T(8,128)(2,1)S(1)}, bf16[32,16,8192]{2,1,0:T(8,128)(2,1)}, u32[]{:S(2)}) %copy-start) | copy-done | bytes 8388632
  4.1 0.7 copy-done.4
  4.8 0.7 copy-done.5
  5.5 2.3 %sums_to_send.1 = (f32[4,64,1024]{2,1,0:T(8,128)S(1)}, bf16[64,512]{1,0:T(8,128)(2,1)S(1)}, f32[64,64]{1,0:T(8,128)S(1)}) custom-call(s32[5]{0:T(128)S(1)} %pad_add_fusion.1.blocks, bf16[512,8192]{1,0:T(8,128)(2,1)S(1)} %bitcast.26, f32[32,64]{1,0:T(8,128)S(1)} %copy-done.5, f32[16,64]{1,0:T(8,128)S(1)} %copy-done.4), custom_call_target="tpu_custom_call" | custom-call | flops 268435456 | bytes 6291456 | tf_op jit(solution)/shard_map/sums_to_send/pallas_call | solution.py:157
  7.9 3.3 %collective-permute-start = (f32[4,64,1024]{2,1,0:T(8,128)S(1)}, f32[4,64,1024]{2,1,0:T(8,128)S(1)}, u32[]{:S(2)}, u32[]{:S(2)}) collective-permute-start(f32[4,64,1024]{2,1,0:T(8,128)S(1)} %get-tuple-element.14), channel_id=1, source_target_pairs={{0,1},{1,0},{2,3},{3,2},{4,5},{5,4},{6,7},{7,6},{8,9},{9,8},{10,11... | collective-permute-start | bytes 3145736 | tf_op jit(solution)/shard_map/ppermute | solution.py:204
  11.3 2.1 %sums_to_keep.1 = f32[4,64,1024]{2,1,0:T(8,128)S(1)} custom-call(s32[5]{0:T(128)S(1)} %pad_add_fusion.blocks, bf16[512,8192]{1,0:T(8,128)(2,1)S(1)} %bitcast.27, bf16[64,512]{1,0:T(8,128)(2,1)S(1)} %get-tuple-element.13.khatri_ref), custom_call_target="tpu_custom_call" | custom-call | flops 268435456 | bytes 6291456 | tf_op jit(solution)/shard_map/sums_to_keep/pallas_call | solution.py:157
  13.4 0.1 collective-permute-done
  13.5 0.9 fusion
  14.3 2.3 %collective-permute-start.2 = (f32[64,1024]{1,0:T(8,128)S(1)}, f32[64,1024]{1,0:T(8,128)S(1)}, u32[]{:S(2)}, u32[]{:S(2)}) collective-permute-start(f32[64,1024]{1,0:T(8,128)S(1)} %get-tuple-element.24), channel_id=1, source_target_pairs={{0,4},{2,6},{4,0},{6,2},{1,5},{3,7},{5,1},{7,3},{8,12},{10,14},{12... | collective-permute-start | bytes 786440 | tf_op jit(solution)/shard_map/ppermute | solution.py:217
  16.6 1.1 collective-permute-start.3
  17.7 1.5 %collective-permute-start.4 = (f32[64,64]{1,0:T(8,128)S(1)}, f32[64,64]{1,0:T(8,128)S(1)}, u32[]{:S(2)}, u32[]{:S(2)}) collective-permute-start(f32[64,64]{1,0:T(8,128)S(1)} %get-tuple-element.15), channel_id=1, source_target_pairs={{0,1},{1,0},{2,3},{3,2},{4,5},{5,4},{6,7},{7,6},{8,9},{9,8},{10,11... | collective-permute-start | bytes 49160 | tf_op jit(solution)/shard_map/ppermute | solution.py:205
  19.2 0.9 collective-permute-done.4
  20.1 0.4 collective-permute-start.5
  20.5 1.5 %collective-permute-start.6 = (f32[64,64]{1,0:T(8,128)S(1)}, f32[64,64]{1,0:T(8,128)S(1)}, u32[]{:S(2)}, u32[]{:S(2)}) collective-permute-start(f32[64,64]{1,0:T(8,128)S(1)} %add.90.gram0), channel_id=1, source_target_pairs={{0,4},{2,6},{4,0},{6,2},{1,5},{3,7},{5,1},{7,3},{8,12},{10,14},{12... | collective-permute-start | bytes 49160 | tf_op jit(solution)/shard_map/ppermute | solution.py:206
  22.0 7.9 %collective-permute-done.5.gram1 = f32[64,64]{1,0:T(8,128)S(1)} collective-permute-done((f32[64,64]{1,0:T(8,128)S(1)}, f32[64,64]{1,0:T(8,128)S(1)}, u32[]{:S(2)}, u32[]{:S(2)}) %collective-permute-start.5) | collective-permute-done | bytes 16416 | tf_op jit(solution)/shard_map/ppermute | solution.py:206
  29.9 2.7 %collective-permute-done.7.gram3 = f32[64,64]{1,0:T(8,128)S(1)} collective-permute-done((f32[64,64]{1,0:T(8,128)S(1)}, f32[64,64]{1,0:T(8,128)S(1)}, u32[]{:S(2)}, u32[]{:S(2)}) %collective-permute-start.7) | collective-permute-done | bytes 16416 | tf_op jit(solution)/shard_map/ppermute | solution.py:206
  32.7 0.6 copy-done.13
  33.3 7.2 %link_inverse.1.inverse_ref = f32[64,64]{1,0:T(8,128)} custom-call(f32[64,64]{1,0:T(8,128)} %copy-done.10, f32[64,64]{1,0:T(8,128)} %copy-done.11, f32[64,64]{1,0:T(8,128)} %copy-done.12, f32[64,64]{1,0:T(8,128)} %copy-done.13, f32[16,64]{1,0:T(8,128)} %day_ref.5), custom_call_target="tpu_custom_call" | custom-call | flops 67108864 | bytes 1048576 | tf_op jit(solution)/shard_map/link_inverse/pallas_call | solution.py:170
  40.6 0.7 copy-done.7
  41.3 0.1 copy-done.8
  41.4 2.6 %link_rows.1 = (f32[64,1024]{1,0:T(8,128)}, bf16[64,1024]{1,0:T(8,128)(2,1)}, f32[64,64]{1,0:T(8,128)}) custom-call(f32[64,1024]{1,0:T(8,128)} %get-tuple-element.26.sum0, f32[64,1024]{1,0:T(8,128)} %copy-done.7, f32[64,1024]{1,0:T(8,128)} %copy-done.8, f32[64,1024]{1,0:T(8,128)} %copy-done.9, f32[64,64]{1,0:T(8,128)} %link_inverse.1.inverse_ref), custom_call_target="tpu_custom_call" | custom-call | flops 67108864 | bytes 1048576 | tf_op jit(solution)/shard_map/link_rows/pallas_call | solution.py:170
  44.0 2.4 %collective-permute-start.11 = (bf16[64,1024]{1,0:T(8,128)(2,1)}, bf16[64,1024]{1,0:T(8,128)(2,1)S(1)}, u32[]{:S(2)}, u32[]{:S(2)}) collective-permute-start(bf16[64,1024]{1,0:T(8,128)(2,1)} %get-tuple-element.17.low0), channel_id=1, source_target_pairs={{0,4},{2,6},{4,0},{6,2},{1,5},{3,7},{5,1},{7,3},{8,12},{10,14},{12... | collective-permute-start | bytes 393224 | tf_op jit(solution)/shard_map/ppermute | solution.py:225
  46.4 0.3 collective-permute-start.13
  46.7 0.6 collective-permute-start.17
  47.3 2.4 %collective-permute-start.16 = (f32[64,64]{1,0:T(8,128)}, f32[64,64]{1,0:T(8,128)S(1)}, u32[]{:S(2)}, u32[]{:S(2)}) collective-permute-start(f32[64,64]{1,0:T(8,128)} %get-tuple-element.18), channel_id=1, source_target_pairs={{0,4},{2,6},{4,0},{6,2},{1,5},{3,7},{5,1},{7,3},{8,12},{10,14},{12... | collective-permute-start | bytes 49160 | tf_op jit(solution)/shard_map/ppermute | solution.py:226
  49.8 2.2 %collective-permute-done.17 = f32[64,64]{1,0:T(8,128)S(1)} collective-permute-done((f32[64,64]{1,0:T(8,128)}, f32[64,64]{1,0:T(8,128)S(1)}, u32[]{:S(2)}, u32[]{:S(2)}) %collective-permute-start.17) | collective-permute-done | bytes 16416 | tf_op jit(solution)/shard_map/ppermute | solution.py:226
  51.9 0.1 collective-permute-start.15
  52.1 0.4 collective-permute-done.16
  52.5 3.8 %collective-permute-start.8 = (bf16[64,1024]{1,0:T(8,128)(2,1)}, bf16[64,1024]{1,0:T(8,128)(2,1)S(1)}, u32[]{:S(2)}, u32[]{:S(2)}) collective-permute-start(bf16[64,1024]{1,0:T(8,128)(2,1)} %get-tuple-element.17.low0), channel_id=1, source_target_pairs={{0,1},{1,0},{2,3},{3,2},{4,5},{5,4},{6,7},{7,6},{8,9},{9,8},{10,11... | collective-permute-start | bytes 393224 | tf_op jit(solution)/shard_map/ppermute | solution.py:228
  56.4 0.5 collective-permute-start.12
  57.0 0.8 add_add_fusion.gram0
  57.7 4.3 %collective-permute-start.18 = (f32[64,64]{1,0:T(8,128)S(1)}, f32[64,64]{1,0:T(8,128)S(1)}, u32[]{:S(2)}, u32[]{:S(2)}) collective-permute-start(f32[64,64]{1,0:T(8,128)S(1)} %add_add_fusion.gram0), channel_id=1, source_target_pairs={{0,1},{1,0},{2,3},{3,2},{4,5},{5,4},{6,7},{7,6},{8,9},{9,8},{10,11... | collective-permute-start | bytes 49160 | tf_op jit(solution)/shard_map/ppermute | solution.py:227
  62.1 3.4 %copy-done.2 = bf16[32,16,8192]{2,1,0:T(8,128)(2,1)S(1)} copy-done((bf16[32,16,8192]{2,1,0:T(8,128)(2,1)S(1)}, bf16[32,16,8192]{2,1,0:T(8,128)(2,1)}, u32[]{:S(2)}) %copy-start.2) | copy-done | bytes 8388632
  65.5 0.9 copy-done.3
  66.4 2.7 %partial_own_core.1.before = f32[64,512]{1,0:T(8,128)S(1)} custom-call(s32[5]{0:T(128)S(1)} %pad_add_fusion.3.blocks, bf16[64,1024]{1,0:T(8,128)(2,1)S(1)} %copy-done.3, bf16[64,1024]{1,0:T(8,128)(2,1)S(1)} %collective-permute-done.9.low1, bf16[64,1024]{1,0:T(8,128)(2,1)S(1)} %collective-permute-done.11.low2, ...), custom_call_target="tpu_custom_call" | custom-call | flops 268435456 | bytes 6291456 | tf_op jit(solution)/shard_map/partial_own_core/pallas_call | solution.py:157
  69.1 2.8 %partial_other_core.1 = f32[4,96,128]{2,1,0:T(8,128)S(1)} custom-call(s32[5]{0:T(128)S(1)} %pad_add_fusion.2.blocks, bf16[64,1024]{1,0:T(8,128)(2,1)S(1)} %collective-permute-done.8.low0, bf16[64,1024]{1,0:T(8,128)(2,1)S(1)} %collective-permute-done.10.low1, bf16[64,1024]{1,0:T(8,128)(2,1)S(1)} %collective-permute-done.12.low2, ...), custom_call_target="tpu_custom_call" | custom-call | flops 268435456 | bytes 6291456 | tf_op jit(solution)/shard_map/partial_other_core/pallas_call | solution.py:157
  71.9 1.3 collective-permute-start.21
  73.2 0.5 collective-permute-start.20
  73.7 0.6 collective-permute-start.19
  74.3 1.0 collective-permute-done.21
  75.3 2.3 %collective-permute-done.20 = f32[96,128]{1,0:T(8,128)S(1)} collective-permute-done((f32[96,128]{1,0:T(8,128)S(1)}, f32[96,128]{1,0:T(8,128)S(1)}, u32[]{:S(2)}, u32[]{:S(2)}) %collective-permute-start.20) | collective-permute-done | bytes 49184 | tf_op jit(solution)/shard_map/ppermute | solution.py:250
  77.7 1.4 %collective-permute-done.19 = f32[96,128]{1,0:T(8,128)S(1)} collective-permute-done((f32[96,128]{1,0:T(8,128)S(1)}, f32[96,128]{1,0:T(8,128)S(1)}, u32[]{:S(2)}, u32[]{:S(2)}) %collective-permute-start.19) | collective-permute-done | bytes 49184 | tf_op jit(solution)/shard_map/ppermute | solution.py:250
  79.1 21.5 %all_to_all.10.recv_ref = f32[8,96,128]{2,1,0:T(8,128)} all-to-all(f32[8,96,128]{2,1,0:T(8,128)S(1)} %broadcast_in_dim.8), channel_id=1, replica_groups=mesh['z'=8,'x'=4,'y'=4,'core'=2] {'z'}, dimensions={0} | all-to-all | bytes 786432 | tf_op jit(solution)/shard_map/all_to_all | solution.py:251
  100.6 8.1 %interval_rows.1 = (f32[32,16,128]{2,1,0:T(8,128)}, f32[64,64]{1,0:T(8,128)}) custom-call(f32[8,96,128]{2,1,0:T(8,128)} %all_to_all.10.recv_ref, f32[16,64]{1,0:T(8,128)} %day_ref.5), custom_call_target="tpu_custom_call" | custom-call | flops 67108864 | bytes 1048576 | tf_op jit(solution)/shard_map/interval_rows/pallas_call | solution.py:170
  108.7 5.7 %all-to-all-start.1 = ((f32[32,16,128]{2,1,0:T(8,128)}), f32[32,16,128]{2,1,0:T(8,128)S(1)}, u32[]{:S(2)}, u32[]{:S(2)}) async-start(f32[32,16,128]{2,1,0:T(8,128)} %get-tuple-element.19), calls=%async_computation.1 | async-start | bytes 524288 | tf_op jit(solution)/shard_map/all_to_all | solution.py:255
  114.4 9.1 %all-to-all-done.1.recv_ref = f32[32,16,128]{2,1,0:T(8,128)S(1)} async-done(((f32[32,16,128]{2,1,0:T(8,128)}), f32[32,16,128]{2,1,0:T(8,128)S(1)}, u32[]{:S(2)}, u32[]{:S(2)}) %all-to-all-start.1) | async-done | bytes 262176 | tf_op jit(solution)/shard_map/all_to_all | solution.py:255
  123.5 0.7 copy-done.6
  124.2 7.4 %day_rows.1 = (f32[32,64]{1,0:T(8,128)}, f32[16,64]{1,0:T(8,128)}) custom-call(s32[1]{0:T(128)} %bitcast.7.place, f32[32,16,128]{2,1,0:T(8,128)} %copy-done.6, f32[64,64]{1,0:T(8,128)} %get-tuple-element.20.gram_ref), custom_call_target="tpu_custom_call" | custom-call | tf_op jit(solution)/shard_map/day_rows/pallas_call | solution.py:256
  (48 shorter events, 0.7 us)
Async XLA Ops:
  0.7 3.4 %copy-start = (bf16[32,16,8192]{2,1,0:T(8,128)(2,1)S(1)}, bf16[32,16,8192]{2,1,0:T(8,128)(2,1)}, u32[]{:S(2)}) copy-start(bf16[32,16,8192]{2,1,0:T(8,128)(2,1)} %param.3) | copy-start | bytes 25165828
  4.1 0.7 copy-start.4
  4.8 0.7 copy-start.5
  5.5 5.7 %copy-start.1 = (bf16[32,16,8192]{2,1,0:T(8,128)(2,1)S(1)}, bf16[32,16,8192]{2,1,0:T(8,128)(2,1)}, u32[]{:S(2)}) copy-start(bf16[32,16,8192]{2,1,0:T(8,128)(2,1)} %param.3) | copy-start | bytes 25165828
  7.9 5.6 %collective-permute-start = (f32[4,64,1024]{2,1,0:T(8,128)S(1)}, f32[4,64,1024]{2,1,0:T(8,128)S(1)}, u32[]{:S(2)}, u32[]{:S(2)}) collective-permute-start(f32[4,64,1024]{2,1,0:T(8,128)S(1)} %get-tuple-element.14), channel_id=1, source_target_pairs={{0,1},{1,0},{2,3},{3,2},{4,5},{5,4},{6,7},{7,6},{8,9},{9,8},{10,11... | collective-permute-start | bytes 3145736 | tf_op jit(solution)/shard_map/ppermute | solution.py:204
  14.3 26.2 %collective-permute-start.1 = (f32[64,1024]{1,0:T(8,128)S(1)}, f32[64,1024]{1,0:T(8,128)S(1)}, u32[]{:S(2)}, u32[]{:S(2)}) collective-permute-start(f32[64,1024]{1,0:T(8,128)S(1)} %get-tuple-element.25), channel_id=1, source_target_pairs={{0,2},{2,4},{4,6},{6,0},{1,3},{3,5},{5,7},{7,1},{8,10},{10,12},{12... | collective-permute-start | bytes 786440 | tf_op jit(solution)/shard_map/ppermute | solution.py:217
  14.3 26.2 %collective-permute-start.2 = (f32[64,1024]{1,0:T(8,128)S(1)}, f32[64,1024]{1,0:T(8,128)S(1)}, u32[]{:S(2)}, u32[]{:S(2)}) collective-permute-start(f32[64,1024]{1,0:T(8,128)S(1)} %get-tuple-element.24), channel_id=1, source_target_pairs={{0,4},{2,6},{4,0},{6,2},{1,5},{3,7},{5,1},{7,3},{8,12},{10,14},{12... | collective-permute-start | bytes 786440 | tf_op jit(solution)/shard_map/ppermute | solution.py:217
  16.6 23.9 %collective-permute-start.3 = (f32[64,1024]{1,0:T(8,128)S(1)}, f32[64,1024]{1,0:T(8,128)S(1)}, u32[]{:S(2)}, u32[]{:S(2)}) collective-permute-start(f32[64,1024]{1,0:T(8,128)S(1)} %get-tuple-element.23), channel_id=1, source_target_pairs={{0,6},{2,0},{4,2},{6,4},{1,7},{3,1},{5,3},{7,5},{8,14},{10,8},{12,... | collective-permute-start | bytes 786440 | tf_op jit(solution)/shard_map/ppermute | solution.py:217
  17.7 2.4 %collective-permute-start.4 = (f32[64,64]{1,0:T(8,128)S(1)}, f32[64,64]{1,0:T(8,128)S(1)}, u32[]{:S(2)}, u32[]{:S(2)}) collective-permute-start(f32[64,64]{1,0:T(8,128)S(1)} %get-tuple-element.15), channel_id=1, source_target_pairs={{0,1},{1,0},{2,3},{3,2},{4,5},{5,4},{6,7},{7,6},{8,9},{9,8},{10,11... | collective-permute-start | bytes 49160 | tf_op jit(solution)/shard_map/ppermute | solution.py:205
  20.1 12.6 %copy-start.10 = (f32[64,64]{1,0:T(8,128)}, f32[64,64]{1,0:T(8,128)S(1)}, u32[]{:S(2)}) copy-start(f32[64,64]{1,0:T(8,128)S(1)} %add.90.gram0) | copy-start | bytes 49156
  20.1 9.8 %collective-permute-start.5 = (f32[64,64]{1,0:T(8,128)S(1)}, f32[64,64]{1,0:T(8,128)S(1)}, u32[]{:S(2)}, u32[]{:S(2)}) collective-permute-start(f32[64,64]{1,0:T(8,128)S(1)} %add.90.gram0), channel_id=1, source_target_pairs={{0,2},{2,4},{4,6},{6,0},{1,3},{3,5},{5,7},{7,1},{8,10},{10,12},{12... | collective-permute-start | bytes 49160 | tf_op jit(solution)/shard_map/ppermute | solution.py:206
  20.5 9.4 %collective-permute-start.6 = (f32[64,64]{1,0:T(8,128)S(1)}, f32[64,64]{1,0:T(8,128)S(1)}, u32[]{:S(2)}, u32[]{:S(2)}) collective-permute-start(f32[64,64]{1,0:T(8,128)S(1)} %add.90.gram0), channel_id=1, source_target_pairs={{0,4},{2,6},{4,0},{6,2},{1,5},{3,7},{5,1},{7,3},{8,12},{10,14},{12... | collective-permute-start | bytes 49160 | tf_op jit(solution)/shard_map/ppermute | solution.py:206
  29.9 2.8 %copy-start.11 = (f32[64,64]{1,0:T(8,128)}, f32[64,64]{1,0:T(8,128)S(1)}, u32[]{:S(2)}) copy-start(f32[64,64]{1,0:T(8,128)S(1)} %collective-permute-done.5.gram1) | copy-start | bytes 49156
  29.9 2.8 %collective-permute-start.7 = (f32[64,64]{1,0:T(8,128)S(1)}, f32[64,64]{1,0:T(8,128)S(1)}, u32[]{:S(2)}, u32[]{:S(2)}) collective-permute-start(f32[64,64]{1,0:T(8,128)S(1)} %add.90.gram0), channel_id=1, source_target_pairs={{0,6},{2,0},{4,2},{6,4},{1,7},{3,1},{5,3},{7,5},{8,14},{10,8},{12,... | collective-permute-start | bytes 49160 | tf_op jit(solution)/shard_map/ppermute | solution.py:206
  29.9 2.7 %copy-start.12 = (f32[64,64]{1,0:T(8,128)}, f32[64,64]{1,0:T(8,128)S(1)}, u32[]{:S(2)}) copy-start(f32[64,64]{1,0:T(8,128)S(1)} %collective-permute-done.6.gram2) | copy-start | bytes 49156
  32.7 0.6 copy-start.13
  40.5 0.7 copy-start.7
  40.5 0.8 copy-start.8
  40.6 0.9 copy-start.9
  44.0 12.3 %collective-permute-start.9 = (bf16[64,1024]{1,0:T(8,128)(2,1)}, bf16[64,1024]{1,0:T(8,128)(2,1)S(1)}, u32[]{:S(2)}, u32[]{:S(2)}) collective-permute-start(bf16[64,1024]{1,0:T(8,128)(2,1)} %get-tuple-element.17.low0), channel_id=1, source_target_pairs={{0,2},{2,4},{4,6},{6,0},{1,3},{3,5},{5,7},{7,1},{8,10},{10,12},{12... | collective-permute-start | bytes 393224 | tf_op jit(solution)/shard_map/ppermute | solution.py:225
  44.0 12.4 %collective-permute-start.11 = (bf16[64,1024]{1,0:T(8,128)(2,1)}, bf16[64,1024]{1,0:T(8,128)(2,1)S(1)}, u32[]{:S(2)}, u32[]{:S(2)}) collective-permute-start(bf16[64,1024]{1,0:T(8,128)(2,1)} %get-tuple-element.17.low0), channel_id=1, source_target_pairs={{0,4},{2,6},{4,0},{6,2},{1,5},{3,7},{5,1},{7,3},{8,12},{10,14},{12... | collective-permute-start | bytes 393224 | tf_op jit(solution)/shard_map/ppermute | solution.py:225
  46.4 10.5 %collective-permute-start.13 = (bf16[64,1024]{1,0:T(8,128)(2,1)}, bf16[64,1024]{1,0:T(8,128)(2,1)S(1)}, u32[]{:S(2)}, u32[]{:S(2)}) collective-permute-start(bf16[64,1024]{1,0:T(8,128)(2,1)} %get-tuple-element.17.low0), channel_id=1, source_target_pairs={{0,6},{2,0},{4,2},{6,4},{1,7},{3,1},{5,3},{7,5},{8,14},{10,8},{12,... | collective-permute-start | bytes 393224 | tf_op jit(solution)/shard_map/ppermute | solution.py:225
  46.7 5.2 %collective-permute-start.17 = (f32[64,64]{1,0:T(8,128)}, f32[64,64]{1,0:T(8,128)S(1)}, u32[]{:S(2)}, u32[]{:S(2)}) collective-permute-start(f32[64,64]{1,0:T(8,128)} %get-tuple-element.18), channel_id=1, source_target_pairs={{0,6},{2,0},{4,2},{6,4},{1,7},{3,1},{5,3},{7,5},{8,14},{10,8},{12,... | collective-permute-start | bytes 49160 | tf_op jit(solution)/shard_map/ppermute | solution.py:226
  47.3 5.2 %collective-permute-start.16 = (f32[64,64]{1,0:T(8,128)}, f32[64,64]{1,0:T(8,128)S(1)}, u32[]{:S(2)}, u32[]{:S(2)}) collective-permute-start(f32[64,64]{1,0:T(8,128)} %get-tuple-element.18), channel_id=1, source_target_pairs={{0,4},{2,6},{4,0},{6,2},{1,5},{3,7},{5,1},{7,3},{8,12},{10,14},{12... | collective-permute-start | bytes 49160 | tf_op jit(solution)/shard_map/ppermute | solution.py:226
  51.9 5.0 %collective-permute-start.15 = (f32[64,64]{1,0:T(8,128)}, f32[64,64]{1,0:T(8,128)S(1)}, u32[]{:S(2)}, u32[]{:S(2)}) collective-permute-start(f32[64,64]{1,0:T(8,128)} %get-tuple-element.18), channel_id=1, source_target_pairs={{0,2},{2,4},{4,6},{6,0},{1,3},{3,5},{5,7},{7,1},{8,10},{10,12},{12... | collective-permute-start | bytes 49160 | tf_op jit(solution)/shard_map/ppermute | solution.py:226
  52.5 16.6 %collective-permute-start.8 = (bf16[64,1024]{1,0:T(8,128)(2,1)}, bf16[64,1024]{1,0:T(8,128)(2,1)S(1)}, u32[]{:S(2)}, u32[]{:S(2)}) collective-permute-start(bf16[64,1024]{1,0:T(8,128)(2,1)} %get-tuple-element.17.low0), channel_id=1, source_target_pairs={{0,1},{1,0},{2,3},{3,2},{4,5},{5,4},{6,7},{7,6},{8,9},{9,8},{10,11... | collective-permute-start | bytes 393224 | tf_op jit(solution)/shard_map/ppermute | solution.py:228
  56.4 12.7 %collective-permute-start.10 = (bf16[64,1024]{1,0:T(8,128)(2,1)S(1)}, bf16[64,1024]{1,0:T(8,128)(2,1)S(1)}, u32[]{:S(2)}, u32[]{:S(2)}) collective-permute-start(bf16[64,1024]{1,0:T(8,128)(2,1)S(1)} %collective-permute-done.9.low1), channel_id=1, source_target_pairs={{0,1},{1,0},{2,3},{3,2},{4,5},{5,4},{6,7},{7,6},{8,9},{9,8},{10,11... | collective-permute-start | bytes 393224 | tf_op jit(solution)/shard_map/ppermute | solution.py:228
  56.4 12.7 %collective-permute-start.12 = (bf16[64,1024]{1,0:T(8,128)(2,1)S(1)}, bf16[64,1024]{1,0:T(8,128)(2,1)S(1)}, u32[]{:S(2)}, u32[]{:S(2)}) collective-permute-start(bf16[64,1024]{1,0:T(8,128)(2,1)S(1)} %collective-permute-done.11.low2), channel_id=1, source_target_pairs={{0,1},{1,0},{2,3},{3,2},{4,5},{5,4},{6,7},{7,6},{8,9},{9,8},{10,11... | collective-permute-start | bytes 393224 | tf_op jit(solution)/shard_map/ppermute | solution.py:228
  56.9 12.2 %collective-permute-start.14 = (bf16[64,1024]{1,0:T(8,128)(2,1)S(1)}, bf16[64,1024]{1,0:T(8,128)(2,1)S(1)}, u32[]{:S(2)}, u32[]{:S(2)}) collective-permute-start(bf16[64,1024]{1,0:T(8,128)(2,1)S(1)} %collective-permute-done.13.low3), channel_id=1, source_target_pairs={{0,1},{1,0},{2,3},{3,2},{4,5},{5,4},{6,7},{7,6},{8,9},{9,8},{10,11... | collective-permute-start | bytes 393224 | tf_op jit(solution)/shard_map/ppermute | solution.py:228
  57.7 11.3 %collective-permute-start.18 = (f32[64,64]{1,0:T(8,128)S(1)}, f32[64,64]{1,0:T(8,128)S(1)}, u32[]{:S(2)}, u32[]{:S(2)}) collective-permute-start(f32[64,64]{1,0:T(8,128)S(1)} %add_add_fusion.gram0), channel_id=1, source_target_pairs={{0,1},{1,0},{2,3},{3,2},{4,5},{5,4},{6,7},{7,6},{8,9},{9,8},{10,11... | collective-permute-start | bytes 49160 | tf_op jit(solution)/shard_map/ppermute | solution.py:227
  62.1 3.4 %copy-start.2 = (bf16[32,16,8192]{2,1,0:T(8,128)(2,1)S(1)}, bf16[32,16,8192]{2,1,0:T(8,128)(2,1)}, u32[]{:S(2)}) copy-start(bf16[32,16,8192]{2,1,0:T(8,128)(2,1)} %param.3) | copy-start | bytes 25165828
  65.5 0.9 copy-start.3
  71.9 3.4 %collective-permute-start.21 = (f32[96,128]{1,0:T(8,128)S(1)}, f32[96,128]{1,0:T(8,128)S(1)}, u32[]{:S(2)}, u32[]{:S(2)}) collective-permute-start(f32[96,128]{1,0:T(8,128)S(1)} %get-tuple-element.28), channel_id=1, source_target_pairs={{0,24},{8,0},{16,8},{24,16},{1,25},{9,1},{17,9},{25,17},{2,26},{10... | collective-permute-start | bytes 147464 | tf_op jit(solution)/shard_map/ppermute | solution.py:250
  73.2 4.5 %collective-permute-start.20 = (f32[96,128]{1,0:T(8,128)S(1)}, f32[96,128]{1,0:T(8,128)S(1)}, u32[]{:S(2)}, u32[]{:S(2)}) collective-permute-start(f32[96,128]{1,0:T(8,128)S(1)} %get-tuple-element.29), channel_id=1, source_target_pairs={{0,16},{8,24},{16,0},{24,8},{1,17},{9,25},{17,1},{25,9},{2,18},{10... | collective-permute-start | bytes 147464 | tf_op jit(solution)/shard_map/ppermute | solution.py:250
  73.7 5.3 %collective-permute-start.19 = (f32[96,128]{1,0:T(8,128)S(1)}, f32[96,128]{1,0:T(8,128)S(1)}, u32[]{:S(2)}, u32[]{:S(2)}) collective-permute-start(f32[96,128]{1,0:T(8,128)S(1)} %get-tuple-element.27), channel_id=1, source_target_pairs={{0,8},{8,16},{16,24},{24,0},{1,9},{9,17},{17,25},{25,1},{2,10},{10... | collective-permute-start | bytes 147464 | tf_op jit(solution)/shard_map/ppermute | solution.py:250
  108.7 14.9 %all-to-all-start.1 = ((f32[32,16,128]{2,1,0:T(8,128)}), f32[32,16,128]{2,1,0:T(8,128)S(1)}, u32[]{:S(2)}, u32[]{:S(2)}) async-start(f32[32,16,128]{2,1,0:T(8,128)} %get-tuple-element.19), calls=%async_computation.1 | async-start | bytes 524288 | tf_op jit(solution)/shard_map/all_to_all | solution.py:255
  123.5 0.7 copy-start.6

commit v2 on v0

v2 whole, which is shorter than its diff:
```python
import jax
import jax.numpy as jnp
from jax import lax
from jax.experimental import pallas as pl
from jax.experimental.pallas import tpu as pltpu
from jax.sharding import Mesh, PartitionSpec as P

RANK = 64
HIGH = lax.Precision.HIGHEST
F32 = jnp.float32
BF16 = jnp.bfloat16


def shifts(n, d):
    return [(i, (i + d) % n) for i in range(n)]


def iota(shape, dim):
    return lax.broadcasted_iota(jnp.int32, shape, dim)


def dot(a, b, contract=((1,), (0,)), precision=HIGH):
    return lax.dot_general(a, b, (contract, ((), ())), precision=precision, preferred_element_type=F32)


def shifted(system):
    eye = iota((RANK, RANK), 0) == iota((RANK, RANK), 1)
    trace = jnp.sum(jnp.sum(jnp.where(eye, system, 0.0), axis=1, keepdims=True), axis=0, keepdims=True)
    return system + jnp.where(eye, 0.01 * trace / RANK, 0.0)


def eliminate(system, rhs):
    work = jnp.concatenate([system, rhs], axis=1)
    parts = [work[at : at + 8] for at in range(0, RANK, 8)]
    row = iota((8, 1), 0)
    for p in range(RANK // 8):
        rows = parts[p]
        columns = [jnp.broadcast_to(rows[:, 8 * p + j : 8 * p + j + 1], rows.shape) for j in range(8)]
        for j in range(8):
            inverse = 1.0 / columns[j][j : j + 1]
            scaled = rows[j : j + 1] * inverse
            rows = jnp.where(row == j, scaled, rows - columns[j] * scaled)
            for i in range(j + 1, 8):
                scaled = columns[i][j : j + 1] * inverse
                columns[i] = jnp.where(row == j, scaled, columns[i] - columns[j] * scaled)
        for q in range(RANK // 8):
            if q != p:
                taken = parts[q][:, 8 * p : 8 * p + 1] * rows[0:1]
                for j in range(1, 8):
                    taken = taken + parts[q][:, 8 * p + j : 8 * p + j + 1] * rows[j : j + 1]
                parts[q] = parts[q] - taken
        parts[p] = rows
    return jnp.concatenate(parts, axis=0)


def load_blocks(place, slab_ref, held_ref, sems, offset):
    copies = []
    for d in range(4):
        at = pl.multiple_of(place[offset + d] * 1024, 1024)
        copies.append(pltpu.make_async_copy(slab_ref.at[:, pl.ds(at, 1024)], held_ref.at[d], sems.at[d]))
        copies[-1].start()
    return copies


def send_kernel(
    place, slab_ref, interval_ref, day_ref, sums_ref, held_ref, khatri_ref, gram_ref, day_out, factor, sems, small_sems
):
    small = [
        pltpu.make_async_copy(interval_ref, factor, small_sems.at[0]),
        pltpu.make_async_copy(day_ref, day_out, small_sems.at[1]),
    ]
    for copy in small:
        copy.start()
    copies = load_blocks(place, slab_ref, held_ref, sems, 4)
    for copy in small:
        copy.wait()
    product = factor[...][:, None, :] * day_out[...][None, :, :]
    khatri = product.reshape(product.shape[0] * product.shape[1], RANK).T.astype(BF16)
    khatri_ref[...] = khatri
    gram_ref[...] = dot(factor[...], factor[...], ((0,), (0,)))
    for d in range(4):
        copies[d].wait()
        sums_ref[d] = dot(khatri, held_ref[d], precision=None)


def keep_kernel(place, slab_ref, khatri_ref, sums_ref, held_ref, sems):
    copies = load_blocks(place, slab_ref, held_ref, sems, 0)
    for d in range(4):
        copies[d].wait()
        sums_ref[d] = dot(khatri_ref[...], held_ref[d], precision=None)


def pack(gram):
    return jnp.concatenate([gram[: RANK // 2], gram[RANK // 2 :]], axis=1)


def unpack(packed):
    return jnp.concatenate([packed[:, :RANK], packed[:, RANK:]], axis=0)


def add_kernel(keep_ref, got_ref, gram_ref, *refs):
    outs, grams = refs[:4], refs[4]
    for d, out in enumerate(outs):
        out[...] = keep_ref[d] + got_ref[d]
    packed = pack(gram_ref[...])
    for i in range(grams.shape[0]):
        grams[i] = packed


def inverse_kernel(grams, day_ref, out_ref):
    packed = grams[0]
    for i in range(1, grams.shape[0]):
        packed = packed + grams[i]
    gram = unpack(packed)
    gram_day = dot(day_ref[...], day_ref[...], ((0,), (0,)))
    eye = jnp.where(iota((RANK, RANK), 0) == iota((RANK, RANK), 1), 1.0, 0.0).astype(F32)
    out_ref[...] = eliminate(shifted(gram * gram_day), eye)[:, RANK:]


def link_kernel(sum0, sum1, sum2, sum3, inverse_ref, link_ref, low_ref):
    sums = (sum0[...] + sum1[...]) + (sum2[...] + sum3[...])
    link = dot(inverse_ref[...], sums)
    link_ref[...] = link
    low_ref[:, : link.shape[1]] = link.astype(BF16)
    gram = dot(link, link, ((1,), (1,)))
    high = gram.astype(BF16)
    rest = (gram - high.astype(F32)).astype(BF16)
    low_ref[:, link.shape[1] :] = jnp.concatenate([high, rest], axis=1)


def times_blocks(lows, held_ref, behind):
    total = None
    for low, d in zip(lows, behind):
        term = dot(low[:, :1024], held_ref[(4 - d) % 4], ((1,), (1,)), None)
        total = term if total is None else total + term
    return total


def first_partial_kernel(low, low_other, keep_ref, send_ref, acc):
    acc[...] = times_blocks((low,), keep_ref, (0,)) + times_blocks((low_other,), send_ref, (0,))


def second_partial_kernel(low0, low1, low2, keep_ref, before, acc):
    acc[...] = before[...] + times_blocks((low0, low1, low2), keep_ref, (2, 1, 3))


def last_partial_kernel(place, *refs):
    lows, (send_ref, before), outs, acc = refs[:8], refs[8:10], refs[10:14], refs[14]
    acc[...] = before[...] + times_blocks(lows[:3], send_ref, (2, 1, 3))
    halves = [low[:, 1024:].astype(F32) for low in lows]
    total = halves[0]
    for half in halves[1:]:
        total = total + half
    packed = pack(total[:, :RANK] + total[:, RANK:])
    for d, out in enumerate(outs):
        at = pl.multiple_of(lax.rem(place[8] + d, 4) * 128, 128)
        out[:RANK] = acc[:, pl.ds(at, 128)]
        out[RANK:] = packed


def interval_kernel(recv_ref, day_ref, out_ref, gram_ref):
    total = recv_ref[0]
    for i in range(1, recv_ref.shape[0]):
        total = total + recv_ref[i]
    partial = total[:RANK]
    gram = unpack(total[RANK:])
    gram_ref[...] = gram
    day = day_ref[...]
    gram_day = dot(day, day, ((0,), (0,)))
    of_day = jnp.where(lax.rem(iota((16, 128), 1), 16) == iota((16, 128), 0), 1.0, 0.0).astype(F32)
    of_interval = jnp.where(lax.div(iota((8, 128), 1), 16) == iota((8, 128), 0), 1.0, 0.0).astype(F32)
    day_lanes = dot(day, of_day, ((0,), (0,)))
    interval_sums = dot(partial * day_lanes, of_interval, ((1,), (1,)))
    rhs = jnp.concatenate([interval_sums, jnp.zeros((RANK, 56), F32)], axis=1)
    solved = eliminate(shifted(gram * gram_day), rhs)
    interval_new = solved[:, RANK : RANK + 8]
    day_part = dot(of_day, partial * dot(interval_new, of_interval), ((1,), (1,)))
    rows = jnp.transpose(solved)[RANK : RANK + 8]
    payload = jnp.concatenate(
        [
            jnp.concatenate([day_part[:8], day_part[8:]], axis=1),
            jnp.concatenate([rows, jnp.zeros((8, RANK), F32)], axis=1),
        ],
        axis=0,
    )
    for i in range(out_ref.shape[0]):
        out_ref[i] = payload


def day_kernel(place, recv_ref, gram_ref, interval_ref, day_ref):
    total = recv_ref[0, :8]
    for i in range(1, 32):
        total = total + recv_ref[i, :8]
    rows = recv_ref[:, 8:, :RANK].reshape(256, RANK)
    gram_new = dot(rows, rows, ((0,), (0,)))
    for i in range(4):
        interval_ref[i * 8 : i * 8 + 8] = recv_ref[i * 8 + place[9], 8:, :RANK]
    turned = jnp.transpose(total)
    rhs = jnp.concatenate([turned[:RANK], turned[RANK:], jnp.zeros((RANK, 48), F32)], axis=1)
    solved = eliminate(shifted(gram_ref[...] * gram_new), rhs)
    day_ref[...] = jnp.transpose(solved)[RANK : RANK + 16]


def shape(dims, dtype=F32):
    return jax.ShapeDtypeStruct(dims, dtype)


def call(kernel, out_shape, args, name, spaces=None, scratch=()):
    spaces = spaces or {}
    return pl.pallas_call(
        kernel,
        out_shape=out_shape,
        in_specs=[pl.BlockSpec(memory_space=spaces.get(i, pltpu.VMEM)) for i in range(len(args))],
        out_specs=jax.tree.map(lambda _: pl.BlockSpec(memory_space=pltpu.VMEM), out_shape),
        scratch_shapes=scratch,
        compiler_params=pltpu.CompilerParams(vmem_limit_bytes=16 * 2**20),
        cost_estimate=pl.CostEstimate(flops=2**20, bytes_accessed=2**16, transcendentals=0),
        name=name,
    )(*args)


def body(slab, interval_factor, day_factor):
    intervals, days, links = slab.shape
    flat = pltpu.with_memory_space_constraint(slab.reshape(intervals * days, links), pltpu.HBM)
    interval_factor = pltpu.with_memory_space_constraint(interval_factor, pltpu.HBM)
    day_factor = pltpu.with_memory_space_constraint(day_factor, pltpu.HBM)
    y, c, x = lax.axis_index("y"), lax.axis_index("core"), lax.axis_index("x")
    at = jnp.arange(10, dtype=jnp.int32)
    core = jnp.where(at < 4, c, 1 - c)
    place = jnp.where(at == 8, x, jnp.where(at == 9, 2 * y + c, 2 * ((y + at) % 4) + core)).astype(jnp.int32)
    held = shape((4, 512, 1024), BF16)

    def other_core(a):
        return lax.ppermute(a, "core", shifts(2, 1))

    send, held_send, khatri, gram_part, day = call(
        send_kernel,
        (shape((4, RANK, 1024)), held, shape((RANK, 512), BF16), shape((RANK, RANK)), shape((16, RANK))),
        (place, flat, interval_factor, day_factor),
        "sums_to_send",
        {0: pltpu.SMEM, 1: pl.ANY, 2: pl.ANY, 3: pl.ANY},
        [pltpu.VMEM((32, RANK), F32), pltpu.SemaphoreType.DMA((4,)), pltpu.SemaphoreType.DMA((2,))],
    )
    got = other_core(send)
    keep, held_keep = call(
        keep_kernel,
        (shape((4, RANK, 1024)), held),
        (place, flat, khatri),
        "sums_to_keep",
        {0: pltpu.SMEM, 1: pl.ANY},
        [pltpu.SemaphoreType.DMA((4,))],
    )
    *sums, grams = call(add_kernel, (shape((RANK, 1024)),) * 4 + (shape((8, 32, 128)),), (keep, got, gram_part), "add_cores")
    parts = [sums[0]] + [lax.ppermute(sums[d], "y", shifts(4, d)) for d in (1, 2, 3)]
    grams = lax.all_to_all(grams, ("y", "core"), 0, 0)
    inverse = call(inverse_kernel, shape((RANK, RANK)), (grams, day), "link_inverse")
    link, low = call(
        link_kernel,
        (shape((RANK, 1024)), shape((RANK, 1152), BF16)),
        (*parts, inverse),
        "link_rows",
    )
    lows = [lax.ppermute(low, "y", shifts(4, d)) for d in (2, 1, 3)]
    low_other = other_core(low)
    acc = call(
        first_partial_kernel, shape((RANK, 512)), (low, low_other, held_keep, held_send), "partial_a"
    )
    lows_other = [other_core(one) for one in lows]
    acc = call(second_partial_kernel, shape((RANK, 512)), (*lows, held_keep, acc), "partial_b")
    outgoing = call(
        last_partial_kernel,
        (shape((96, 128)),) * 4,
        (place, *lows_other, *lows, low, low_other, held_send, acc),
        "partial_c",
        {0: pltpu.SMEM},
        [pltpu.VMEM((RANK, 512), F32)],
    )
    over_x = sum([lax.ppermute(outgoing[d], "x", shifts(4, d)) for d in (2, 1, 3)], outgoing[0])
    over_z = lax.all_to_all(jnp.broadcast_to(over_x[None], (8, 96, 128)), "z", 0, 0)
    outgoing, gram_link = call(
        interval_kernel, (shape((32, 16, 128)), shape((RANK, RANK))), (over_z, day), "interval_rows"
    )
    everyone = lax.all_to_all(outgoing, ("x", "y", "core"), 0, 0)
    interval_new, day_new = call(
        day_kernel,
        (shape((32, RANK)), shape((16, RANK))),
        (place, everyone, gram_link),
        "day_rows",
        {0: pltpu.SMEM},
    )
    return link.T, interval_new, day_new


def solution(mesh):
    split = Mesh(mesh.devices.reshape(8, 4, 4, 2), ("z", "x", "y", "core"))
    link, intv = ("z", "x"), ("y", "core")
    return jax.shard_map(
        body,
        mesh=split,
        in_specs=(P(intv, None, link), P(intv, None), P()),
        out_specs=(P(link + intv, None), P(intv, None), P()),
        check_vma=False,
    )
```

time: 414 us -> 96.1 us (0.23)
  blocking collectives: 338 us -> 49.6 us
  other arithmetic: 38.4 us -> 0.03 us
  Pallas kernels: 0 us -> 19.5 us
  starting transfers between devices: 0.08 us -> 18.8 us
  matrix products: 17.7 us -> 0 us
  between operations: 16.2 us -> 0.76 us
  waiting for transfers between devices: 0.09 us -> 7.14 us
    psum x5 -> x0, blocking collectives: 338 us -> none  [the longest x1 111 us: body(): interval_sums = lax.psum(interval_part, 'link')]
    all_to_all x0 -> x3, blocking collectives: none -> 49.6 us  [the longest x1 19.1 us: body(): lax.all_to_all(jnp.broadcast_to(over_x[None], (8, 96, 128)), 'z', 0, 0)]
    another operation x15 -> x0, other arithmetic: 36.2 us -> none  [the longest x9 19.6 us: solve_rows(): factor = jnp.linalg.cholesky(shifted)]
    pallas_call x0 -> x10, Pallas kernels: none -> 19.5 us  [call(): pl.pallas_call(kernel, out_shape=out_shape, in_specs=[pl.BlockSpec(memory...]
    ppermute x0 -> x14, starting transfers between devices: none -> 18.8 us  [the longest x5 7.66 us: other_core(): return lax.ppermute(a, 'core', shifts(2, 1))]
    dot_general x6 -> x0, matrix products: 14.4 us -> none  [the longest x1 6.38 us: body(): lax.dot_general(flat, khatri, (((0,), (0,)), ((), ())), preferred_element...]
    ppermute x0 -> x14, waiting for transfers between devices: none -> 7.14 us  [the longest x3 5.12 us: body(): lows = [lax.ppermute(low, 'y', shifts(4, d)) for d in (2, 1, 3)]]
  transfers between devices with their start and end apart: 2 -> 14, of which waited for: 0 -> 3; matrix products, arithmetic and copies ran while one was open for 6% -> 0% of each run, Pallas kernels for 0% -> 7%
where the time goes in v2:
time: 96.1 us; the launch traced here: 95.9 us
  blocking collectives  49.6 us (52%)
  Pallas kernels  19.5 us (20%)
  starting transfers between devices  18.8 us (20%)
  waiting for transfers between devices  7.14 us (7%)
    pallas_call x10, Pallas kernels, call(): pl.pallas_call(kernel, out_shape=out_shape, in_specs=[pl.BlockSpec(memory...  19.5 us
    all_to_all x1, blocking collectives, body(): lax.all_to_all(jnp.broadcast_to(over_x[None], (8, 96, 128)), 'z', 0, 0)  19.1 us
    all_to_all x1, blocking collectives, body(): everyone = lax.all_to_all(outgoing, ('x', 'y', 'core'), 0, 0)  17.2 us
    all_to_all x1, blocking collectives, body(): grams = lax.all_to_all(grams, ('y', 'core'), 0, 0)  13.3 us
    ppermute x5, starting transfers between devices, other_core(): return lax.ppermute(a, 'core', shifts(2, 1))  7.66 us
    ppermute x3, waiting for transfers between devices, body(): lows = [lax.ppermute(low, 'y', shifts(4, d)) for d in (2, 1, 3)]  5.12 us
    ppermute x3, starting transfers between devices, body(): lax.ppermute(outgoing[d], 'x', shifts(4, d))  4.12 us
    ppermute x3, starting transfers between devices, body(): lows = [lax.ppermute(low, 'y', shifts(4, d)) for d in (2, 1, 3)]  3.73 us
  transfers between devices with their start and end apart: 14, of which 3 were waited for; matrix products, arithmetic and copies ran while one was open for 0% of the time, Pallas kernels for 7%

profile of v2, /device:TPU:1, one launch (start us, length us, event | category | flops | bytes accessed | tf_op | source)
XLA Modules:
  0.0 95.9 jit_solution(18385744683367777513)
XLA Ops:
  0.7 3.8 %sums_to_send.1 = (f32[4,64,1024]{2,1,0:T(8,128)S(1)}, bf16[4,512,1024]{2,1,0:T(8,128)(2,1)S(1)}, bf16[64,512]{1,0:T(8,128)(2,1)S(1)}, f32[64,64]{1,0:T(8,128)S(1)}, f32[16,64]{1,0:T(8,128)S(1)}) custom-call(s32[10]{0:T(128)S(1)} %compare_select_fusion.4.place, bf16[512,8192]{1,0:T(8,128)(2,1)} %bitcast.2, f32[32,64]{1,0:T(8,128)} %interval_ref.1, ...), custom_call_target="tpu_custom_call" | custom-call | flops 1048576 | bytes 65536 | tf_op jit(solution)/shard_map/sums_to_send/pallas_call | solution.py:210
  4.4 3.3 %collective-permute-start = (f32[4,64,1024]{2,1,0:T(8,128)S(1)}, f32[4,64,1024]{2,1,0:T(8,128)S(1)}, u32[]{:S(2)}, u32[]{:S(2)}) collective-permute-start(f32[4,64,1024]{2,1,0:T(8,128)S(1)} %get-tuple-element.27), channel_id=1, source_target_pairs={{0,1},{1,0},{2,3},{3,2},{4,5},{5,4},{6,7},{7,6},{8,9},{9,8},{10,11... | collective-permute-start | bytes 3145736 | tf_op jit(solution)/shard_map/ppermute | solution.py:234
  7.7 3.1 %sums_to_keep.1 = (f32[4,64,1024]{2,1,0:T(8,128)S(1)}, bf16[4,512,1024]{2,1,0:T(8,128)(2,1)S(1)}) custom-call(s32[10]{0:T(128)S(1)} %compare_select_fusion.4.place, bf16[512,8192]{1,0:T(8,128)(2,1)} %bitcast.3, bf16[64,512]{1,0:T(8,128)(2,1)S(1)} %get-tuple-element.25.khatri_ref), custom_call_target="tpu_custom_call" | custom-call | flops 1048576 | bytes 65536 | tf_op jit(solution)/shard_map/sums_to_keep/pallas_call | solution.py:210
  10.8 0.0 collective-permute-done.got_ref
  10.8 0.1 add_cores.1
  10.9 0.1 collective-permute-start.1
  11.0 2.2 %collective-permute-start.2 = (f32[64,1024]{1,0:T(8,128)S(1)}, f32[64,1024]{1,0:T(8,128)S(1)}, u32[]{:S(2)}, u32[]{:S(2)}) collective-permute-start(f32[64,1024]{1,0:T(8,128)S(1)} %get-tuple-element.31), channel_id=1, source_target_pairs={{0,4},{2,6},{4,0},{6,2},{1,5},{3,7},{5,1},{7,3},{8,12},{10,14},{12... | collective-permute-start | bytes 786440 | tf_op jit(solution)/shard_map/ppermute | solution.py:254
  13.2 1.1 %collective-permute-start.3 = (f32[64,1024]{1,0:T(8,128)S(1)}, f32[64,1024]{1,0:T(8,128)S(1)}, u32[]{:S(2)}, u32[]{:S(2)}) collective-permute-start(f32[64,1024]{1,0:T(8,128)S(1)} %get-tuple-element.32), channel_id=1, source_target_pairs={{0,6},{2,0},{4,2},{6,4},{1,7},{3,1},{5,3},{7,5},{8,14},{10,8},{12,... | collective-permute-start | bytes 786440 | tf_op jit(solution)/shard_map/ppermute | solution.py:254
  14.3 13.3 %all_to_all.15.grams = f32[8,32,128]{2,1,0:T(8,128)S(1)} all-to-all(f32[8,32,128]{2,1,0:T(8,128)S(1)} %get-tuple-element.33), channel_id=1, replica_groups=mesh['z'=8,'x'=4,'y'=4,'core'=2] {'y','core'}, dimensions={0} | all-to-all | bytes 262144 | tf_op jit(solution)/shard_map/all_to_all | solution.py:255
  27.6 1.7 %link_inverse.1.inverse_ref = f32[64,64]{1,0:T(8,128)S(1)} custom-call(f32[8,32,128]{2,1,0:T(8,128)S(1)} %all_to_all.15.grams, f32[16,64]{1,0:T(8,128)S(1)} %get-tuple-element.34.day_ref), custom_call_target="tpu_custom_call" | custom-call | flops 1048576 | bytes 65536 | tf_op jit(solution)/shard_map/link_inverse/pallas_call | solution.py:210
  29.3 0.0 collective-permute-done.1.sum1
  29.3 0.0 collective-permute-done.2.sum2
  29.3 0.0 collective-permute-done.3.sum3
  29.4 1.3 %link_rows.1 = (f32[64,1024]{1,0:T(8,128)}, bf16[64,1152]{1,0:T(8,128)(2,1)S(1)}) custom-call(f32[64,1024]{1,0:T(8,128)S(1)} %get-tuple-element.29.sum0, f32[64,1024]{1,0:T(8,128)S(1)} %collective-permute-done.1.sum1, f32[64,1024]{1,0:T(8,128)S(1)} %collective-permute-done.2.sum2, f32[64,1024]{1,0:T(8,128)S(1)} %collective-permute-done.3.sum3, ...), custom_call_target="tpu_custom_call" | custom-call | flops 1048576 | bytes 65536 | tf_op jit(solution)/shard_map/link_rows/pallas_call | solution.py:210
  30.6 2.5 %collective-permute-start.8 = (bf16[64,1152]{1,0:T(8,128)(2,1)S(1)}, bf16[64,1152]{1,0:T(8,128)(2,1)S(1)}, u32[]{:S(2)}, u32[]{:S(2)}) collective-permute-start(bf16[64,1152]{1,0:T(8,128)(2,1)S(1)} %get-tuple-element.36.low.refs_6_), channel_id=1, source_target_pairs={{0,6},{2,0},{4,2},{6,4},{1,7},{3,1},{5,3},{7,5},{8,14},{10,8},{12,... | collective-permute-start | bytes 442376 | tf_op jit(solution)/shard_map/ppermute | solution.py:263
  33.2 0.0 collective-permute-start.6
  33.2 1.2 %collective-permute-start.4 = (bf16[64,1152]{1,0:T(8,128)(2,1)S(1)}, bf16[64,1152]{1,0:T(8,128)(2,1)S(1)}, u32[]{:S(2)}, u32[]{:S(2)}) collective-permute-start(bf16[64,1152]{1,0:T(8,128)(2,1)S(1)} %get-tuple-element.36.low.refs_6_), channel_id=1, source_target_pairs={{0,4},{2,6},{4,0},{6,2},{1,5},{3,7},{5,1},{7,3},{8,12},{10,14},{12... | collective-permute-start | bytes 442376 | tf_op jit(solution)/shard_map/ppermute | solution.py:263
  34.3 1.4 %collective-permute-start.10 = (bf16[64,1152]{1,0:T(8,128)(2,1)S(1)}, bf16[64,1152]{1,0:T(8,128)(2,1)S(1)}, u32[]{:S(2)}, u32[]{:S(2)}) collective-permute-start(bf16[64,1152]{1,0:T(8,128)(2,1)S(1)} %get-tuple-element.36.low.refs_6_), channel_id=1, source_target_pairs={{0,1},{1,0},{2,3},{3,2},{4,5},{5,4},{6,7},{7,6},{8,9},{9,8},{10,11... | collective-permute-start | bytes 442376 | tf_op jit(solution)/shard_map/ppermute | solution.py:234
  35.8 0.0 collective-permute-done.8.low2.refs_5_
  35.8 1.5 %collective-permute-start.9 = (bf16[64,1152]{1,0:T(8,128)(2,1)S(1)}, bf16[64,1152]{1,0:T(8,128)(2,1)S(1)}, u32[]{:S(2)}, u32[]{:S(2)}) collective-permute-start(bf16[64,1152]{1,0:T(8,128)(2,1)S(1)} %collective-permute-done.8.low2.refs_5_), channel_id=1, source_target_pairs={{0,1},{1,0},{2,3},{3,2},{4,5},{5,4},{6,7},{7,6},{8,9},{9,8},{10,11... | collective-permute-start | bytes 442376 | tf_op jit(solution)/shard_map/ppermute | solution.py:234
  37.3 5.1 %collective-permute-done.6.low1.refs_4_ = bf16[64,1152]{1,0:T(8,128)(2,1)S(1)} collective-permute-done((bf16[64,1152]{1,0:T(8,128)(2,1)S(1)}, bf16[64,1152]{1,0:T(8,128)(2,1)S(1)}, u32[]{:S(2)}, u32[]{:S(2)}) %collective-permute-start.6) | collective-permute-done | bytes 147488 | tf_op jit(solution)/shard_map/ppermute | solution.py:263
  42.4 1.4 %collective-permute-start.7 = (bf16[64,1152]{1,0:T(8,128)(2,1)S(1)}, bf16[64,1152]{1,0:T(8,128)(2,1)S(1)}, u32[]{:S(2)}, u32[]{:S(2)}) collective-permute-start(bf16[64,1152]{1,0:T(8,128)(2,1)S(1)} %collective-permute-done.6.low1.refs_4_), channel_id=1, source_target_pairs={{0,1},{1,0},{2,3},{3,2},{4,5},{5,4},{6,7},{7,6},{8,9},{9,8},{10,11... | collective-permute-start | bytes 442376 | tf_op jit(solution)/shard_map/ppermute | solution.py:234
  43.8 0.0 collective-permute-done.4.low0.refs_3_
  43.8 0.0 collective-permute-start.5
  43.8 0.0 collective-permute-done.10.low_other.refs_7_
  43.8 0.8 partial_a.1.before
  44.6 1.1 %partial_b.1.refs_9_ = f32[64,512]{1,0:T(8,128)S(1)} custom-call(bf16[64,1152]{1,0:T(8,128)(2,1)S(1)} %collective-permute-done.4.low0.refs_3_, bf16[64,1152]{1,0:T(8,128)(2,1)S(1)} %collective-permute-done.6.low1.refs_4_, bf16[64,1152]{1,0:T(8,128)(2,1)S(1)} %collective-permute-done.8.low2.refs_5_, bf16[4,512,1024]{2,1,0:T(8,128)(2,1)S(1)} %get-tuple-element.38.keep_ref, ...), custom_call_target="tpu_custom_call" | custom-call | flops 1048576 | bytes 65536 | tf_op jit(solution)/shard_map/partial_b/pallas_call | solution.py:210
  45.6 0.0 collective-permute-done.9.refs_2_
  45.6 0.0 collective-permute-done.7.refs_1_
  45.7 0.0 collective-permute-done.5.refs_0_
  45.7 1.7 %partial_c.1 = (f32[96,128]{1,0:T(8,128)S(1)}, f32[96,128]{1,0:T(8,128)S(1)}, f32[96,128]{1,0:T(8,128)S(1)}, f32[96,128]{1,0:T(8,128)S(1)}) custom-call(s32[10]{0:T(128)S(1)} %compare_select_fusion.4.place, bf16[64,1152]{1,0:T(8,128)(2,1)S(1)} %collective-permute-done.5.refs_0_, bf16[64,1152]{1,0:T(8,128)(2,1)S(1)} %collective-permute-done.7.refs_1_, ...), custom_call_target="tpu_custom_call" | custom-call | flops 1048576 | bytes 65536 | tf_op jit(solution)/shard_map/partial_c/pallas_call | solution.py:210
  47.3 1.4 %collective-permute-start.11 = (f32[96,128]{1,0:T(8,128)S(1)}, f32[96,128]{1,0:T(8,128)S(1)}, u32[]{:S(2)}, u32[]{:S(2)}) collective-permute-start(f32[96,128]{1,0:T(8,128)S(1)} %get-tuple-element.40), channel_id=1, source_target_pairs={{0,16},{8,24},{16,0},{24,8},{1,17},{9,25},{17,1},{25,9},{2,18},{10... | collective-permute-start | bytes 147464 | tf_op jit(solution)/shard_map/ppermute | solution.py:278
  48.8 0.3 collective-permute-start.12
  49.1 2.4 %collective-permute-start.13 = (f32[96,128]{1,0:T(8,128)S(1)}, f32[96,128]{1,0:T(8,128)S(1)}, u32[]{:S(2)}, u32[]{:S(2)}) collective-permute-start(f32[96,128]{1,0:T(8,128)S(1)} %get-tuple-element.42), channel_id=1, source_target_pairs={{0,24},{8,0},{16,8},{24,16},{1,25},{9,1},{17,9},{25,17},{2,26},{10... | collective-permute-start | bytes 147464 | tf_op jit(solution)/shard_map/ppermute | solution.py:278
  51.4 0.6 collective-permute-done.11
  52.0 1.4 %collective-permute-done.12 = f32[96,128]{1,0:T(8,128)S(1)} collective-permute-done((f32[96,128]{1,0:T(8,128)S(1)}, f32[96,128]{1,0:T(8,128)S(1)}, u32[]{:S(2)}, u32[]{:S(2)}) %collective-permute-start.12) | collective-permute-done | bytes 49184 | tf_op jit(solution)/shard_map/ppermute | solution.py:278
  53.4 0.0 collective-permute-done.13
  53.5 19.1 %all_to_all.16.recv_ref = f32[8,96,128]{2,1,0:T(8,128)S(1)} all-to-all(f32[8,96,128]{2,1,0:T(8,128)S(1)} %broadcast_in_dim.25), channel_id=1, replica_groups=mesh['z'=8,'x'=4,'y'=4,'core'=2] {'z'}, dimensions={0} | all-to-all | bytes 786432 | tf_op jit(solution)/shard_map/all_to_all | solution.py:279
  72.6 3.1 %interval_rows.1 = (f32[32,16,128]{2,1,0:T(8,128)S(1)}, f32[64,64]{1,0:T(8,128)S(1)}) custom-call(f32[8,96,128]{2,1,0:T(8,128)S(1)} %all_to_all.16.recv_ref, f32[16,64]{1,0:T(8,128)S(1)} %get-tuple-element.34.day_ref), custom_call_target="tpu_custom_call" | custom-call | flops 1048576 | bytes 65536 | tf_op jit(solution)/shard_map/interval_rows/pallas_call | solution.py:210
  75.7 17.2 %all_to_all.17.recv_ref = f32[32,16,128]{2,1,0:T(8,128)S(1)} all-to-all(f32[32,16,128]{2,1,0:T(8,128)S(1)} %get-tuple-element.43), channel_id=1, replica_groups=mesh['z'=8,'x'=4,'y'=4,'core'=2] {'x','y','core'}, dimensions={0} | all-to-all | bytes 524288 | tf_op jit(solution)/shard_map/all_to_all | solution.py:283
  93.0 2.9 %day_rows.1 = (f32[32,64]{1,0:T(8,128)}, f32[16,64]{1,0:T(8,128)}) custom-call(s32[10]{0:T(128)S(1)} %compare_select_fusion.4.place, f32[32,16,128]{2,1,0:T(8,128)S(1)} %all_to_all.17.recv_ref, f32[64,64]{1,0:T(8,128)S(1)} %get-tuple-element.44.gram_ref), custom_call_target="tpu_custom_call" | custom-call | flops 1048576 | bytes 65536 | tf_op jit(solution)/shard_map/day_rows/pallas_call | solution.py:210
  (3 shorter events, 0.1 us)
Async XLA Ops:
  4.4 6.4 %collective-permute-start = (f32[4,64,1024]{2,1,0:T(8,128)S(1)}, f32[4,64,1024]{2,1,0:T(8,128)S(1)}, u32[]{:S(2)}, u32[]{:S(2)}) collective-permute-start(f32[4,64,1024]{2,1,0:T(8,128)S(1)} %get-tuple-element.27), channel_id=1, source_target_pairs={{0,1},{1,0},{2,3},{3,2},{4,5},{5,4},{6,7},{7,6},{8,9},{9,8},{10,11... | collective-permute-start | bytes 3145736 | tf_op jit(solution)/shard_map/ppermute | solution.py:234
  10.9 18.4 %collective-permute-start.1 = (f32[64,1024]{1,0:T(8,128)S(1)}, f32[64,1024]{1,0:T(8,128)S(1)}, u32[]{:S(2)}, u32[]{:S(2)}) collective-permute-start(f32[64,1024]{1,0:T(8,128)S(1)} %get-tuple-element.30), channel_id=1, source_target_pairs={{0,2},{2,4},{4,6},{6,0},{1,3},{3,5},{5,7},{7,1},{8,10},{10,12},{12... | collective-permute-start | bytes 786440 | tf_op jit(solution)/shard_map/ppermute | solution.py:254
  11.0 18.3 %collective-permute-start.2 = (f32[64,1024]{1,0:T(8,128)S(1)}, f32[64,1024]{1,0:T(8,128)S(1)}, u32[]{:S(2)}, u32[]{:S(2)}) collective-permute-start(f32[64,1024]{1,0:T(8,128)S(1)} %get-tuple-element.31), channel_id=1, source_target_pairs={{0,4},{2,6},{4,0},{6,2},{1,5},{3,7},{5,1},{7,3},{8,12},{10,14},{12... | collective-permute-start | bytes 786440 | tf_op jit(solution)/shard_map/ppermute | solution.py:254
  13.2 16.1 %collective-permute-start.3 = (f32[64,1024]{1,0:T(8,128)S(1)}, f32[64,1024]{1,0:T(8,128)S(1)}, u32[]{:S(2)}, u32[]{:S(2)}) collective-permute-start(f32[64,1024]{1,0:T(8,128)S(1)} %get-tuple-element.32), channel_id=1, source_target_pairs={{0,6},{2,0},{4,2},{6,4},{1,7},{3,1},{5,3},{7,5},{8,14},{10,8},{12,... | collective-permute-start | bytes 786440 | tf_op jit(solution)/shard_map/ppermute | solution.py:254
  30.6 5.2 %collective-permute-start.8 = (bf16[64,1152]{1,0:T(8,128)(2,1)S(1)}, bf16[64,1152]{1,0:T(8,128)(2,1)S(1)}, u32[]{:S(2)}, u32[]{:S(2)}) collective-permute-start(bf16[64,1152]{1,0:T(8,128)(2,1)S(1)} %get-tuple-element.36.low.refs_6_), channel_id=1, source_target_pairs={{0,6},{2,0},{4,2},{6,4},{1,7},{3,1},{5,3},{7,5},{8,14},{10,8},{12,... | collective-permute-start | bytes 442376 | tf_op jit(solution)/shard_map/ppermute | solution.py:263
  33.2 9.2 %collective-permute-start.6 = (bf16[64,1152]{1,0:T(8,128)(2,1)S(1)}, bf16[64,1152]{1,0:T(8,128)(2,1)S(1)}, u32[]{:S(2)}, u32[]{:S(2)}) collective-permute-start(bf16[64,1152]{1,0:T(8,128)(2,1)S(1)} %get-tuple-element.36.low.refs_6_), channel_id=1, source_target_pairs={{0,2},{2,4},{4,6},{6,0},{1,3},{3,5},{5,7},{7,1},{8,10},{10,12},{12... | collective-permute-start | bytes 442376 | tf_op jit(solution)/shard_map/ppermute | solution.py:263
  33.2 10.6 %collective-permute-start.4 = (bf16[64,1152]{1,0:T(8,128)(2,1)S(1)}, bf16[64,1152]{1,0:T(8,128)(2,1)S(1)}, u32[]{:S(2)}, u32[]{:S(2)}) collective-permute-start(bf16[64,1152]{1,0:T(8,128)(2,1)S(1)} %get-tuple-element.36.low.refs_6_), channel_id=1, source_target_pairs={{0,4},{2,6},{4,0},{6,2},{1,5},{3,7},{5,1},{7,3},{8,12},{10,14},{12... | collective-permute-start | bytes 442376 | tf_op jit(solution)/shard_map/ppermute | solution.py:263
  34.3 9.5 %collective-permute-start.10 = (bf16[64,1152]{1,0:T(8,128)(2,1)S(1)}, bf16[64,1152]{1,0:T(8,128)(2,1)S(1)}, u32[]{:S(2)}, u32[]{:S(2)}) collective-permute-start(bf16[64,1152]{1,0:T(8,128)(2,1)S(1)} %get-tuple-element.36.low.refs_6_), channel_id=1, source_target_pairs={{0,1},{1,0},{2,3},{3,2},{4,5},{5,4},{6,7},{7,6},{8,9},{9,8},{10,11... | collective-permute-start | bytes 442376 | tf_op jit(solution)/shard_map/ppermute | solution.py:234
  35.8 9.9 %collective-permute-start.9 = (bf16[64,1152]{1,0:T(8,128)(2,1)S(1)}, bf16[64,1152]{1,0:T(8,128)(2,1)S(1)}, u32[]{:S(2)}, u32[]{:S(2)}) collective-permute-start(bf16[64,1152]{1,0:T(8,128)(2,1)S(1)} %collective-permute-done.8.low2.refs_5_), channel_id=1, source_target_pairs={{0,1},{1,0},{2,3},{3,2},{4,5},{5,4},{6,7},{7,6},{8,9},{9,8},{10,11... | collective-permute-start | bytes 442376 | tf_op jit(solution)/shard_map/ppermute | solution.py:234
  42.4 3.3 %collective-permute-start.7 = (bf16[64,1152]{1,0:T(8,128)(2,1)S(1)}, bf16[64,1152]{1,0:T(8,128)(2,1)S(1)}, u32[]{:S(2)}, u32[]{:S(2)}) collective-permute-start(bf16[64,1152]{1,0:T(8,128)(2,1)S(1)} %collective-permute-done.6.low1.refs_4_), channel_id=1, source_target_pairs={{0,1},{1,0},{2,3},{3,2},{4,5},{5,4},{6,7},{7,6},{8,9},{9,8},{10,11... | collective-permute-start | bytes 442376 | tf_op jit(solution)/shard_map/ppermute | solution.py:234
  43.8 1.9 %collective-permute-start.5 = (bf16[64,1152]{1,0:T(8,128)(2,1)S(1)}, bf16[64,1152]{1,0:T(8,128)(2,1)S(1)}, u32[]{:S(2)}, u32[]{:S(2)}) collective-permute-start(bf16[64,1152]{1,0:T(8,128)(2,1)S(1)} %collective-permute-done.4.low0.refs_3_), channel_id=1, source_target_pairs={{0,1},{1,0},{2,3},{3,2},{4,5},{5,4},{6,7},{7,6},{8,9},{9,8},{10,11... | collective-permute-start | bytes 442376 | tf_op jit(solution)/shard_map/ppermute | solution.py:234
  47.3 4.7 %collective-permute-start.11 = (f32[96,128]{1,0:T(8,128)S(1)}, f32[96,128]{1,0:T(8,128)S(1)}, u32[]{:S(2)}, u32[]{:S(2)}) collective-permute-start(f32[96,128]{1,0:T(8,128)S(1)} %get-tuple-element.40), channel_id=1, source_target_pairs={{0,16},{8,24},{16,0},{24,8},{1,17},{9,25},{17,1},{25,9},{2,18},{10... | collective-permute-start | bytes 147464 | tf_op jit(solution)/shard_map/ppermute | solution.py:278
  48.8 4.7 %collective-permute-start.12 = (f32[96,128]{1,0:T(8,128)S(1)}, f32[96,128]{1,0:T(8,128)S(1)}, u32[]{:S(2)}, u32[]{:S(2)}) collective-permute-start(f32[96,128]{1,0:T(8,128)S(1)} %get-tuple-element.41), channel_id=1, source_target_pairs={{0,8},{8,16},{16,24},{24,0},{1,9},{9,17},{17,25},{25,1},{2,10},{10... | collective-permute-start | bytes 147464 | tf_op jit(solution)/shard_map/ppermute | solution.py:278
  49.1 4.4 %collective-permute-start.13 = (f32[96,128]{1,0:T(8,128)S(1)}, f32[96,128]{1,0:T(8,128)S(1)}, u32[]{:S(2)}, u32[]{:S(2)}) collective-permute-start(f32[96,128]{1,0:T(8,128)S(1)} %get-tuple-element.42), channel_id=1, source_target_pairs={{0,24},{8,0},{16,8},{24,16},{1,25},{9,1},{17,9},{25,17},{2,26},{10... | collective-permute-start | bytes 147464 | tf_op jit(solution)/shard_map/ppermute | solution.py:278

commit v3 on v2

v3 whole, which is shorter than its diff:
```python
import functools

import jax
import jax.numpy as jnp
from jax import lax
from jax.experimental import pallas as pl
from jax.experimental.pallas import tpu as pltpu
from jax.sharding import Mesh, PartitionSpec as P

RANK = 64
HALF = 512
HIGH = lax.Precision.HIGHEST
F32 = jnp.float32
BF16 = jnp.bfloat16


def shifts(n, d):
    return [(i, (i + d) % n) for i in range(n)]


def iota(shape, dim):
    return lax.broadcasted_iota(jnp.int32, shape, dim)


def dot(a, b, contract=((1,), (0,)), precision=HIGH):
    return lax.dot_general(a, b, (contract, ((), ())), precision=precision, preferred_element_type=F32)


def shifted(system):
    eye = iota((RANK, RANK), 0) == iota((RANK, RANK), 1)
    trace = jnp.sum(jnp.sum(jnp.where(eye, system, 0.0), axis=1, keepdims=True), axis=0, keepdims=True)
    return system + jnp.where(eye, 0.01 * trace / RANK, 0.0)


def eliminate(system, rhs):
    work = jnp.concatenate([system, rhs], axis=1)
    parts = [work[at : at + 8] for at in range(0, RANK, 8)]
    row = iota((8, 1), 0)
    for p in range(RANK // 8):
        rows = parts[p]
        columns = [jnp.broadcast_to(rows[:, 8 * p + j : 8 * p + j + 1], rows.shape) for j in range(8)]
        for j in range(8):
            inverse = 1.0 / columns[j][j : j + 1]
            scaled = rows[j : j + 1] * inverse
            rows = jnp.where(row == j, scaled, rows - columns[j] * scaled)
            for i in range(j + 1, 8):
                scaled = columns[i][j : j + 1] * inverse
                columns[i] = jnp.where(row == j, scaled, columns[i] - columns[j] * scaled)
        for q in range(RANK // 8):
            if q != p:
                taken = parts[q][:, 8 * p : 8 * p + 1] * rows[0:1]
                for j in range(1, 8):
                    taken = taken + parts[q][:, 8 * p + j : 8 * p + j + 1] * rows[j : j + 1]
                parts[q] = parts[q] - taken
        parts[p] = rows
    return jnp.concatenate(parts, axis=0)


def to_lanes(gram):
    return jnp.concatenate([gram[at : at + 8] for at in range(0, RANK, 8)], axis=1)


def from_lanes(wide):
    return jnp.concatenate([wide[:, at : at + RANK] for at in range(0, 8 * RANK, RANK)], axis=0)


def load_blocks(place, slab_ref, held_ref, sems, core):
    copies = []
    for d in range(4):
        at = pl.multiple_of((2 * lax.rem(place[1] + d, 4) + core) * 1024, 1024)
        copies.append(pltpu.make_async_copy(slab_ref.at[:, pl.ds(at, 1024)], held_ref.at[d], sems.at[d]))
        copies[-1].start()
    return copies


def send_kernel(
    place, slab_ref, interval_ref, day_ref, sums_ref, held_ref, khatri_ref, gram_day_ref, day_twice_ref, sems, *own
):
    factor, day, small_sems = own
    small = [
        pltpu.make_async_copy(interval_ref, factor, small_sems.at[0]),
        pltpu.make_async_copy(day_ref, day, small_sems.at[1]),
    ]
    for copy in small:
        copy.start()
    copies = load_blocks(place, slab_ref, held_ref, sems, 1 - place[0])
    for copy in small:
        copy.wait()
    product = factor[...][:, None, :] * day[...][None, :, :]
    khatri = product.reshape(product.shape[0] * product.shape[1], RANK).T.astype(BF16)
    khatri_ref[...] = khatri
    sums_ref[4 * RANK :, : 8 * RANK] = to_lanes(dot(factor[...], factor[...], ((0,), (0,))))
    sums_ref[4 * RANK :, 8 * RANK :] = jnp.zeros((8, 1024 - 8 * RANK), F32)
    gram_day_ref[...] = dot(day[...], day[...], ((0,), (0,)))
    day_twice_ref[...] = jnp.concatenate([day[...], day[...]], axis=1)
    for d in range(4):
        copies[d].wait()
        sums_ref[d * RANK : (d + 1) * RANK] = dot(khatri, held_ref[d], precision=None)


def keep_kernel(place, slab_ref, khatri_ref, sums_ref, held_ref, sems):
    copies = load_blocks(place, slab_ref, held_ref, sems, place[0])
    for d in range(4):
        copies[d].wait()
        sums_ref[d] = dot(khatri_ref[...], held_ref[d], precision=None)


def pack(gram):
    return jnp.concatenate([gram[: RANK // 2], gram[RANK // 2 :]], axis=1)


def unpack(packed):
    return jnp.concatenate([packed[:, :RANK], packed[:, RANK:]], axis=0)


def add_kernel(keep_ref, sent_ref, got_ref, own, two, one_a, three_a, one_b, three_b):
    gram = sent_ref[4 * RANK :, : 8 * RANK] + got_ref[4 * RANK :, : 8 * RANK]

    def total(d, lanes):
        return keep_ref[d, :, lanes] + got_ref[d * RANK : (d + 1) * RANK, lanes]

    for d, out in ((0, own), (2, two)):
        out[:RANK] = total(d, slice(0, 1024))
        out[RANK:, : 8 * RANK] = gram
        out[RANK:, 8 * RANK :] = jnp.zeros((8, 1024 - 8 * RANK), F32)
    for d, first, second in ((1, one_a, one_b), (3, three_a, three_b)):
        first[:RANK] = total(d, slice(0, HALF))
        first[RANK:] = gram
        second[...] = total(d, slice(HALF, 1024))


def inverse_kernel(own, two, one, three, gram_day_ref, inverse_ref):
    gram = (own[RANK:, : 8 * RANK] + two[RANK:, : 8 * RANK]) + (one[RANK:] + three[RANK:])
    inverse_ref[...] = inverse_of(from_lanes(gram) * gram_day_ref[...])


def link_kernel(own, two, one_a, three_a, one_b, three_b, inverse_ref, link_ref, low_ref):
    first = (own[:RANK, :HALF] + two[:RANK, :HALF]) + (one_a[:RANK] + three_a[:RANK])
    second = (own[:RANK, HALF:] + two[:RANK, HALF:]) + (one_b[...] + three_b[...])
    link = dot(inverse_ref[...], jnp.concatenate([first, second], axis=1))
    link_ref[...] = link
    low_ref[:, :1024] = link.astype(BF16)
    gram = dot(link, link, ((1,), (1,)))
    high = gram.astype(BF16)
    rest = (gram - high.astype(F32)).astype(BF16)
    low_ref[:, 1024:] = jnp.concatenate([high, rest], axis=1)


def times_blocks(lows, held_ref, blocks):
    total = None
    for low, i in zip(lows, blocks):
        term = dot(held_ref[i], low[:, : 1024], ((1,), (1,)), None)
        total = term if total is None else total + term
    return total


def first_partial_kernel(low, low_other, keep_ref, send_ref, acc):
    acc[...] = times_blocks((low,), keep_ref, (0,)) + times_blocks((low_other,), send_ref, (0,))


def second_partial_kernel(low0, low1, low2, keep_ref, before, acc):
    acc[...] = before[...] + times_blocks((low0, low1, low2), keep_ref, (2, 3, 1))


def last_partial_kernel(place, *refs):
    lows, (held, before), outs, acc = refs[:8], refs[8:10], refs[10:14], refs[14]
    acc[...] = before[...] + times_blocks(lows[:3], held, (2, 3, 1))
    halves = [low[:, 1024 :].astype(F32) for low in lows]
    total = halves[0]
    for half in halves[1:]:
        total = total + half
    packed = pack(total[:, :RANK] + total[:, RANK:])
    for d, out in enumerate(outs):
        at = pl.multiple_of(lax.rem(place[2] + d, 4) * 128, 128)
        out[:RANK] = jnp.concatenate([acc[pl.ds(at, RANK)], acc[pl.ds(at + RANK, RANK)]], axis=1)
        out[RANK:] = packed


def inverse_of(system):
    eye = jnp.where(iota((RANK, RANK), 0) == iota((RANK, RANK), 1), 1.0, 0.0).astype(F32)
    return eliminate(shifted(system), eye)[:, RANK:]


def solve_rows(system, rows):
    count = rows.shape[0]
    wide = jnp.concatenate([rows, jnp.zeros((count, RANK), F32)], axis=1)
    rhs = jnp.concatenate([jnp.transpose(wide)[:RANK], jnp.zeros((RANK, RANK - count), F32)], axis=1)
    return jnp.transpose(eliminate(shifted(system), rhs))[RANK : RANK + count]


def interval_kernel(place, total_ref, other_ref, gram_day_ref, day_ref, out_ref, gram_ref):
    gram = unpack(total_ref[RANK:] + other_ref[RANK:])
    gram_ref[...] = gram
    partial = (total_ref[:RANK] + other_ref[:RANK]).reshape(4, 16, 2 * RANK)
    sums = jnp.sum(partial * day_ref[...][None], axis=1)
    rows = solve_rows(gram * gram_day_ref[...], jnp.concatenate([sums[:, :RANK], sums[:, RANK:]], axis=0))
    day_part = jnp.sum(partial * jnp.concatenate([rows[:4], rows[4:]], axis=1)[:, None, :], axis=0)
    day_part = day_part[:, :RANK] + day_part[:, RANK:]
    none = jnp.zeros((8, RANK), F32)
    out_ref[:8] = jnp.concatenate([day_part[:8], day_part[8:]], axis=1)
    out_ref[8:] = jnp.where(
        place[0] == 0, jnp.concatenate([rows, none], axis=1), jnp.concatenate([none, rows], axis=1)
    )


def day_kernel(place, recv_ref, gram_ref, interval_ref, day_ref):
    rows = recv_ref[:, 8:].reshape(8 * recv_ref.shape[0], 2 * RANK)
    gram_new = dot(rows, rows, ((0,), (0,)))
    gram_new = gram_new[:RANK, :RANK] + gram_new[RANK:, RANK:]
    total = recv_ref[0, :8]
    for i in range(1, recv_ref.shape[0]):
        total = total + recv_ref[i, :8]
    for i in range(4):
        both = recv_ref[i * 4 + place[1], 8:]
        interval_ref[i * 8 : i * 8 + 8] = jnp.where(place[0] == 0, both[:, :RANK], both[:, RANK:])
    day_ref[...] = solve_rows(
        gram_ref[...] * gram_new, jnp.concatenate([total[:, :RANK], total[:, RANK:]], axis=0)
    )


def shape(dims, dtype=F32):
    return jax.ShapeDtypeStruct(dims, dtype)


def call(kernel, out_shape, args, name, spaces=None, scratch=()):
    spaces = spaces or {}
    return pl.pallas_call(
        kernel,
        out_shape=out_shape,
        in_specs=[pl.BlockSpec(memory_space=spaces.get(i, pltpu.VMEM)) for i in range(len(args))],
        out_specs=jax.tree.map(lambda _: pl.BlockSpec(memory_space=pltpu.VMEM), out_shape),
        scratch_shapes=scratch,
        compiler_params=pltpu.CompilerParams(vmem_limit_bytes=16 * 2**20),
        cost_estimate=pl.CostEstimate(flops=2**20, bytes_accessed=2**16, transcendentals=0),
        name=name,
    )(*args)


def body(slab, interval_factor, day_factor):
    intervals, days, links = slab.shape
    flat = pltpu.with_memory_space_constraint(slab.reshape(intervals * days, links), pltpu.HBM)
    interval_factor = pltpu.with_memory_space_constraint(interval_factor, pltpu.HBM)
    day_factor = pltpu.with_memory_space_constraint(day_factor, pltpu.HBM)
    place = jnp.stack([lax.axis_index(axis) for axis in ("core", "y", "x")]).astype(jnp.int32)
    held = shape((4, 512, 1024), BF16)
    smem = {0: pltpu.SMEM}

    def other_core(a):
        return lax.ppermute(a, "core", shifts(2, 1))

    def along_y(a, d):
        return lax.ppermute(a, "y", shifts(4, d))

    send, held_send, khatri, gram_day, day_twice = call(
        send_kernel,
        (shape((264, 1024)), held, shape((RANK, 512), BF16), shape((RANK, RANK)), shape((16, 2 * RANK))),
        (place, flat, interval_factor, day_factor),
        "sums_to_send",
        {0: pltpu.SMEM, 1: pl.ANY, 2: pl.ANY, 3: pl.ANY},
        [
            pltpu.SemaphoreType.DMA((4,)),
            pltpu.VMEM((32, RANK), F32),
            pltpu.VMEM((16, RANK), F32),
            pltpu.SemaphoreType.DMA((2,)),
        ],
    )
    got = other_core(send)
    keep, held_keep = call(
        keep_kernel,
        (shape((4, RANK, 1024)), held),
        (place, flat, khatri),
        "sums_to_keep",
        {0: pltpu.SMEM, 1: pl.ANY},
        [pltpu.SemaphoreType.DMA((4,))],
    )
    sums = call(
        add_kernel,
        (shape((72, 1024)),) * 2 + (shape((72, HALF)),) * 2 + (shape((RANK, HALF)),) * 2,
        (keep, send, got),
        "add_cores",
    )
    parts = [sums[0]] + [along_y(one, d) for one, d in zip(sums[1:], (2, 1, 3, 1, 3))]
    inverse = call(inverse_kernel, shape((RANK, RANK)), (*parts[:4], gram_day), "link_inverse")
    link, low = call(
        link_kernel, (shape((RANK, 1024)), shape((RANK, 1152), BF16)), (*parts, inverse), "link_rows"
    )
    lows = [along_y(low, d) for d in (2, 1, 3)]
    low_other = other_core(low)
    acc = call(first_partial_kernel, shape((512, RANK)), (low, low_other, held_keep, held_send), "partial_own")
    lows = [lax.optimization_barrier((one, acc))[0] for one in lows]
    others = [other_core(one) for one in lows]
    acc = call(second_partial_kernel, shape((512, RANK)), (*lows, held_keep, acc), "partial_own_core")
    outgoing = call(
        last_partial_kernel,
        (shape((96, 128)),) * 4,
        (place, *others, *lows, low, low_other, held_send, acc),
        "partial_other_core",
        smem,
        [pltpu.VMEM((512, RANK), F32)],
    )
    over_x = sum([lax.ppermute(outgoing[d], "x", shifts(4, d)) for d in (2, 1, 3)], outgoing[0])
    over_z = sum([lax.ppermute(over_x, "z", shifts(8, d)) for d in (6, 2, 4)], over_x)
    z_other = lax.ppermute(over_z, "z", [(i, i ^ 1) for i in range(8)])
    found, gram_link = call(
        interval_kernel,
        (shape((16, 128)), shape((RANK, RANK))),
        (place, over_z, z_other, gram_day, day_twice),
        "interval_rows",
        smem,
    )
    found = found + other_core(found)
    everyone = lax.all_to_all(jnp.broadcast_to(found[None], (16, 16, 128)), ("x", "y"), 0, 0)
    interval_new, day_new = call(
        day_kernel, (shape((32, RANK)), shape((16, RANK))), (place, everyone, gram_link), "day_rows", smem
    )
    return link.T, interval_new, day_new


def solution(mesh):
    split = Mesh(mesh.devices.reshape(8, 4, 4, 2), ("z", "x", "y", "core"))
    link, intv = ("z", "x"), ("y", "core")
    return jax.shard_map(
        body,
        mesh=split,
        in_specs=(P(intv, None, link), P(intv, None), P()),
        out_specs=(P(link + intv, None), P(intv, None), P()),
        check_vma=False,
    )
```

time: 96.1 us -> 88.4 us (0.920)
  blocking collectives: 49.6 us -> 10.8 us
  starting transfers between devices: 18.8 us -> 35.1 us
  waiting for transfers between devices: 7.14 us -> 22.7 us
    all_to_all x3 -> x1, blocking collectives: 49.6 us -> 10.8 us  [body(): lax.all_to_all(jnp.broadcast_to(found[None], (16, 16, 128)), ('x', 'y'),...]
    ppermute x6 -> x12, waiting for transfers between devices: 5.13 us -> 20.3 us  [the longest x8 15.5 us: along_y(): return lax.ppermute(a, 'y', shifts(4, d))]
    ppermute x6 -> x12, starting transfers between devices: 7.07 us -> 20.5 us  [the longest x3 10.6 us: body(): lax.ppermute(over_x, 'z', shifts(8, d))]
    ppermute x5 -> x6, starting transfers between devices: 7.66 us -> 9.11 us  [other_core(): return lax.ppermute(a, 'core', shifts(2, 1))]
    ppermute x3, starting transfers between devices: 4.12 us -> 5.5 us  [body(): lax.ppermute(outgoing[d], 'x', shifts(4, d))]
  transfers between devices with their start and end apart: 14 -> 21, of which waited for: 3 -> 10; matrix products, arithmetic and copies ran while one was open for 0% -> 0% of each run, Pallas kernels for 7% -> 7%
where the time goes in v3:
time: 88.4 us; the launch traced here: 88.1 us
  starting transfers between devices  35.1 us (40%)
  waiting for transfers between devices  22.7 us (26%)
  Pallas kernels  18.6 us (21%)
  blocking collectives  10.8 us (12%)
    pallas_call x10, Pallas kernels, call(): pl.pallas_call(kernel, out_shape=out_shape, in_specs=[pl.BlockSpec(memory...  18.6 us
    ppermute x8, waiting for transfers between devices, along_y(): return lax.ppermute(a, 'y', shifts(4, d))  15.5 us
    all_to_all x1, blocking collectives, body(): lax.all_to_all(jnp.broadcast_to(found[None], (16, 16, 128)), ('x', 'y'),...  10.8 us
    ppermute x3, starting transfers between devices, body(): lax.ppermute(over_x, 'z', shifts(8, d))  10.6 us
    ppermute x8, starting transfers between devices, along_y(): return lax.ppermute(a, 'y', shifts(4, d))  9.32 us
    ppermute x6, starting transfers between devices, other_core(): return lax.ppermute(a, 'core', shifts(2, 1))  9.11 us
    ppermute x3, starting transfers between devices, body(): lax.ppermute(outgoing[d], 'x', shifts(4, d))  5.5 us
    ppermute x1, waiting for transfers between devices, body(): z_other = lax.ppermute(over_z, 'z', [(i, i ^ 1) for i in range(8)])  2.51 us
  transfers between devices with their start and end apart: 21, of which 10 were waited for; matrix products, arithmetic and copies ran while one was open for 0% of the time, Pallas kernels for 7%

profile of v3, /device:TPU:1, one launch (start us, length us, event | category | flops | bytes accessed | tf_op | source)
XLA Modules:
  0.0 88.1 jit_solution(13449755215354155615)
XLA Ops:
  0.6 0.1 pad_add_fusion.place
  0.7 3.8 %sums_to_send.1 = (f32[264,1024]{1,0:T(8,128)S(1)}, bf16[4,512,1024]{2,1,0:T(8,128)(2,1)S(1)}, bf16[64,512]{1,0:T(8,128)(2,1)S(1)}, f32[64,64]{1,0:T(8,128)S(1)}, f32[16,128]{1,0:T(8,128)S(1)}) custom-call(s32[3]{0:T(128)S(1)} %pad_add_fusion.place, bf16[512,8192]{1,0:T(8,128)(2,1)} %bitcast.5, f32[32,64]{1,0:T(8,128)} %interval_ref.1, f32[16,64]{1,0:T(8,128)} %day_ref.1), custom_call_target="tpu_custom_call" | custom-call | flops 1048576 | bytes 65536 | tf_op jit(solution)/shard_map/sums_to_send/pallas_call | solution.py:227
  4.5 3.3 %collective-permute-start = (f32[264,1024]{1,0:T(8,128)S(1)}, f32[264,1024]{1,0:T(8,128)S(1)}, u32[]{:S(2)}, u32[]{:S(2)}) collective-permute-start(f32[264,1024]{1,0:T(8,128)S(1)} %get-tuple-element.31.sent_ref), channel_id=1, source_target_pairs={{0,1},{1,0},{2,3},{3,2},{4,5},{5,4},{6,7},{7,6},{8,9},{9,8},{10,11... | collective-permute-start | bytes 3244040 | tf_op jit(solution)/shard_map/ppermute | solution.py:249
  7.8 3.1 %sums_to_keep.1 = (f32[4,64,1024]{2,1,0:T(8,128)S(1)}, bf16[4,512,1024]{2,1,0:T(8,128)(2,1)S(1)}) custom-call(s32[3]{0:T(128)S(1)} %pad_add_fusion.place, bf16[512,8192]{1,0:T(8,128)(2,1)} %bitcast.6, bf16[64,512]{1,0:T(8,128)(2,1)S(1)} %get-tuple-element.29.khatri_ref), custom_call_target="tpu_custom_call" | custom-call | flops 1048576 | bytes 65536 | tf_op jit(solution)/shard_map/sums_to_keep/pallas_call | solution.py:227
  10.9 0.1 add_cores.1
  11.0 1.3 %collective-permute-start.1 = (f32[72,1024]{1,0:T(8,128)S(1)}, f32[72,1024]{1,0:T(8,128)S(1)}, u32[]{:S(2)}, u32[]{:S(2)}) collective-permute-start(f32[72,1024]{1,0:T(8,128)S(1)} %get-tuple-element.33), channel_id=1, source_target_pairs={{0,4},{2,6},{4,0},{6,2},{1,5},{3,7},{5,1},{7,3},{8,12},{10,14},{12... | collective-permute-start | bytes 884744 | tf_op jit(solution)/shard_map/ppermute | solution.py:252
  12.3 0.4 collective-permute-start.2
  12.7 2.3 %collective-permute-start.3 = (f32[72,512]{1,0:T(8,128)S(1)}, f32[72,512]{1,0:T(8,128)S(1)}, u32[]{:S(2)}, u32[]{:S(2)}) collective-permute-start(f32[72,512]{1,0:T(8,128)S(1)} %get-tuple-element.35), channel_id=1, source_target_pairs={{0,6},{2,0},{4,2},{6,4},{1,7},{3,1},{5,3},{7,5},{8,14},{10,8},{12,... | collective-permute-start | bytes 442376 | tf_op jit(solution)/shard_map/ppermute | solution.py:252
  15.0 2.7 %collective-permute-start.5 = (f32[64,512]{1,0:T(8,128)S(1)}, f32[64,512]{1,0:T(8,128)S(1)}, u32[]{:S(2)}, u32[]{:S(2)}) collective-permute-start(f32[64,512]{1,0:T(8,128)S(1)} %get-tuple-element.37), channel_id=1, source_target_pairs={{0,6},{2,0},{4,2},{6,4},{1,7},{3,1},{5,3},{7,5},{8,14},{10,8},{12,... | collective-permute-start | bytes 393224 | tf_op jit(solution)/shard_map/ppermute | solution.py:252
  17.7 7.1 %collective-permute-done.2.one.one_a = f32[72,512]{1,0:T(8,128)S(1)} collective-permute-done((f32[72,512]{1,0:T(8,128)S(1)}, f32[72,512]{1,0:T(8,128)S(1)}, u32[]{:S(2)}, u32[]{:S(2)}) %collective-permute-start.2) | collective-permute-done | bytes 147488 | tf_op jit(solution)/shard_map/ppermute | solution.py:252
  24.8 0.0 collective-permute-done.3.three.three_a
  24.8 0.0 collective-permute-done.1.two
  24.8 1.6 %link_inverse.1.inverse_ref = f32[64,64]{1,0:T(8,128)S(1)} custom-call(f32[72,1024]{1,0:T(8,128)S(1)} %get-tuple-element.32.own, f32[72,1024]{1,0:T(8,128)S(1)} %collective-permute-done.1.two, f32[72,512]{1,0:T(8,128)S(1)} %collective-permute-done.2.one.one_a, f32[72,512]{1,0:T(8,128)S(1)} %collective-permute-done.3.three.three_a, ...), custom_call_target="tpu_custom_call" | custom-call | flops 1048576 | bytes 65536 | tf_op jit(solution)/shard_map/link_inverse/pallas_call | solution.py:227
  26.3 1.2 %collective-permute-done.4.one_b = f32[64,512]{1,0:T(8,128)S(1)} collective-permute-done((f32[64,512]{1,0:T(8,128)S(1)}, f32[64,512]{1,0:T(8,128)S(1)}, u32[]{:S(2)}, u32[]{:S(2)}) %collective-permute-start.4) | collective-permute-done | bytes 131104 | tf_op jit(solution)/shard_map/ppermute | solution.py:252
  27.6 1.2 %link_rows.1 = (f32[64,1024]{1,0:T(8,128)}, bf16[64,1152]{1,0:T(8,128)(2,1)S(1)}) custom-call(f32[72,1024]{1,0:T(8,128)S(1)} %get-tuple-element.32.own, f32[72,1024]{1,0:T(8,128)S(1)} %collective-permute-done.1.two, f32[72,512]{1,0:T(8,128)S(1)} %collective-permute-done.2.one.one_a, f32[72,512]{1,0:T(8,128)S(1)} %collective-permute-done.3.three.three_a, ...), custom_call_target="tpu_custom_call" | custom-call | flops 1048576 | bytes 65536 | tf_op jit(solution)/shard_map/link_rows/pallas_call | solution.py:227
  28.8 0.5 collective-permute-start.7
  29.3 1.0 %collective-permute-start.11 = (bf16[64,1152]{1,0:T(8,128)(2,1)S(1)}, bf16[64,1152]{1,0:T(8,128)(2,1)S(1)}, u32[]{:S(2)}, u32[]{:S(2)}) collective-permute-start(bf16[64,1152]{1,0:T(8,128)(2,1)S(1)} %get-tuple-element.40.low.refs_6_), channel_id=1, source_target_pairs={{0,6},{2,0},{4,2},{6,4},{1,7},{3,1},{5,3},{7,5},{8,14},{10,8},{12,... | collective-permute-start | bytes 442376 | tf_op jit(solution)/shard_map/ppermute | solution.py:252
  30.3 0.5 collective-permute-start.9
  30.7 1.2 %collective-permute-start.6 = (bf16[64,1152]{1,0:T(8,128)(2,1)S(1)}, bf16[64,1152]{1,0:T(8,128)(2,1)S(1)}, u32[]{:S(2)}, u32[]{:S(2)}) collective-permute-start(bf16[64,1152]{1,0:T(8,128)(2,1)S(1)} %get-tuple-element.40.low.refs_6_), channel_id=1, source_target_pairs={{0,4},{2,6},{4,0},{6,2},{1,5},{3,7},{5,1},{7,3},{8,12},{10,14},{12... | collective-permute-start | bytes 442376 | tf_op jit(solution)/shard_map/ppermute | solution.py:252
  31.9 0.0 collective-permute-done.7.low_other.refs_7_
  32.0 0.7 partial_own.1.before
  32.6 2.1 %collective-permute-done.11.low2.refs_5_ = bf16[64,1152]{1,0:T(8,128)(2,1)S(1)} collective-permute-done((bf16[64,1152]{1,0:T(8,128)(2,1)S(1)}, bf16[64,1152]{1,0:T(8,128)(2,1)S(1)}, u32[]{:S(2)}, u32[]{:S(2)}) %collective-permute-start.11) | collective-permute-done | bytes 147488 | tf_op jit(solution)/shard_map/ppermute | solution.py:252
  34.7 5.1 %collective-permute-done.9.low1.refs_4_ = bf16[64,1152]{1,0:T(8,128)(2,1)S(1)} collective-permute-done((bf16[64,1152]{1,0:T(8,128)(2,1)S(1)}, bf16[64,1152]{1,0:T(8,128)(2,1)S(1)}, u32[]{:S(2)}, u32[]{:S(2)}) %collective-permute-start.9) | collective-permute-done | bytes 147488 | tf_op jit(solution)/shard_map/ppermute | solution.py:252
  39.8 1.1 %collective-permute-start.8 = (bf16[64,1152]{1,0:T(8,128)(2,1)S(1)}, bf16[64,1152]{1,0:T(8,128)(2,1)S(1)}, u32[]{:S(2)}, u32[]{:S(2)}) collective-permute-start(bf16[64,1152]{1,0:T(8,128)(2,1)S(1)} %collective-permute-done.6.low0.refs_3_), channel_id=1, source_target_pairs={{0,1},{1,0},{2,3},{3,2},{4,5},{5,4},{6,7},{7,6},{8,9},{9,8},{10,11... | collective-permute-start | bytes 442376 | tf_op jit(solution)/shard_map/ppermute | solution.py:249
  40.9 0.0 collective-permute-start.10
  40.9 0.5 collective-permute-start.12
  41.4 1.0 %partial_own_core.1.refs_9_ = f32[512,64]{1,0:T(8,128)S(1)} custom-call(bf16[64,1152]{1,0:T(8,128)(2,1)S(1)} %collective-permute-done.6.low0.refs_3_, bf16[64,1152]{1,0:T(8,128)(2,1)S(1)} %collective-permute-done.9.low1.refs_4_, bf16[64,1152]{1,0:T(8,128)(2,1)S(1)} %collective-permute-done.11.low2.refs_5_, ...), custom_call_target="tpu_custom_call" | custom-call | flops 1048576 | bytes 65536 | tf_op jit(solution)/shard_map/partial_own_core/pallas_call | solution.py:227
  42.4 0.0 collective-permute-done.8.refs_0_
  42.4 0.0 collective-permute-done.10.refs_1_
  42.4 0.1 collective-permute-done.12.refs_2_
  42.5 1.6 %partial_other_core.1 = (f32[96,128]{1,0:T(8,128)S(1)}, f32[96,128]{1,0:T(8,128)S(1)}, f32[96,128]{1,0:T(8,128)S(1)}, f32[96,128]{1,0:T(8,128)S(1)}) custom-call(s32[3]{0:T(128)S(1)} %pad_add_fusion.place, bf16[64,1152]{1,0:T(8,128)(2,1)S(1)} %collective-permute-done.8.refs_0_, bf16[64,1152]{1,0:T(8,128)(2,1)S(1)} %collective-permute-done.10.refs_1_, ...), custom_call_target="tpu_custom_call" | custom-call | flops 1048576 | bytes 65536 | tf_op jit(solution)/shard_map/partial_other_core/pallas_call | solution.py:227
  44.1 2.8 %collective-permute-start.13 = (f32[96,128]{1,0:T(8,128)S(1)}, f32[96,128]{1,0:T(8,128)S(1)}, u32[]{:S(2)}, u32[]{:S(2)}) collective-permute-start(f32[96,128]{1,0:T(8,128)S(1)} %get-tuple-element.47), channel_id=1, source_target_pairs={{0,16},{8,24},{16,0},{24,8},{1,17},{9,25},{17,1},{25,9},{2,18},{10... | collective-permute-start | bytes 147464 | tf_op jit(solution)/shard_map/ppermute | solution.py:301
  46.9 0.3 collective-permute-start.14
  47.3 2.4 %collective-permute-start.15 = (f32[96,128]{1,0:T(8,128)S(1)}, f32[96,128]{1,0:T(8,128)S(1)}, u32[]{:S(2)}, u32[]{:S(2)}) collective-permute-start(f32[96,128]{1,0:T(8,128)S(1)} %get-tuple-element.49), channel_id=1, source_target_pairs={{0,24},{8,0},{16,8},{24,16},{1,25},{9,1},{17,9},{25,17},{2,26},{10... | collective-permute-start | bytes 147464 | tf_op jit(solution)/shard_map/ppermute | solution.py:301
  49.6 0.0 collective-permute-done.13
  49.6 1.5 %collective-permute-done.14 = f32[96,128]{1,0:T(8,128)S(1)} collective-permute-done((f32[96,128]{1,0:T(8,128)S(1)}, f32[96,128]{1,0:T(8,128)S(1)}, u32[]{:S(2)}, u32[]{:S(2)}) %collective-permute-start.14) | collective-permute-done | bytes 49184 | tf_op jit(solution)/shard_map/ppermute | solution.py:301
  51.1 7.0 %collective-permute-start.18 = (f32[96,128]{1,0:T(8,128)S(1)}, f32[96,128]{1,0:T(8,128)S(1)}, u32[]{:S(2)}, u32[]{:S(2)}) collective-permute-start(f32[96,128]{1,0:T(8,128)S(1)} %add_add_fusion.1), channel_id=1, source_target_pairs={{0,128},{32,160},{64,192},{96,224},{128,0},{160,32},{192,64},{224,... | collective-permute-start | bytes 147464 | tf_op jit(solution)/shard_map/ppermute | solution.py:302
  58.1 1.2 %collective-permute-start.17 = (f32[96,128]{1,0:T(8,128)S(1)}, f32[96,128]{1,0:T(8,128)S(1)}, u32[]{:S(2)}, u32[]{:S(2)}) collective-permute-start(f32[96,128]{1,0:T(8,128)S(1)} %add_add_fusion.1), channel_id=1, source_target_pairs={{0,64},{32,96},{64,128},{96,160},{128,192},{160,224},{192,0},{224,... | collective-permute-start | bytes 147464 | tf_op jit(solution)/shard_map/ppermute | solution.py:302
  59.3 2.4 %collective-permute-start.16 = (f32[96,128]{1,0:T(8,128)S(1)}, f32[96,128]{1,0:T(8,128)S(1)}, u32[]{:S(2)}, u32[]{:S(2)}) collective-permute-start(f32[96,128]{1,0:T(8,128)S(1)} %add_add_fusion.1), channel_id=1, source_target_pairs={{0,192},{32,224},{64,0},{96,32},{128,64},{160,96},{192,128},{224,1... | collective-permute-start | bytes 147464 | tf_op jit(solution)/shard_map/ppermute | solution.py:302
  61.7 1.5 %collective-permute-done.17 = f32[96,128]{1,0:T(8,128)S(1)} collective-permute-done((f32[96,128]{1,0:T(8,128)S(1)}, f32[96,128]{1,0:T(8,128)S(1)}, u32[]{:S(2)}, u32[]{:S(2)}) %collective-permute-start.17) | collective-permute-done | bytes 49184 | tf_op jit(solution)/shard_map/ppermute | solution.py:302
  63.2 0.8 collective-permute-done.16
  64.0 0.6 collective-permute-start.19
  64.7 2.5 %collective-permute-done.19.other_ref = f32[96,128]{1,0:T(8,128)S(1)} collective-permute-done((f32[96,128]{1,0:T(8,128)S(1)}, f32[96,128]{1,0:T(8,128)S(1)}, u32[]{:S(2)}, u32[]{:S(2)}) %collective-permute-start.19) | collective-permute-done | bytes 49184 | tf_op jit(solution)/shard_map/ppermute | solution.py:303
  67.2 2.5 %interval_rows.1 = (f32[16,128]{1,0:T(8,128)S(1)}, f32[64,64]{1,0:T(8,128)S(1)}) custom-call(s32[3]{0:T(128)S(1)} %pad_add_fusion.place, f32[96,128]{1,0:T(8,128)S(1)} %add_add_fusion.total_ref, f32[96,128]{1,0:T(8,128)S(1)} %collective-permute-done.19.other_ref, f32[64,64]{1,0:T(8,128)S(1)} %get-tuple-element.38.gram_day_ref, ...), custom_call_target="tpu_custom_call" | custom-call | flops 1048576 | bytes 65536 | tf_op jit(solution)/shard_map/interval_rows/pallas_call | solution.py:227
  69.7 3.7 %collective-permute-start.20 = (f32[16,128]{1,0:T(8,128)S(1)}, f32[16,128]{1,0:T(8,128)S(1)}, u32[]{:S(2)}, u32[]{:S(2)}) collective-permute-start(f32[16,128]{1,0:T(8,128)S(1)} %get-tuple-element.51), channel_id=1, source_target_pairs={{0,1},{1,0},{2,3},{3,2},{4,5},{5,4},{6,7},{7,6},{8,9},{9,8},{10,11... | collective-permute-start | bytes 24584 | tf_op jit(solution)/shard_map/ppermute | solution.py:249
  73.4 0.8 collective-permute-done.20
  74.3 10.8 %all_to_all.5.recv_ref = f32[16,16,128]{2,1,0:T(8,128)S(1)} all-to-all(f32[16,16,128]{2,1,0:T(8,128)S(1)} %broadcast_in_dim.2), channel_id=1, replica_groups=mesh['z'=8,'x'=4,'y'=4,'core'=2] {'x','y'}, dimensions={0} | all-to-all | bytes 262144 | tf_op jit(solution)/shard_map/all_to_all | solution.py:312
  85.1 3.0 %day_rows.1 = (f32[32,64]{1,0:T(8,128)}, f32[16,64]{1,0:T(8,128)}) custom-call(s32[3]{0:T(128)S(1)} %pad_add_fusion.place, f32[16,16,128]{2,1,0:T(8,128)S(1)} %all_to_all.5.recv_ref, f32[64,64]{1,0:T(8,128)S(1)} %get-tuple-element.52.gram_ref), custom_call_target="tpu_custom_call" | custom-call | flops 1048576 | bytes 65536 | tf_op jit(solution)/shard_map/day_rows/pallas_call | solution.py:227
  (10 shorter events, 0.1 us)
Async XLA Ops:
  4.5 6.4 %collective-permute-start = (f32[264,1024]{1,0:T(8,128)S(1)}, f32[264,1024]{1,0:T(8,128)S(1)}, u32[]{:S(2)}, u32[]{:S(2)}) collective-permute-start(f32[264,1024]{1,0:T(8,128)S(1)} %get-tuple-element.31.sent_ref), channel_id=1, source_target_pairs={{0,1},{1,0},{2,3},{3,2},{4,5},{5,4},{6,7},{7,6},{8,9},{9,8},{10,11... | collective-permute-start | bytes 3244040 | tf_op jit(solution)/shard_map/ppermute | solution.py:249
  11.0 13.7 %collective-permute-start.1 = (f32[72,1024]{1,0:T(8,128)S(1)}, f32[72,1024]{1,0:T(8,128)S(1)}, u32[]{:S(2)}, u32[]{:S(2)}) collective-permute-start(f32[72,1024]{1,0:T(8,128)S(1)} %get-tuple-element.33), channel_id=1, source_target_pairs={{0,4},{2,6},{4,0},{6,2},{1,5},{3,7},{5,1},{7,3},{8,12},{10,14},{12... | collective-permute-start | bytes 884744 | tf_op jit(solution)/shard_map/ppermute | solution.py:252
  12.3 12.4 %collective-permute-start.2 = (f32[72,512]{1,0:T(8,128)S(1)}, f32[72,512]{1,0:T(8,128)S(1)}, u32[]{:S(2)}, u32[]{:S(2)}) collective-permute-start(f32[72,512]{1,0:T(8,128)S(1)} %get-tuple-element.34), channel_id=1, source_target_pairs={{0,2},{2,4},{4,6},{6,0},{1,3},{3,5},{5,7},{7,1},{8,10},{10,12},{12... | collective-permute-start | bytes 442376 | tf_op jit(solution)/shard_map/ppermute | solution.py:252
  12.7 12.0 %collective-permute-start.3 = (f32[72,512]{1,0:T(8,128)S(1)}, f32[72,512]{1,0:T(8,128)S(1)}, u32[]{:S(2)}, u32[]{:S(2)}) collective-permute-start(f32[72,512]{1,0:T(8,128)S(1)} %get-tuple-element.35), channel_id=1, source_target_pairs={{0,6},{2,0},{4,2},{6,4},{1,7},{3,1},{5,3},{7,5},{8,14},{10,8},{12,... | collective-permute-start | bytes 442376 | tf_op jit(solution)/shard_map/ppermute | solution.py:252
  15.0 12.5 %collective-permute-start.4 = (f32[64,512]{1,0:T(8,128)S(1)}, f32[64,512]{1,0:T(8,128)S(1)}, u32[]{:S(2)}, u32[]{:S(2)}) collective-permute-start(f32[64,512]{1,0:T(8,128)S(1)} %get-tuple-element.36), channel_id=1, source_target_pairs={{0,2},{2,4},{4,6},{6,0},{1,3},{3,5},{5,7},{7,1},{8,10},{10,12},{12... | collective-permute-start | bytes 393224 | tf_op jit(solution)/shard_map/ppermute | solution.py:252
  15.0 12.5 %collective-permute-start.5 = (f32[64,512]{1,0:T(8,128)S(1)}, f32[64,512]{1,0:T(8,128)S(1)}, u32[]{:S(2)}, u32[]{:S(2)}) collective-permute-start(f32[64,512]{1,0:T(8,128)S(1)} %get-tuple-element.37), channel_id=1, source_target_pairs={{0,6},{2,0},{4,2},{6,4},{1,7},{3,1},{5,3},{7,5},{8,14},{10,8},{12,... | collective-permute-start | bytes 393224 | tf_op jit(solution)/shard_map/ppermute | solution.py:252
  28.8 3.1 %collective-permute-start.7 = (bf16[64,1152]{1,0:T(8,128)(2,1)S(1)}, bf16[64,1152]{1,0:T(8,128)(2,1)S(1)}, u32[]{:S(2)}, u32[]{:S(2)}) collective-permute-start(bf16[64,1152]{1,0:T(8,128)(2,1)S(1)} %get-tuple-element.40.low.refs_6_), channel_id=1, source_target_pairs={{0,1},{1,0},{2,3},{3,2},{4,5},{5,4},{6,7},{7,6},{8,9},{9,8},{10,11... | collective-permute-start | bytes 442376 | tf_op jit(solution)/shard_map/ppermute | solution.py:249
  29.3 5.4 %collective-permute-start.11 = (bf16[64,1152]{1,0:T(8,128)(2,1)S(1)}, bf16[64,1152]{1,0:T(8,128)(2,1)S(1)}, u32[]{:S(2)}, u32[]{:S(2)}) collective-permute-start(bf16[64,1152]{1,0:T(8,128)(2,1)S(1)} %get-tuple-element.40.low.refs_6_), channel_id=1, source_target_pairs={{0,6},{2,0},{4,2},{6,4},{1,7},{3,1},{5,3},{7,5},{8,14},{10,8},{12,... | collective-permute-start | bytes 442376 | tf_op jit(solution)/shard_map/ppermute | solution.py:252
  30.3 9.5 %collective-permute-start.9 = (bf16[64,1152]{1,0:T(8,128)(2,1)S(1)}, bf16[64,1152]{1,0:T(8,128)(2,1)S(1)}, u32[]{:S(2)}, u32[]{:S(2)}) collective-permute-start(bf16[64,1152]{1,0:T(8,128)(2,1)S(1)} %get-tuple-element.40.low.refs_6_), channel_id=1, source_target_pairs={{0,2},{2,4},{4,6},{6,0},{1,3},{3,5},{5,7},{7,1},{8,10},{10,12},{12... | collective-permute-start | bytes 442376 | tf_op jit(solution)/shard_map/ppermute | solution.py:252
  30.7 9.1 %collective-permute-start.6 = (bf16[64,1152]{1,0:T(8,128)(2,1)S(1)}, bf16[64,1152]{1,0:T(8,128)(2,1)S(1)}, u32[]{:S(2)}, u32[]{:S(2)}) collective-permute-start(bf16[64,1152]{1,0:T(8,128)(2,1)S(1)} %get-tuple-element.40.low.refs_6_), channel_id=1, source_target_pairs={{0,4},{2,6},{4,0},{6,2},{1,5},{3,7},{5,1},{7,3},{8,12},{10,14},{12... | collective-permute-start | bytes 442376 | tf_op jit(solution)/shard_map/ppermute | solution.py:252
  39.8 2.6 %collective-permute-start.8 = (bf16[64,1152]{1,0:T(8,128)(2,1)S(1)}, bf16[64,1152]{1,0:T(8,128)(2,1)S(1)}, u32[]{:S(2)}, u32[]{:S(2)}) collective-permute-start(bf16[64,1152]{1,0:T(8,128)(2,1)S(1)} %collective-permute-done.6.low0.refs_3_), channel_id=1, source_target_pairs={{0,1},{1,0},{2,3},{3,2},{4,5},{5,4},{6,7},{7,6},{8,9},{9,8},{10,11... | collective-permute-start | bytes 442376 | tf_op jit(solution)/shard_map/ppermute | solution.py:249
  40.9 1.5 %collective-permute-start.10 = (bf16[64,1152]{1,0:T(8,128)(2,1)S(1)}, bf16[64,1152]{1,0:T(8,128)(2,1)S(1)}, u32[]{:S(2)}, u32[]{:S(2)}) collective-permute-start(bf16[64,1152]{1,0:T(8,128)(2,1)S(1)} %collective-permute-done.9.low1.refs_4_), channel_id=1, source_target_pairs={{0,1},{1,0},{2,3},{3,2},{4,5},{5,4},{6,7},{7,6},{8,9},{9,8},{10,11... | collective-permute-start | bytes 442376 | tf_op jit(solution)/shard_map/ppermute | solution.py:249
  40.9 1.6 %collective-permute-start.12 = (bf16[64,1152]{1,0:T(8,128)(2,1)S(1)}, bf16[64,1152]{1,0:T(8,128)(2,1)S(1)}, u32[]{:S(2)}, u32[]{:S(2)}) collective-permute-start(bf16[64,1152]{1,0:T(8,128)(2,1)S(1)} %collective-permute-done.11.low2.refs_5_), channel_id=1, source_target_pairs={{0,1},{1,0},{2,3},{3,2},{4,5},{5,4},{6,7},{7,6},{8,9},{9,8},{10,11... | collective-permute-start | bytes 442376 | tf_op jit(solution)/shard_map/ppermute | solution.py:249
  44.1 5.5 %collective-permute-start.13 = (f32[96,128]{1,0:T(8,128)S(1)}, f32[96,128]{1,0:T(8,128)S(1)}, u32[]{:S(2)}, u32[]{:S(2)}) collective-permute-start(f32[96,128]{1,0:T(8,128)S(1)} %get-tuple-element.47), channel_id=1, source_target_pairs={{0,16},{8,24},{16,0},{24,8},{1,17},{9,25},{17,1},{25,9},{2,18},{10... | collective-permute-start | bytes 147464 | tf_op jit(solution)/shard_map/ppermute | solution.py:301
  46.9 4.2 %collective-permute-start.14 = (f32[96,128]{1,0:T(8,128)S(1)}, f32[96,128]{1,0:T(8,128)S(1)}, u32[]{:S(2)}, u32[]{:S(2)}) collective-permute-start(f32[96,128]{1,0:T(8,128)S(1)} %get-tuple-element.48), channel_id=1, source_target_pairs={{0,8},{8,16},{16,24},{24,0},{1,9},{9,17},{17,25},{25,1},{2,10},{10... | collective-permute-start | bytes 147464 | tf_op jit(solution)/shard_map/ppermute | solution.py:301
  47.3 3.8 %collective-permute-start.15 = (f32[96,128]{1,0:T(8,128)S(1)}, f32[96,128]{1,0:T(8,128)S(1)}, u32[]{:S(2)}, u32[]{:S(2)}) collective-permute-start(f32[96,128]{1,0:T(8,128)S(1)} %get-tuple-element.49), channel_id=1, source_target_pairs={{0,24},{8,0},{16,8},{24,16},{1,25},{9,1},{17,9},{25,17},{2,26},{10... | collective-permute-start | bytes 147464 | tf_op jit(solution)/shard_map/ppermute | solution.py:301
  51.1 10.6 %collective-permute-start.18 = (f32[96,128]{1,0:T(8,128)S(1)}, f32[96,128]{1,0:T(8,128)S(1)}, u32[]{:S(2)}, u32[]{:S(2)}) collective-permute-start(f32[96,128]{1,0:T(8,128)S(1)} %add_add_fusion.1), channel_id=1, source_target_pairs={{0,128},{32,160},{64,192},{96,224},{128,0},{160,32},{192,64},{224,... | collective-permute-start | bytes 147464 | tf_op jit(solution)/shard_map/ppermute | solution.py:302
  58.1 5.1 %collective-permute-start.17 = (f32[96,128]{1,0:T(8,128)S(1)}, f32[96,128]{1,0:T(8,128)S(1)}, u32[]{:S(2)}, u32[]{:S(2)}) collective-permute-start(f32[96,128]{1,0:T(8,128)S(1)} %add_add_fusion.1), channel_id=1, source_target_pairs={{0,64},{32,96},{64,128},{96,160},{128,192},{160,224},{192,0},{224,... | collective-permute-start | bytes 147464 | tf_op jit(solution)/shard_map/ppermute | solution.py:302
  59.3 4.7 %collective-permute-start.16 = (f32[96,128]{1,0:T(8,128)S(1)}, f32[96,128]{1,0:T(8,128)S(1)}, u32[]{:S(2)}, u32[]{:S(2)}) collective-permute-start(f32[96,128]{1,0:T(8,128)S(1)} %add_add_fusion.1), channel_id=1, source_target_pairs={{0,192},{32,224},{64,0},{96,32},{128,64},{160,96},{192,128},{224,1... | collective-permute-start | bytes 147464 | tf_op jit(solution)/shard_map/ppermute | solution.py:302
  64.0 3.2 %collective-permute-start.19 = (f32[96,128]{1,0:T(8,128)S(1)}, f32[96,128]{1,0:T(8,128)S(1)}, u32[]{:S(2)}, u32[]{:S(2)}) collective-permute-start(f32[96,128]{1,0:T(8,128)S(1)} %add_add_fusion.total_ref), channel_id=1, source_target_pairs={{0,32},{32,0},{64,96},{96,64},{128,160},{160,128},{192,224},{224,1... | collective-permute-start | bytes 147464 | tf_op jit(solution)/shard_map/ppermute | solution.py:303
  69.7 4.5 %collective-permute-start.20 = (f32[16,128]{1,0:T(8,128)S(1)}, f32[16,128]{1,0:T(8,128)S(1)}, u32[]{:S(2)}, u32[]{:S(2)}) collective-permute-start(f32[16,128]{1,0:T(8,128)S(1)} %get-tuple-element.51), channel_id=1, source_target_pairs={{0,1},{1,0},{2,3},{3,2},{4,5},{5,4},{6,7},{7,6},{8,9},{9,8},{10,11... | collective-permute-start | bytes 24584 | tf_op jit(solution)/shard_map/ppermute | solution.py:249

commit v4 on v3

--- a/solution.py
+++ b/solution.py
@@ -9,13 +9,14 @@
 
 RANK = 64
 HALF = 512
+ORDER = (3, 1, 2)
 HIGH = lax.Precision.HIGHEST
 F32 = jnp.float32
 BF16 = jnp.bfloat16
 
 
-def shifts(n, d):
-    return [(i, (i + d) % n) for i in range(n)]
+def partners(n, d):
+    return [(i, i ^ d) for i in range(n)]
 
 
 def iota(shape, dim):
@@ -67,14 +68,14 @@
 def load_blocks(place, slab_ref, held_ref, sems, core):
     copies = []
     for d in range(4):
-        at = pl.multiple_of((2 * lax.rem(place[1] + d, 4) + core) * 1024, 1024)
+        at = pl.multiple_of((2 * (place[1] ^ d) + core) * 1024, 1024)
         copies.append(pltpu.make_async_copy(slab_ref.at[:, pl.ds(at, 1024)], held_ref.at[d], sems.at[d]))
         copies[-1].start()
     return copies
 
 
 def send_kernel(
-    place, slab_ref, interval_ref, day_ref, sums_ref, held_ref, khatri_ref, gram_day_ref, day_twice_ref, sems, *own
+    place, slab_ref, interval_ref, day_ref, sums_ref, held_ref, khatri_ref, day_twice_ref, sems, *own
 ):
     factor, day, small_sems = own
     small = [
@@ -91,7 +92,6 @@
     khatri_ref[...] = khatri
     sums_ref[4 * RANK :, : 8 * RANK] = to_lanes(dot(factor[...], factor[...], ((0,), (0,))))
     sums_ref[4 * RANK :, 8 * RANK :] = jnp.zeros((8, 1024 - 8 * RANK), F32)
-    gram_day_ref[...] = dot(day[...], day[...], ((0,), (0,)))
     day_twice_ref[...] = jnp.concatenate([day[...], day[...]], axis=1)
     for d in range(4):
         copies[d].wait()
@@ -129,9 +129,12 @@
         second[...] = total(d, slice(HALF, 1024))
 
 
-def inverse_kernel(own, two, one, three, gram_day_ref, inverse_ref):
+def inverse_kernel(own, two, one, three, day_ref, inverse_ref, gram_day_ref):
+    day = day_ref[:, :RANK]
+    gram_day = dot(day, day, ((0,), (0,)))
+    gram_day_ref[...] = gram_day
     gram = (own[RANK:, : 8 * RANK] + two[RANK:, : 8 * RANK]) + (one[RANK:] + three[RANK:])
-    inverse_ref[...] = inverse_of(from_lanes(gram) * gram_day_ref[...])
+    inverse_ref[...] = inverse_of(from_lanes(gram) * gram_day)
 
 
 def link_kernel(own, two, one_a, three_a, one_b, three_b, inverse_ref, link_ref, low_ref):
@@ -159,19 +162,19 @@
 
 
 def second_partial_kernel(low0, low1, low2, keep_ref, before, acc):
-    acc[...] = before[...] + times_blocks((low0, low1, low2), keep_ref, (2, 3, 1))
+    acc[...] = before[...] + times_blocks((low0, low1, low2), keep_ref, ORDER)
 
 
 def last_partial_kernel(place, *refs):
     lows, (held, before), outs, acc = refs[:8], refs[8:10], refs[10:14], refs[14]
-    acc[...] = before[...] + times_blocks(lows[:3], held, (2, 3, 1))
+    acc[...] = before[...] + times_blocks(lows[:3], held, ORDER)
     halves = [low[:, 1024 :].astype(F32) for low in lows]
     total = halves[0]
     for half in halves[1:]:
         total = total + half
     packed = pack(total[:, :RANK] + total[:, RANK:])
     for d, out in enumerate(outs):
-        at = pl.multiple_of(lax.rem(place[2] + d, 4) * 128, 128)
+        at = pl.multiple_of((place[2] ^ d) * 128, 128)
         out[:RANK] = jnp.concatenate([acc[pl.ds(at, RANK)], acc[pl.ds(at + RANK, RANK)]], axis=1)
         out[RANK:] = packed
 
@@ -246,14 +249,14 @@
     smem = {0: pltpu.SMEM}
 
     def other_core(a):
-        return lax.ppermute(a, "core", shifts(2, 1))
+        return lax.ppermute(a, "core", partners(2, 1))
 
     def along_y(a, d):
-        return lax.ppermute(a, "y", shifts(4, d))
-
-    send, held_send, khatri, gram_day, day_twice = call(
+        return lax.ppermute(a, "y", partners(4, d))
+
+    send, held_send, khatri, day_twice = call(
         send_kernel,
-        (shape((264, 1024)), held, shape((RANK, 512), BF16), shape((RANK, RANK)), shape((16, 2 * RANK))),
+        (shape((264, 1024)), held, shape((RANK, 512), BF16), shape((16, 2 * RANK))),
         (place, flat, interval_factor, day_factor),
         "sums_to_send",
         {0: pltpu.SMEM, 1: pl.ANY, 2: pl.ANY, 3: pl.ANY},
@@ -280,14 +283,16 @@
         "add_cores",
     )
     parts = [sums[0]] + [along_y(one, d) for one, d in zip(sums[1:], (2, 1, 3, 1, 3))]
-    inverse = call(inverse_kernel, shape((RANK, RANK)), (*parts[:4], gram_day), "link_inverse")
+    inverse, gram_day = call(
+        inverse_kernel, (shape((RANK, RANK)),) * 2, (*parts[:4], day_twice), "link_inverse"
+    )
     link, low = call(
         link_kernel, (shape((RANK, 1024)), shape((RANK, 1152), BF16)), (*parts, inverse), "link_rows"
     )
-    lows = [along_y(low, d) for d in (2, 1, 3)]
+    lows = [along_y(low, d) for d in ORDER]
     low_other = other_core(low)
     acc = call(first_partial_kernel, shape((512, RANK)), (low, low_other, held_keep, held_send), "partial_own")
-    lows = [lax.optimization_barrier((one, acc))[0] for one in lows]
+    lows[0] = lax.optimization_barrier((lows[0], acc))[0]
     others = [other_core(one) for one in lows]
     acc = call(second_partial_kernel, shape((512, RANK)), (*lows, held_keep, acc), "partial_own_core")
     outgoing = call(
@@ -298,9 +303,9 @@
         smem,
         [pltpu.VMEM((512, RANK), F32)],
     )
-    over_x = sum([lax.ppermute(outgoing[d], "x", shifts(4, d)) for d in (2, 1, 3)], outgoing[0])
-    over_z = sum([lax.ppermute(over_x, "z", shifts(8, d)) for d in (6, 2, 4)], over_x)
-    z_other = lax.ppermute(over_z, "z", [(i, i ^ 1) for i in range(8)])
+    over_x = sum([lax.ppermute(outgoing[d], "x", partners(4, d)) for d in (1, 2, 3)], outgoing[0])
+    over_z = sum([lax.ppermute(over_x, "z", partners(8, d)) for d in (2, 6, 4)], over_x)
+    z_other = lax.ppermute(over_z, "z", partners(8, 1))
     found, gram_link = call(
         interval_kernel,
         (shape((16, 128)), shape((RANK, RANK))),

time: 88.4 us -> 86.9 us (0.983)
  starting transfers between devices: 35.1 us -> 30.8 us
  waiting for transfers between devices: 22.7 us -> 25.8 us
    ppermute x21, starting transfers between devices: 35.1 us -> 30.8 us  [the longest x6 9.8 us: other_core(): return lax.ppermute(a, 'core', partners(2, 1))]
    ppermute x21, waiting for transfers between devices: 22.7 us -> 25.8 us  [the longest x8 15.8 us: along_y(): return lax.ppermute(a, 'y', partners(4, d))]
  transfers between devices with their start and end apart: 21 -> 21, of which waited for: 10 -> 11; matrix products, arithmetic and copies ran while one was open for 0% -> 0% of each run, Pallas kernels for 7% -> 7%
where the time goes in v4:
time: 86.9 us; the launch traced here: 86.7 us
  starting transfers between devices  30.8 us (35%)
  waiting for transfers between devices  25.8 us (30%)
  Pallas kernels  18.8 us (22%)
  blocking collectives  10.5 us (12%)
    pallas_call x10, Pallas kernels, call(): pl.pallas_call(kernel, out_shape=out_shape, in_specs=[pl.BlockSpec(memory...  18.8 us
    ppermute x8, waiting for transfers between devices, along_y(): return lax.ppermute(a, 'y', partners(4, d))  15.8 us
    all_to_all x1, blocking collectives, body(): lax.all_to_all(jnp.broadcast_to(found[None], (16, 16, 128)), ('x', 'y'),...  10.5 us
    ppermute x6, starting transfers between devices, other_core(): return lax.ppermute(a, 'core', partners(2, 1))  9.8 us
    ppermute x3, starting transfers between devices, body(): lax.ppermute(over_x, 'z', partners(8, d))  8.19 us
    ppermute x8, starting transfers between devices, along_y(): return lax.ppermute(a, 'y', partners(4, d))  8.08 us
    ppermute x3, waiting for transfers between devices, body(): lax.ppermute(over_x, 'z', partners(8, d))  3.94 us
    ppermute x3, starting transfers between devices, body(): lax.ppermute(outgoing[d], 'x', partners(4, d))  3.94 us
  transfers between devices with their start and end apart: 21, of which 11 were waited for; matrix products, arithmetic and copies ran while one was open for 0% of the time, Pallas kernels for 7%

profile of v4, /device:TPU:1, one launch (start us, length us, event | category | flops | bytes accessed | tf_op | source)
XLA Modules:
  0.0 86.7 jit_solution(1660163612798380244)
XLA Ops:
  0.6 0.1 pad_add_fusion.place
  0.7 3.8 %sums_to_send.1 = (f32[264,1024]{1,0:T(8,128)S(1)}, bf16[4,512,1024]{2,1,0:T(8,128)(2,1)S(1)}, bf16[64,512]{1,0:T(8,128)(2,1)S(1)}, f32[16,128]{1,0:T(8,128)S(1)}) custom-call(s32[3]{0:T(128)S(1)} %pad_add_fusion.place, bf16[512,8192]{1,0:T(8,128)(2,1)} %bitcast.5, f32[32,64]{1,0:T(8,128)} %interval_ref.1, f32[16,64]{1,0:T(8,128)} %day_ref.1), custom_call_target="tpu_custom_call" | custom-call | flops 1048576 | bytes 65536 | tf_op jit(solution)/shard_map/sums_to_send/pallas_call | solution.py:230
  4.5 3.3 %collective-permute-start = (f32[264,1024]{1,0:T(8,128)S(1)}, f32[264,1024]{1,0:T(8,128)S(1)}, u32[]{:S(2)}, u32[]{:S(2)}) collective-permute-start(f32[264,1024]{1,0:T(8,128)S(1)} %get-tuple-element.30.sent_ref), channel_id=1, source_target_pairs={{0,1},{1,0},{2,3},{3,2},{4,5},{5,4},{6,7},{7,6},{8,9},{9,8},{10,11... | collective-permute-start | bytes 3244040 | tf_op jit(solution)/shard_map/ppermute | solution.py:252
  7.9 3.1 %sums_to_keep.1 = (f32[4,64,1024]{2,1,0:T(8,128)S(1)}, bf16[4,512,1024]{2,1,0:T(8,128)(2,1)S(1)}) custom-call(s32[3]{0:T(128)S(1)} %pad_add_fusion.place, bf16[512,8192]{1,0:T(8,128)(2,1)} %bitcast.6, bf16[64,512]{1,0:T(8,128)(2,1)S(1)} %get-tuple-element.28.khatri_ref), custom_call_target="tpu_custom_call" | custom-call | flops 1048576 | bytes 65536 | tf_op jit(solution)/shard_map/sums_to_keep/pallas_call | solution.py:230
  10.9 0.0 collective-permute-done.got_ref
  10.9 0.1 add_cores.1
  11.1 1.3 %collective-permute-start.1 = (f32[72,1024]{1,0:T(8,128)S(1)}, f32[72,1024]{1,0:T(8,128)S(1)}, u32[]{:S(2)}, u32[]{:S(2)}) collective-permute-start(f32[72,1024]{1,0:T(8,128)S(1)} %get-tuple-element.32), channel_id=1, source_target_pairs={{0,4},{2,6},{4,0},{6,2},{1,5},{3,7},{5,1},{7,3},{8,12},{10,14},{12... | collective-permute-start | bytes 884744 | tf_op jit(solution)/shard_map/ppermute | solution.py:255
  12.4 0.4 collective-permute-start.2
  12.7 1.7 %collective-permute-start.3 = (f32[72,512]{1,0:T(8,128)S(1)}, f32[72,512]{1,0:T(8,128)S(1)}, u32[]{:S(2)}, u32[]{:S(2)}) collective-permute-start(f32[72,512]{1,0:T(8,128)S(1)} %get-tuple-element.34), channel_id=1, source_target_pairs={{0,6},{2,4},{4,2},{6,0},{1,7},{3,5},{5,3},{7,1},{8,14},{10,12},{12... | collective-permute-start | bytes 442376 | tf_op jit(solution)/shard_map/ppermute | solution.py:255
  14.4 1.5 %collective-permute-start.5 = (f32[64,512]{1,0:T(8,128)S(1)}, f32[64,512]{1,0:T(8,128)S(1)}, u32[]{:S(2)}, u32[]{:S(2)}) collective-permute-start(f32[64,512]{1,0:T(8,128)S(1)} %get-tuple-element.36), channel_id=1, source_target_pairs={{0,6},{2,4},{4,2},{6,0},{1,7},{3,5},{5,3},{7,1},{8,14},{10,12},{12... | collective-permute-start | bytes 393224 | tf_op jit(solution)/shard_map/ppermute | solution.py:255
  15.9 7.2 %collective-permute-done.2.one.one_a = f32[72,512]{1,0:T(8,128)S(1)} collective-permute-done((f32[72,512]{1,0:T(8,128)S(1)}, f32[72,512]{1,0:T(8,128)S(1)}, u32[]{:S(2)}, u32[]{:S(2)}) %collective-permute-start.2) | collective-permute-done | bytes 147488 | tf_op jit(solution)/shard_map/ppermute | solution.py:255
  23.1 1.7 %collective-permute-done.3.three.three_a = f32[72,512]{1,0:T(8,128)S(1)} collective-permute-done((f32[72,512]{1,0:T(8,128)S(1)}, f32[72,512]{1,0:T(8,128)S(1)}, u32[]{:S(2)}, u32[]{:S(2)}) %collective-permute-start.3) | collective-permute-done | bytes 147488 | tf_op jit(solution)/shard_map/ppermute | solution.py:255
  24.8 1.8 %link_inverse.1 = (f32[64,64]{1,0:T(8,128)S(1)}, f32[64,64]{1,0:T(8,128)S(1)}) custom-call(f32[72,1024]{1,0:T(8,128)S(1)} %get-tuple-element.31.own, f32[72,1024]{1,0:T(8,128)S(1)} %collective-permute-done.1.two, f32[72,512]{1,0:T(8,128)S(1)} %collective-permute-done.2.one.one_a, f32[72,512]{1,0:T(8,128)S(1)} %collective-permute-done.3.three.three_a, ...), custom_call_target="tpu_custom_call" | custom-call | flops 1048576 | bytes 65536 | tf_op jit(solution)/shard_map/link_inverse/pallas_call | solution.py:230
  26.5 1.0 %collective-permute-done.5.three_b = f32[64,512]{1,0:T(8,128)S(1)} collective-permute-done((f32[64,512]{1,0:T(8,128)S(1)}, f32[64,512]{1,0:T(8,128)S(1)}, u32[]{:S(2)}, u32[]{:S(2)}) %collective-permute-start.5) | collective-permute-done | bytes 131104 | tf_op jit(solution)/shard_map/ppermute | solution.py:255
  27.6 1.2 %link_rows.1 = (f32[64,1024]{1,0:T(8,128)}, bf16[64,1152]{1,0:T(8,128)(2,1)S(1)}) custom-call(f32[72,1024]{1,0:T(8,128)S(1)} %get-tuple-element.31.own, f32[72,1024]{1,0:T(8,128)S(1)} %collective-permute-done.1.two, f32[72,512]{1,0:T(8,128)S(1)} %collective-permute-done.2.one.one_a, f32[72,512]{1,0:T(8,128)S(1)} %collective-permute-done.3.three.three_a, ...), custom_call_target="tpu_custom_call" | custom-call | flops 1048576 | bytes 65536 | tf_op jit(solution)/shard_map/link_rows/pallas_call | solution.py:230
  28.8 0.5 collective-permute-start.7
  29.3 1.0 %collective-permute-start.6 = (bf16[64,1152]{1,0:T(8,128)(2,1)S(1)}, bf16[64,1152]{1,0:T(8,128)(2,1)S(1)}, u32[]{:S(2)}, u32[]{:S(2)}) collective-permute-start(bf16[64,1152]{1,0:T(8,128)(2,1)S(1)} %get-tuple-element.40.low.refs_6_), channel_id=1, source_target_pairs={{0,6},{2,4},{4,2},{6,0},{1,7},{3,5},{5,3},{7,1},{8,14},{10,12},{12... | collective-permute-start | bytes 442376 | tf_op jit(solution)/shard_map/ppermute | solution.py:255
  30.3 0.5 collective-permute-start.11
  30.8 1.7 %collective-permute-start.9 = (bf16[64,1152]{1,0:T(8,128)(2,1)S(1)}, bf16[64,1152]{1,0:T(8,128)(2,1)S(1)}, u32[]{:S(2)}, u32[]{:S(2)}) collective-permute-start(bf16[64,1152]{1,0:T(8,128)(2,1)S(1)} %get-tuple-element.40.low.refs_6_), channel_id=1, source_target_pairs={{0,2},{2,0},{4,6},{6,4},{1,3},{3,1},{5,7},{7,5},{8,10},{10,8},{12,... | collective-permute-start | bytes 442376 | tf_op jit(solution)/shard_map/ppermute | solution.py:255
  32.5 0.0 collective-permute-done.7.low_other.refs_7_
  32.5 0.7 partial_own.1.before
  33.2 5.9 %collective-permute-done.6.low0.refs_3_ = bf16[64,1152]{1,0:T(8,128)(2,1)S(1)} collective-permute-done((bf16[64,1152]{1,0:T(8,128)(2,1)S(1)}, bf16[64,1152]{1,0:T(8,128)(2,1)S(1)}, u32[]{:S(2)}, u32[]{:S(2)}) %collective-permute-start.6) | collective-permute-done | bytes 147488 | tf_op jit(solution)/shard_map/ppermute | solution.py:255
  39.1 0.0 collective-permute-done.11.low2.refs_5_
  39.1 0.8 collective-permute-start.12
  39.9 0.0 collective-permute-done.9.low1.refs_4_
  39.9 0.6 collective-permute-start.10
  40.5 0.0 collective-permute-start.8
  40.6 1.0 %partial_own_core.1.refs_9_ = f32[512,64]{1,0:T(8,128)S(1)} custom-call(bf16[64,1152]{1,0:T(8,128)(2,1)S(1)} %collective-permute-done.6.low0.refs_3_, bf16[64,1152]{1,0:T(8,128)(2,1)S(1)} %collective-permute-done.9.low1.refs_4_, bf16[64,1152]{1,0:T(8,128)(2,1)S(1)} %collective-permute-done.11.low2.refs_5_, ...), custom_call_target="tpu_custom_call" | custom-call | flops 1048576 | bytes 65536 | tf_op jit(solution)/shard_map/partial_own_core/pallas_call | solution.py:230
  41.5 0.0 collective-permute-done.12.refs_2_
  41.5 0.0 collective-permute-done.10.refs_1_
  41.6 0.4 collective-permute-done.8.refs_0_
  41.9 1.6 %partial_other_core.1 = (f32[96,128]{1,0:T(8,128)S(1)}, f32[96,128]{1,0:T(8,128)S(1)}, f32[96,128]{1,0:T(8,128)S(1)}, f32[96,128]{1,0:T(8,128)S(1)}) custom-call(s32[3]{0:T(128)S(1)} %pad_add_fusion.place, bf16[64,1152]{1,0:T(8,128)(2,1)S(1)} %collective-permute-done.8.refs_0_, bf16[64,1152]{1,0:T(8,128)(2,1)S(1)} %collective-permute-done.10.refs_1_, ...), custom_call_target="tpu_custom_call" | custom-call | flops 1048576 | bytes 65536 | tf_op jit(solution)/shard_map/partial_other_core/pallas_call | solution.py:230
  43.5 0.1 collective-permute-start.13
  43.6 2.3 %collective-permute-start.14 = (f32[96,128]{1,0:T(8,128)S(1)}, f32[96,128]{1,0:T(8,128)S(1)}, u32[]{:S(2)}, u32[]{:S(2)}) collective-permute-start(f32[96,128]{1,0:T(8,128)S(1)} %get-tuple-element.46), channel_id=1, source_target_pairs={{0,16},{8,24},{16,0},{24,8},{1,17},{9,25},{17,1},{25,9},{2,18},{10... | collective-permute-start | bytes 147464 | tf_op jit(solution)/shard_map/ppermute | solution.py:306
  45.9 1.5 %collective-permute-start.15 = (f32[96,128]{1,0:T(8,128)S(1)}, f32[96,128]{1,0:T(8,128)S(1)}, u32[]{:S(2)}, u32[]{:S(2)}) collective-permute-start(f32[96,128]{1,0:T(8,128)S(1)} %get-tuple-element.47), channel_id=1, source_target_pairs={{0,24},{8,16},{16,8},{24,0},{1,25},{9,17},{17,9},{25,1},{2,26},{10... | collective-permute-start | bytes 147464 | tf_op jit(solution)/shard_map/ppermute | solution.py:306
  47.5 1.5 %collective-permute-done.14 = f32[96,128]{1,0:T(8,128)S(1)} collective-permute-done((f32[96,128]{1,0:T(8,128)S(1)}, f32[96,128]{1,0:T(8,128)S(1)}, u32[]{:S(2)}, u32[]{:S(2)}) %collective-permute-start.14) | collective-permute-done | bytes 49184 | tf_op jit(solution)/shard_map/ppermute | solution.py:306
  49.0 1.1 %collective-permute-done.15 = f32[96,128]{1,0:T(8,128)S(1)} collective-permute-done((f32[96,128]{1,0:T(8,128)S(1)}, f32[96,128]{1,0:T(8,128)S(1)}, u32[]{:S(2)}, u32[]{:S(2)}) %collective-permute-start.15) | collective-permute-done | bytes 49184 | tf_op jit(solution)/shard_map/ppermute | solution.py:306
  50.1 7.0 %collective-permute-start.18 = (f32[96,128]{1,0:T(8,128)S(1)}, f32[96,128]{1,0:T(8,128)S(1)}, u32[]{:S(2)}, u32[]{:S(2)}) collective-permute-start(f32[96,128]{1,0:T(8,128)S(1)} %add_add_fusion.1), channel_id=1, source_target_pairs={{0,128},{32,160},{64,192},{96,224},{128,0},{160,32},{192,64},{224,... | collective-permute-start | bytes 147464 | tf_op jit(solution)/shard_map/ppermute | solution.py:307
  57.1 1.2 %collective-permute-start.16 = (f32[96,128]{1,0:T(8,128)S(1)}, f32[96,128]{1,0:T(8,128)S(1)}, u32[]{:S(2)}, u32[]{:S(2)}) collective-permute-start(f32[96,128]{1,0:T(8,128)S(1)} %add_add_fusion.1), channel_id=1, source_target_pairs={{0,64},{32,96},{64,0},{96,32},{128,192},{160,224},{192,128},{224,1... | collective-permute-start | bytes 147464 | tf_op jit(solution)/shard_map/ppermute | solution.py:307
  58.3 0.3 collective-permute-done.18
  58.6 3.7 %collective-permute-done.17 = f32[96,128]{1,0:T(8,128)S(1)} collective-permute-done((f32[96,128]{1,0:T(8,128)S(1)}, f32[96,128]{1,0:T(8,128)S(1)}, u32[]{:S(2)}, u32[]{:S(2)}) %collective-permute-start.17) | collective-permute-done | bytes 49184 | tf_op jit(solution)/shard_map/ppermute | solution.py:307
  62.3 0.8 collective-permute-start.19
  63.0 2.3 %collective-permute-done.19.other_ref = f32[96,128]{1,0:T(8,128)S(1)} collective-permute-done((f32[96,128]{1,0:T(8,128)S(1)}, f32[96,128]{1,0:T(8,128)S(1)}, u32[]{:S(2)}, u32[]{:S(2)}) %collective-permute-start.19) | collective-permute-done | bytes 49184 | tf_op jit(solution)/shard_map/ppermute | solution.py:308
  65.3 2.5 %interval_rows.1 = (f32[16,128]{1,0:T(8,128)S(1)}, f32[64,64]{1,0:T(8,128)S(1)}) custom-call(s32[3]{0:T(128)S(1)} %pad_add_fusion.place, f32[96,128]{1,0:T(8,128)S(1)} %add_add_fusion.total_ref, f32[96,128]{1,0:T(8,128)S(1)} %collective-permute-done.19.other_ref, f32[64,64]{1,0:T(8,128)S(1)} %get-tuple-element.48.gram_day_ref, ...), custom_call_target="tpu_custom_call" | custom-call | flops 1048576 | bytes 65536 | tf_op jit(solution)/shard_map/interval_rows/pallas_call | solution.py:230
  67.8 4.6 %collective-permute-start.20 = (f32[16,128]{1,0:T(8,128)S(1)}, f32[16,128]{1,0:T(8,128)S(1)}, u32[]{:S(2)}, u32[]{:S(2)}) collective-permute-start(f32[16,128]{1,0:T(8,128)S(1)} %get-tuple-element.49), channel_id=1, source_target_pairs={{0,1},{1,0},{2,3},{3,2},{4,5},{5,4},{6,7},{7,6},{8,9},{9,8},{10,11... | collective-permute-start | bytes 24584 | tf_op jit(solution)/shard_map/ppermute | solution.py:252
  72.4 0.8 collective-permute-done.20
  73.3 10.5 %all_to_all.5.recv_ref = f32[16,16,128]{2,1,0:T(8,128)S(1)} all-to-all(f32[16,16,128]{2,1,0:T(8,128)S(1)} %broadcast_in_dim.2), channel_id=1, replica_groups=mesh['z'=8,'x'=4,'y'=4,'core'=2] {'x','y'}, dimensions={0} | all-to-all | bytes 262144 | tf_op jit(solution)/shard_map/all_to_all | solution.py:317
  83.7 3.0 %day_rows.1 = (f32[32,64]{1,0:T(8,128)}, f32[16,64]{1,0:T(8,128)}) custom-call(s32[3]{0:T(128)S(1)} %pad_add_fusion.place, f32[16,16,128]{2,1,0:T(8,128)S(1)} %all_to_all.5.recv_ref, f32[64,64]{1,0:T(8,128)S(1)} %get-tuple-element.50.gram_ref), custom_call_target="tpu_custom_call" | custom-call | flops 1048576 | bytes 65536 | tf_op jit(solution)/shard_map/day_rows/pallas_call | solution.py:230
  (10 shorter events, 0.1 us)
Async XLA Ops:
  4.5 6.4 %collective-permute-start = (f32[264,1024]{1,0:T(8,128)S(1)}, f32[264,1024]{1,0:T(8,128)S(1)}, u32[]{:S(2)}, u32[]{:S(2)}) collective-permute-start(f32[264,1024]{1,0:T(8,128)S(1)} %get-tuple-element.30.sent_ref), channel_id=1, source_target_pairs={{0,1},{1,0},{2,3},{3,2},{4,5},{5,4},{6,7},{7,6},{8,9},{9,8},{10,11... | collective-permute-start | bytes 3244040 | tf_op jit(solution)/shard_map/ppermute | solution.py:252
  11.1 13.7 %collective-permute-start.1 = (f32[72,1024]{1,0:T(8,128)S(1)}, f32[72,1024]{1,0:T(8,128)S(1)}, u32[]{:S(2)}, u32[]{:S(2)}) collective-permute-start(f32[72,1024]{1,0:T(8,128)S(1)} %get-tuple-element.32), channel_id=1, source_target_pairs={{0,4},{2,6},{4,0},{6,2},{1,5},{3,7},{5,1},{7,3},{8,12},{10,14},{12... | collective-permute-start | bytes 884744 | tf_op jit(solution)/shard_map/ppermute | solution.py:255
  12.4 10.7 %collective-permute-start.2 = (f32[72,512]{1,0:T(8,128)S(1)}, f32[72,512]{1,0:T(8,128)S(1)}, u32[]{:S(2)}, u32[]{:S(2)}) collective-permute-start(f32[72,512]{1,0:T(8,128)S(1)} %get-tuple-element.33), channel_id=1, source_target_pairs={{0,2},{2,0},{4,6},{6,4},{1,3},{3,1},{5,7},{7,5},{8,10},{10,8},{12,... | collective-permute-start | bytes 442376 | tf_op jit(solution)/shard_map/ppermute | solution.py:255
  12.7 12.0 %collective-permute-start.3 = (f32[72,512]{1,0:T(8,128)S(1)}, f32[72,512]{1,0:T(8,128)S(1)}, u32[]{:S(2)}, u32[]{:S(2)}) collective-permute-start(f32[72,512]{1,0:T(8,128)S(1)} %get-tuple-element.34), channel_id=1, source_target_pairs={{0,6},{2,4},{4,2},{6,0},{1,7},{3,5},{5,3},{7,1},{8,14},{10,12},{12... | collective-permute-start | bytes 442376 | tf_op jit(solution)/shard_map/ppermute | solution.py:255
  14.4 12.1 %collective-permute-start.4 = (f32[64,512]{1,0:T(8,128)S(1)}, f32[64,512]{1,0:T(8,128)S(1)}, u32[]{:S(2)}, u32[]{:S(2)}) collective-permute-start(f32[64,512]{1,0:T(8,128)S(1)} %get-tuple-element.35), channel_id=1, source_target_pairs={{0,2},{2,0},{4,6},{6,4},{1,3},{3,1},{5,7},{7,5},{8,10},{10,8},{12,... | collective-permute-start | bytes 393224 | tf_op jit(solution)/shard_map/ppermute | solution.py:255
  14.4 13.1 %collective-permute-start.5 = (f32[64,512]{1,0:T(8,128)S(1)}, f32[64,512]{1,0:T(8,128)S(1)}, u32[]{:S(2)}, u32[]{:S(2)}) collective-permute-start(f32[64,512]{1,0:T(8,128)S(1)} %get-tuple-element.36), channel_id=1, source_target_pairs={{0,6},{2,4},{4,2},{6,0},{1,7},{3,5},{5,3},{7,1},{8,14},{10,12},{12... | collective-permute-start | bytes 393224 | tf_op jit(solution)/shard_map/ppermute | solution.py:255
  28.8 3.8 %collective-permute-start.7 = (bf16[64,1152]{1,0:T(8,128)(2,1)S(1)}, bf16[64,1152]{1,0:T(8,128)(2,1)S(1)}, u32[]{:S(2)}, u32[]{:S(2)}) collective-permute-start(bf16[64,1152]{1,0:T(8,128)(2,1)S(1)} %get-tuple-element.40.low.refs_6_), channel_id=1, source_target_pairs={{0,1},{1,0},{2,3},{3,2},{4,5},{5,4},{6,7},{7,6},{8,9},{9,8},{10,11... | collective-permute-start | bytes 442376 | tf_op jit(solution)/shard_map/ppermute | solution.py:252
  29.3 9.8 %collective-permute-start.6 = (bf16[64,1152]{1,0:T(8,128)(2,1)S(1)}, bf16[64,1152]{1,0:T(8,128)(2,1)S(1)}, u32[]{:S(2)}, u32[]{:S(2)}) collective-permute-start(bf16[64,1152]{1,0:T(8,128)(2,1)S(1)} %get-tuple-element.40.low.refs_6_), channel_id=1, source_target_pairs={{0,6},{2,4},{4,2},{6,0},{1,7},{3,5},{5,3},{7,1},{8,14},{10,12},{12... | collective-permute-start | bytes 442376 | tf_op jit(solution)/shard_map/ppermute | solution.py:255
  30.3 8.8 %collective-permute-start.11 = (bf16[64,1152]{1,0:T(8,128)(2,1)S(1)}, bf16[64,1152]{1,0:T(8,128)(2,1)S(1)}, u32[]{:S(2)}, u32[]{:S(2)}) collective-permute-start(bf16[64,1152]{1,0:T(8,128)(2,1)S(1)} %get-tuple-element.40.low.refs_6_), channel_id=1, source_target_pairs={{0,4},{2,6},{4,0},{6,2},{1,5},{3,7},{5,1},{7,3},{8,12},{10,14},{12... | collective-permute-start | bytes 442376 | tf_op jit(solution)/shard_map/ppermute | solution.py:255
  30.8 9.1 %collective-permute-start.9 = (bf16[64,1152]{1,0:T(8,128)(2,1)S(1)}, bf16[64,1152]{1,0:T(8,128)(2,1)S(1)}, u32[]{:S(2)}, u32[]{:S(2)}) collective-permute-start(bf16[64,1152]{1,0:T(8,128)(2,1)S(1)} %get-tuple-element.40.low.refs_6_), channel_id=1, source_target_pairs={{0,2},{2,0},{4,6},{6,4},{1,3},{3,1},{5,7},{7,5},{8,10},{10,8},{12,... | collective-permute-start | bytes 442376 | tf_op jit(solution)/shard_map/ppermute | solution.py:255
  39.1 2.4 %collective-permute-start.12 = (bf16[64,1152]{1,0:T(8,128)(2,1)S(1)}, bf16[64,1152]{1,0:T(8,128)(2,1)S(1)}, u32[]{:S(2)}, u32[]{:S(2)}) collective-permute-start(bf16[64,1152]{1,0:T(8,128)(2,1)S(1)} %collective-permute-done.11.low2.refs_5_), channel_id=1, source_target_pairs={{0,1},{1,0},{2,3},{3,2},{4,5},{5,4},{6,7},{7,6},{8,9},{9,8},{10,11... | collective-permute-start | bytes 442376 | tf_op jit(solution)/shard_map/ppermute | solution.py:252
  39.9 1.6 %collective-permute-start.10 = (bf16[64,1152]{1,0:T(8,128)(2,1)S(1)}, bf16[64,1152]{1,0:T(8,128)(2,1)S(1)}, u32[]{:S(2)}, u32[]{:S(2)}) collective-permute-start(bf16[64,1152]{1,0:T(8,128)(2,1)S(1)} %collective-permute-done.9.low1.refs_4_), channel_id=1, source_target_pairs={{0,1},{1,0},{2,3},{3,2},{4,5},{5,4},{6,7},{7,6},{8,9},{9,8},{10,11... | collective-permute-start | bytes 442376 | tf_op jit(solution)/shard_map/ppermute | solution.py:252
  40.5 1.4 %collective-permute-start.8 = (bf16[64,1152]{1,0:T(8,128)(2,1)S(1)}, bf16[64,1152]{1,0:T(8,128)(2,1)S(1)}, u32[]{:S(2)}, u32[]{:S(2)}) collective-permute-start(bf16[64,1152]{1,0:T(8,128)(2,1)S(1)} %collective-permute-done.6.low0.refs_3_), channel_id=1, source_target_pairs={{0,1},{1,0},{2,3},{3,2},{4,5},{5,4},{6,7},{7,6},{8,9},{9,8},{10,11... | collective-permute-start | bytes 442376 | tf_op jit(solution)/shard_map/ppermute | solution.py:252
  43.5 3.9 %collective-permute-start.13 = (f32[96,128]{1,0:T(8,128)S(1)}, f32[96,128]{1,0:T(8,128)S(1)}, u32[]{:S(2)}, u32[]{:S(2)}) collective-permute-start(f32[96,128]{1,0:T(8,128)S(1)} %get-tuple-element.45), channel_id=1, source_target_pairs={{0,8},{8,0},{16,24},{24,16},{1,9},{9,1},{17,25},{25,17},{2,10},{10... | collective-permute-start | bytes 147464 | tf_op jit(solution)/shard_map/ppermute | solution.py:306
  43.6 5.4 %collective-permute-start.14 = (f32[96,128]{1,0:T(8,128)S(1)}, f32[96,128]{1,0:T(8,128)S(1)}, u32[]{:S(2)}, u32[]{:S(2)}) collective-permute-start(f32[96,128]{1,0:T(8,128)S(1)} %get-tuple-element.46), channel_id=1, source_target_pairs={{0,16},{8,24},{16,0},{24,8},{1,17},{9,25},{17,1},{25,9},{2,18},{10... | collective-permute-start | bytes 147464 | tf_op jit(solution)/shard_map/ppermute | solution.py:306
  45.9 4.2 %collective-permute-start.15 = (f32[96,128]{1,0:T(8,128)S(1)}, f32[96,128]{1,0:T(8,128)S(1)}, u32[]{:S(2)}, u32[]{:S(2)}) collective-permute-start(f32[96,128]{1,0:T(8,128)S(1)} %get-tuple-element.47), channel_id=1, source_target_pairs={{0,24},{8,16},{16,8},{24,0},{1,25},{9,17},{17,9},{25,1},{2,26},{10... | collective-permute-start | bytes 147464 | tf_op jit(solution)/shard_map/ppermute | solution.py:306
  50.1 8.5 %collective-permute-start.18 = (f32[96,128]{1,0:T(8,128)S(1)}, f32[96,128]{1,0:T(8,128)S(1)}, u32[]{:S(2)}, u32[]{:S(2)}) collective-permute-start(f32[96,128]{1,0:T(8,128)S(1)} %add_add_fusion.1), channel_id=1, source_target_pairs={{0,128},{32,160},{64,192},{96,224},{128,0},{160,32},{192,64},{224,... | collective-permute-start | bytes 147464 | tf_op jit(solution)/shard_map/ppermute | solution.py:307
  57.1 5.1 %collective-permute-start.17 = (f32[96,128]{1,0:T(8,128)S(1)}, f32[96,128]{1,0:T(8,128)S(1)}, u32[]{:S(2)}, u32[]{:S(2)}) collective-permute-start(f32[96,128]{1,0:T(8,128)S(1)} %add_add_fusion.1), channel_id=1, source_target_pairs={{0,192},{32,224},{64,128},{96,160},{128,64},{160,96},{192,0},{224,... | collective-permute-start | bytes 147464 | tf_op jit(solution)/shard_map/ppermute | solution.py:307
  57.1 5.1 %collective-permute-start.16 = (f32[96,128]{1,0:T(8,128)S(1)}, f32[96,128]{1,0:T(8,128)S(1)}, u32[]{:S(2)}, u32[]{:S(2)}) collective-permute-start(f32[96,128]{1,0:T(8,128)S(1)} %add_add_fusion.1), channel_id=1, source_target_pairs={{0,64},{32,96},{64,0},{96,32},{128,192},{160,224},{192,128},{224,1... | collective-permute-start | bytes 147464 | tf_op jit(solution)/shard_map/ppermute | solution.py:307
  62.3 3.0 %collective-permute-start.19 = (f32[96,128]{1,0:T(8,128)S(1)}, f32[96,128]{1,0:T(8,128)S(1)}, u32[]{:S(2)}, u32[]{:S(2)}) collective-permute-start(f32[96,128]{1,0:T(8,128)S(1)} %add_add_fusion.total_ref), channel_id=1, source_target_pairs={{0,32},{32,0},{64,96},{96,64},{128,160},{160,128},{192,224},{224,1... | collective-permute-start | bytes 147464 | tf_op jit(solution)/shard_map/ppermute | solution.py:308
  67.8 5.4 %collective-permute-start.20 = (f32[16,128]{1,0:T(8,128)S(1)}, f32[16,128]{1,0:T(8,128)S(1)}, u32[]{:S(2)}, u32[]{:S(2)}) collective-permute-start(f32[16,128]{1,0:T(8,128)S(1)} %get-tuple-element.49), channel_id=1, source_target_pairs={{0,1},{1,0},{2,3},{3,2},{4,5},{5,4},{6,7},{7,6},{8,9},{9,8},{10,11... | collective-permute-start | bytes 24584 | tf_op jit(solution)/shard_map/ppermute | solution.py:252

commit v5 on v4

--- a/solution.py
+++ b/solution.py
@@ -9,7 +9,7 @@
 
 RANK = 64
 HALF = 512
-ORDER = (3, 1, 2)
+ORDER = (2, 3, 1)
 HIGH = lax.Precision.HIGHEST
 F32 = jnp.float32
 BF16 = jnp.bfloat16
@@ -57,12 +57,12 @@
     return jnp.concatenate(parts, axis=0)
 
 
-def to_lanes(gram):
-    return jnp.concatenate([gram[at : at + 8] for at in range(0, RANK, 8)], axis=1)
+def to_lanes(rows):
+    return jnp.concatenate([rows[at : at + 8] for at in range(0, rows.shape[0], 8)], axis=1)
 
 
 def from_lanes(wide):
-    return jnp.concatenate([wide[:, at : at + RANK] for at in range(0, 8 * RANK, RANK)], axis=0)
+    return jnp.concatenate([wide[:, at : at + RANK] for at in range(0, wide.shape[1], RANK)], axis=0)
 
 
 def load_blocks(place, slab_ref, held_ref, sems, core):
@@ -90,8 +90,8 @@
     product = factor[...][:, None, :] * day[...][None, :, :]
     khatri = product.reshape(product.shape[0] * product.shape[1], RANK).T.astype(BF16)
     khatri_ref[...] = khatri
-    sums_ref[4 * RANK :, : 8 * RANK] = to_lanes(dot(factor[...], factor[...], ((0,), (0,))))
-    sums_ref[4 * RANK :, 8 * RANK :] = jnp.zeros((8, 1024 - 8 * RANK), F32)
+    sums_ref[4 * RANK :, : 4 * RANK] = to_lanes(factor[...])
+    sums_ref[4 * RANK :, 4 * RANK :] = jnp.zeros((8, 1024 - 4 * RANK), F32)
     day_twice_ref[...] = jnp.concatenate([day[...], day[...]], axis=1)
     for d in range(4):
         copies[d].wait()
@@ -114,18 +114,18 @@
 
 
 def add_kernel(keep_ref, sent_ref, got_ref, own, two, one_a, three_a, one_b, three_b):
-    gram = sent_ref[4 * RANK :, : 8 * RANK] + got_ref[4 * RANK :, : 8 * RANK]
+    factor = jnp.concatenate([sent_ref[4 * RANK :, : 4 * RANK], got_ref[4 * RANK :, : 4 * RANK]], axis=1)
 
     def total(d, lanes):
         return keep_ref[d, :, lanes] + got_ref[d * RANK : (d + 1) * RANK, lanes]
 
     for d, out in ((0, own), (2, two)):
         out[:RANK] = total(d, slice(0, 1024))
-        out[RANK:, : 8 * RANK] = gram
+        out[RANK:, : 8 * RANK] = factor
         out[RANK:, 8 * RANK :] = jnp.zeros((8, 1024 - 8 * RANK), F32)
     for d, first, second in ((1, one_a, one_b), (3, three_a, three_b)):
         first[:RANK] = total(d, slice(0, HALF))
-        first[RANK:] = gram
+        first[RANK:] = factor
         second[...] = total(d, slice(HALF, 1024))
 
 
@@ -133,8 +133,9 @@
     day = day_ref[:, :RANK]
     gram_day = dot(day, day, ((0,), (0,)))
     gram_day_ref[...] = gram_day
-    gram = (own[RANK:, : 8 * RANK] + two[RANK:, : 8 * RANK]) + (one[RANK:] + three[RANK:])
-    inverse_ref[...] = inverse_of(from_lanes(gram) * gram_day)
+    wide = (own[RANK:, :HALF], two[RANK:, :HALF], one[RANK:], three[RANK:])
+    factor = jnp.concatenate([from_lanes(rows) for rows in wide], axis=0)
+    inverse_ref[...] = inverse_of(dot(factor, factor, ((0,), (0,))) * gram_day)
 
 
 def link_kernel(own, two, one_a, three_a, one_b, three_b, inverse_ref, link_ref, low_ref):
@@ -142,17 +143,14 @@
     second = (own[:RANK, HALF:] + two[:RANK, HALF:]) + (one_b[...] + three_b[...])
     link = dot(inverse_ref[...], jnp.concatenate([first, second], axis=1))
     link_ref[...] = link
-    low_ref[:, :1024] = link.astype(BF16)
-    gram = dot(link, link, ((1,), (1,)))
-    high = gram.astype(BF16)
-    rest = (gram - high.astype(F32)).astype(BF16)
-    low_ref[:, 1024:] = jnp.concatenate([high, rest], axis=1)
+    low_ref[...] = link.astype(BF16)
 
 
 def times_blocks(lows, held_ref, blocks):
     total = None
     for low, i in zip(lows, blocks):
-        term = dot(held_ref[i], low[:, : 1024], ((1,), (1,)), None)
+        rows = low[...]
+        term = dot(jnp.concatenate([held_ref[i], rows], axis=0), rows, ((1,), (1,)), None)
         total = term if total is None else total + term
     return total
 
@@ -165,14 +163,10 @@
     acc[...] = before[...] + times_blocks((low0, low1, low2), keep_ref, ORDER)
 
 
-def last_partial_kernel(place, *refs):
-    lows, (held, before), outs, acc = refs[:8], refs[8:10], refs[10:14], refs[14]
-    acc[...] = before[...] + times_blocks(lows[:3], held, ORDER)
-    halves = [low[:, 1024 :].astype(F32) for low in lows]
-    total = halves[0]
-    for half in halves[1:]:
-        total = total + half
-    packed = pack(total[:, :RANK] + total[:, RANK:])
+def last_partial_kernel(place, low0, low1, low2, send_ref, before, *refs):
+    outs, acc = refs[:4], refs[4]
+    acc[...] = before[...] + times_blocks((low0, low1, low2), send_ref, ORDER)
+    packed = pack(acc[512:])
     for d, out in enumerate(outs):
         at = pl.multiple_of((place[2] ^ d) * 128, 128)
         out[:RANK] = jnp.concatenate([acc[pl.ds(at, RANK)], acc[pl.ds(at + RANK, RANK)]], axis=1)
@@ -287,21 +281,21 @@
         inverse_kernel, (shape((RANK, RANK)),) * 2, (*parts[:4], day_twice), "link_inverse"
     )
     link, low = call(
-        link_kernel, (shape((RANK, 1024)), shape((RANK, 1152), BF16)), (*parts, inverse), "link_rows"
+        link_kernel, (shape((RANK, 1024)), shape((RANK, 1024), BF16)), (*parts, inverse), "link_rows"
     )
     lows = [along_y(low, d) for d in ORDER]
     low_other = other_core(low)
-    acc = call(first_partial_kernel, shape((512, RANK)), (low, low_other, held_keep, held_send), "partial_own")
+    acc = call(first_partial_kernel, shape((576, RANK)), (low, low_other, held_keep, held_send), "partial_own")
     lows[0] = lax.optimization_barrier((lows[0], acc))[0]
     others = [other_core(one) for one in lows]
-    acc = call(second_partial_kernel, shape((512, RANK)), (*lows, held_keep, acc), "partial_own_core")
+    acc = call(second_partial_kernel, shape((576, RANK)), (*lows, held_keep, acc), "partial_own_core")
     outgoing = call(
         last_partial_kernel,
         (shape((96, 128)),) * 4,
-        (place, *others, *lows, low, low_other, held_send, acc),
+        (place, *others, held_send, acc),
         "partial_other_core",
         smem,
-        [pltpu.VMEM((512, RANK), F32)],
+        [pltpu.VMEM((576, RANK), F32)],
     )
     over_x = sum([lax.ppermute(outgoing[d], "x", partners(4, d)) for d in (1, 2, 3)], outgoing[0])
     over_z = sum([lax.ppermute(over_x, "z", partners(8, d)) for d in (2, 6, 4)], over_x)

time: 86.9 us -> 85.6 us (0.985)
  waiting for transfers between devices: 25.8 us -> 24.8 us
    ppermute x8, waiting for transfers between devices: 15.8 us -> 14.7 us  [along_y(): return lax.ppermute(a, 'y', partners(4, d))]
  transfers between devices with their start and end apart: 21 -> 21, of which waited for: 11 -> 13; matrix products, arithmetic and copies ran while one was open for 0% -> 0% of each run, Pallas kernels for 7% -> 8%
where the time goes in v5:
time: 85.6 us; the launch traced here: 85.4 us
  starting transfers between devices  30.7 us (36%)
  waiting for transfers between devices  24.8 us (29%)
  Pallas kernels  18.8 us (22%)
  blocking collectives  10.2 us (12%)
    pallas_call x10, Pallas kernels, call(): pl.pallas_call(kernel, out_shape=out_shape, in_specs=[pl.BlockSpec(memory...  18.8 us
    ppermute x8, waiting for transfers between devices, along_y(): return lax.ppermute(a, 'y', partners(4, d))  14.7 us
    all_to_all x1, blocking collectives, body(): lax.all_to_all(jnp.broadcast_to(found[None], (16, 16, 128)), ('x', 'y'),...  10.2 us
    ppermute x6, starting transfers between devices, other_core(): return lax.ppermute(a, 'core', partners(2, 1))  9.75 us
    ppermute x3, starting transfers between devices, body(): lax.ppermute(over_x, 'z', partners(8, d))  8.2 us
    ppermute x8, starting transfers between devices, along_y(): return lax.ppermute(a, 'y', partners(4, d))  8.08 us
    ppermute x3, starting transfers between devices, body(): lax.ppermute(outgoing[d], 'x', partners(4, d))  3.95 us
    ppermute x3, waiting for transfers between devices, body(): lax.ppermute(over_x, 'z', partners(8, d))  3.93 us
  transfers between devices with their start and end apart: 21, of which 13 were waited for; matrix products, arithmetic and copies ran while one was open for 0% of the time, Pallas kernels for 8%

profile of v5, /device:TPU:1, one launch (start us, length us, event | category | flops | bytes accessed | tf_op | source)
XLA Modules:
  0.0 85.4 jit_solution(4418678567426693259)
XLA Ops:
  0.6 0.1 pad_add_fusion.place
  0.7 3.6 %sums_to_send.1 = (f32[264,1024]{1,0:T(8,128)S(1)}, bf16[4,512,1024]{2,1,0:T(8,128)(2,1)S(1)}, bf16[64,512]{1,0:T(8,128)(2,1)S(1)}, f32[16,128]{1,0:T(8,128)S(1)}) custom-call(s32[3]{0:T(128)S(1)} %pad_add_fusion.place, bf16[512,8192]{1,0:T(8,128)(2,1)} %bitcast.5, f32[32,64]{1,0:T(8,128)} %interval_ref.1, f32[16,64]{1,0:T(8,128)} %day_ref.1), custom_call_target="tpu_custom_call" | custom-call | flops 1048576 | bytes 65536 | tf_op jit(solution)/shard_map/sums_to_send/pallas_call | solution.py:224
  4.3 3.3 %collective-permute-start = (f32[264,1024]{1,0:T(8,128)S(1)}, f32[264,1024]{1,0:T(8,128)S(1)}, u32[]{:S(2)}, u32[]{:S(2)}) collective-permute-start(f32[264,1024]{1,0:T(8,128)S(1)} %get-tuple-element.30.sent_ref), channel_id=1, source_target_pairs={{0,1},{1,0},{2,3},{3,2},{4,5},{5,4},{6,7},{7,6},{8,9},{9,8},{10,11... | collective-permute-start | bytes 3244040 | tf_op jit(solution)/shard_map/ppermute | solution.py:246
  7.6 3.1 %sums_to_keep.1 = (f32[4,64,1024]{2,1,0:T(8,128)S(1)}, bf16[4,512,1024]{2,1,0:T(8,128)(2,1)S(1)}) custom-call(s32[3]{0:T(128)S(1)} %pad_add_fusion.place, bf16[512,8192]{1,0:T(8,128)(2,1)} %bitcast.6, bf16[64,512]{1,0:T(8,128)(2,1)S(1)} %get-tuple-element.28.khatri_ref), custom_call_target="tpu_custom_call" | custom-call | flops 1048576 | bytes 65536 | tf_op jit(solution)/shard_map/sums_to_keep/pallas_call | solution.py:224
  10.7 0.0 collective-permute-done.got_ref
  10.7 0.1 add_cores.1
  10.8 1.3 %collective-permute-start.1 = (f32[72,1024]{1,0:T(8,128)S(1)}, f32[72,1024]{1,0:T(8,128)S(1)}, u32[]{:S(2)}, u32[]{:S(2)}) collective-permute-start(f32[72,1024]{1,0:T(8,128)S(1)} %get-tuple-element.32), channel_id=1, source_target_pairs={{0,4},{2,6},{4,0},{6,2},{1,5},{3,7},{5,1},{7,3},{8,12},{10,14},{12... | collective-permute-start | bytes 884744 | tf_op jit(solution)/shard_map/ppermute | solution.py:249
  12.1 0.4 collective-permute-start.2
  12.5 1.7 %collective-permute-start.3 = (f32[72,512]{1,0:T(8,128)S(1)}, f32[72,512]{1,0:T(8,128)S(1)}, u32[]{:S(2)}, u32[]{:S(2)}) collective-permute-start(f32[72,512]{1,0:T(8,128)S(1)} %get-tuple-element.34), channel_id=1, source_target_pairs={{0,6},{2,4},{4,2},{6,0},{1,7},{3,5},{5,3},{7,1},{8,14},{10,12},{12... | collective-permute-start | bytes 442376 | tf_op jit(solution)/shard_map/ppermute | solution.py:249
  14.2 0.0 collective-permute-start.4
  14.2 1.5 %collective-permute-start.5 = (f32[64,512]{1,0:T(8,128)S(1)}, f32[64,512]{1,0:T(8,128)S(1)}, u32[]{:S(2)}, u32[]{:S(2)}) collective-permute-start(f32[64,512]{1,0:T(8,128)S(1)} %get-tuple-element.36), channel_id=1, source_target_pairs={{0,6},{2,4},{4,2},{6,0},{1,7},{3,5},{5,3},{7,1},{8,14},{10,12},{12... | collective-permute-start | bytes 393224 | tf_op jit(solution)/shard_map/ppermute | solution.py:249
  15.7 7.2 %collective-permute-done.2.one.one_a = f32[72,512]{1,0:T(8,128)S(1)} collective-permute-done((f32[72,512]{1,0:T(8,128)S(1)}, f32[72,512]{1,0:T(8,128)S(1)}, u32[]{:S(2)}, u32[]{:S(2)}) %collective-permute-start.2) | collective-permute-done | bytes 147488 | tf_op jit(solution)/shard_map/ppermute | solution.py:249
  22.9 1.7 %collective-permute-done.3.three.three_a = f32[72,512]{1,0:T(8,128)S(1)} collective-permute-done((f32[72,512]{1,0:T(8,128)S(1)}, f32[72,512]{1,0:T(8,128)S(1)}, u32[]{:S(2)}, u32[]{:S(2)}) %collective-permute-start.3) | collective-permute-done | bytes 147488 | tf_op jit(solution)/shard_map/ppermute | solution.py:249
  24.5 0.0 collective-permute-done.1.two
  24.5 1.8 %link_inverse.1 = (f32[64,64]{1,0:T(8,128)S(1)}, f32[64,64]{1,0:T(8,128)S(1)}) custom-call(f32[72,1024]{1,0:T(8,128)S(1)} %get-tuple-element.31.own, f32[72,1024]{1,0:T(8,128)S(1)} %collective-permute-done.1.two, f32[72,512]{1,0:T(8,128)S(1)} %collective-permute-done.2.one.one_a, f32[72,512]{1,0:T(8,128)S(1)} %collective-permute-done.3.three.three_a, ...), custom_call_target="tpu_custom_call" | custom-call | flops 1048576 | bytes 65536 | tf_op jit(solution)/shard_map/link_inverse/pallas_call | solution.py:224
  26.4 1.0 %collective-permute-done.5.three_b = f32[64,512]{1,0:T(8,128)S(1)} collective-permute-done((f32[64,512]{1,0:T(8,128)S(1)}, f32[64,512]{1,0:T(8,128)S(1)}, u32[]{:S(2)}, u32[]{:S(2)}) %collective-permute-start.5) | collective-permute-done | bytes 131104 | tf_op jit(solution)/shard_map/ppermute | solution.py:249
  27.3 1.1 %link_rows.1 = (f32[64,1024]{1,0:T(8,128)}, bf16[64,1024]{1,0:T(8,128)(2,1)S(1)}) custom-call(f32[72,1024]{1,0:T(8,128)S(1)} %get-tuple-element.31.own, f32[72,1024]{1,0:T(8,128)S(1)} %collective-permute-done.1.two, f32[72,512]{1,0:T(8,128)S(1)} %collective-permute-done.2.one.one_a, f32[72,512]{1,0:T(8,128)S(1)} %collective-permute-done.3.three.three_a, ...), custom_call_target="tpu_custom_call" | custom-call | flops 1048576 | bytes 65536 | tf_op jit(solution)/shard_map/link_rows/pallas_call | solution.py:224
  28.4 0.5 collective-permute-start.7
  28.9 1.2 %collective-permute-start.6 = (bf16[64,1024]{1,0:T(8,128)(2,1)S(1)}, bf16[64,1024]{1,0:T(8,128)(2,1)S(1)}, u32[]{:S(2)}, u32[]{:S(2)}) collective-permute-start(bf16[64,1024]{1,0:T(8,128)(2,1)S(1)} %get-tuple-element.40.low), channel_id=1, source_target_pairs={{0,4},{2,6},{4,0},{6,2},{1,5},{3,7},{5,1},{7,3},{8,12},{10,14},{12... | collective-permute-start | bytes 393224 | tf_op jit(solution)/shard_map/ppermute | solution.py:249
  30.1 0.4 collective-permute-start.11
  30.5 1.7 %collective-permute-start.9 = (bf16[64,1024]{1,0:T(8,128)(2,1)S(1)}, bf16[64,1024]{1,0:T(8,128)(2,1)S(1)}, u32[]{:S(2)}, u32[]{:S(2)}) collective-permute-start(bf16[64,1024]{1,0:T(8,128)(2,1)S(1)} %get-tuple-element.40.low), channel_id=1, source_target_pairs={{0,6},{2,4},{4,2},{6,0},{1,7},{3,5},{5,3},{7,1},{8,14},{10,12},{12... | collective-permute-start | bytes 393224 | tf_op jit(solution)/shard_map/ppermute | solution.py:249
  32.2 0.8 partial_own.1.before
  33.0 2.6 %collective-permute-done.6.low0 = bf16[64,1024]{1,0:T(8,128)(2,1)S(1)} collective-permute-done((bf16[64,1024]{1,0:T(8,128)(2,1)S(1)}, bf16[64,1024]{1,0:T(8,128)(2,1)S(1)}, u32[]{:S(2)}, u32[]{:S(2)}) %collective-permute-start.6) | collective-permute-done | bytes 131104 | tf_op jit(solution)/shard_map/ppermute | solution.py:249
  35.6 1.4 %collective-permute-done.11.low2 = bf16[64,1024]{1,0:T(8,128)(2,1)S(1)} collective-permute-done((bf16[64,1024]{1,0:T(8,128)(2,1)S(1)}, bf16[64,1024]{1,0:T(8,128)(2,1)S(1)}, u32[]{:S(2)}, u32[]{:S(2)}) %collective-permute-start.11) | collective-permute-done | bytes 131104 | tf_op jit(solution)/shard_map/ppermute | solution.py:249
  37.0 0.8 collective-permute-start.12
  37.8 0.9 %collective-permute-done.9.low1 = bf16[64,1024]{1,0:T(8,128)(2,1)S(1)} collective-permute-done((bf16[64,1024]{1,0:T(8,128)(2,1)S(1)}, bf16[64,1024]{1,0:T(8,128)(2,1)S(1)}, u32[]{:S(2)}, u32[]{:S(2)}) %collective-permute-start.9) | collective-permute-done | bytes 131104 | tf_op jit(solution)/shard_map/ppermute | solution.py:249
  38.7 0.5 collective-permute-start.10
  39.2 0.0 collective-permute-start.8
  39.2 1.1 %partial_own_core.1.before = f32[576,64]{1,0:T(8,128)S(1)} custom-call(bf16[64,1024]{1,0:T(8,128)(2,1)S(1)} %collective-permute-done.6.low0, bf16[64,1024]{1,0:T(8,128)(2,1)S(1)} %collective-permute-done.9.low1, bf16[64,1024]{1,0:T(8,128)(2,1)S(1)} %collective-permute-done.11.low2, bf16[4,512,1024]{2,1,0:T(8,128)(2,1)S(1)} %get-tuple-element.41.keep_ref, ...), custom_call_target="tpu_custom_call" | custom-call | flops 1048576 | bytes 65536 | tf_op jit(solution)/shard_map/partial_own_core/pallas_call | solution.py:224
  40.3 0.2 collective-permute-done.8.low0
  40.5 1.7 %partial_other_core.1 = (f32[96,128]{1,0:T(8,128)S(1)}, f32[96,128]{1,0:T(8,128)S(1)}, f32[96,128]{1,0:T(8,128)S(1)}, f32[96,128]{1,0:T(8,128)S(1)}) custom-call(s32[3]{0:T(128)S(1)} %pad_add_fusion.place, bf16[64,1024]{1,0:T(8,128)(2,1)S(1)} %collective-permute-done.8.low0, bf16[64,1024]{1,0:T(8,128)(2,1)S(1)} %collective-permute-done.10.low1, ...), custom_call_target="tpu_custom_call" | custom-call | flops 1048576 | bytes 65536 | tf_op jit(solution)/shard_map/partial_other_core/pallas_call | solution.py:224
  42.2 0.2 collective-permute-start.13
  42.4 2.4 %collective-permute-start.14 = (f32[96,128]{1,0:T(8,128)S(1)}, f32[96,128]{1,0:T(8,128)S(1)}, u32[]{:S(2)}, u32[]{:S(2)}) collective-permute-start(f32[96,128]{1,0:T(8,128)S(1)} %get-tuple-element.46), channel_id=1, source_target_pairs={{0,16},{8,24},{16,0},{24,8},{1,17},{9,25},{17,1},{25,9},{2,18},{10... | collective-permute-start | bytes 147464 | tf_op jit(solution)/shard_map/ppermute | solution.py:300
  44.9 1.3 %collective-permute-start.15 = (f32[96,128]{1,0:T(8,128)S(1)}, f32[96,128]{1,0:T(8,128)S(1)}, u32[]{:S(2)}, u32[]{:S(2)}) collective-permute-start(f32[96,128]{1,0:T(8,128)S(1)} %get-tuple-element.47), channel_id=1, source_target_pairs={{0,24},{8,16},{16,8},{24,0},{1,25},{9,17},{17,9},{25,1},{2,26},{10... | collective-permute-start | bytes 147464 | tf_op jit(solution)/shard_map/ppermute | solution.py:300
  46.2 0.0 collective-permute-done.13
  46.2 1.0 %collective-permute-done.14 = f32[96,128]{1,0:T(8,128)S(1)} collective-permute-done((f32[96,128]{1,0:T(8,128)S(1)}, f32[96,128]{1,0:T(8,128)S(1)}, u32[]{:S(2)}, u32[]{:S(2)}) %collective-permute-start.14) | collective-permute-done | bytes 49184 | tf_op jit(solution)/shard_map/ppermute | solution.py:300
  47.2 1.8 %collective-permute-done.15 = f32[96,128]{1,0:T(8,128)S(1)} collective-permute-done((f32[96,128]{1,0:T(8,128)S(1)}, f32[96,128]{1,0:T(8,128)S(1)}, u32[]{:S(2)}, u32[]{:S(2)}) %collective-permute-start.15) | collective-permute-done | bytes 49184 | tf_op jit(solution)/shard_map/ppermute | solution.py:300
  49.0 7.0 %collective-permute-start.18 = (f32[96,128]{1,0:T(8,128)S(1)}, f32[96,128]{1,0:T(8,128)S(1)}, u32[]{:S(2)}, u32[]{:S(2)}) collective-permute-start(f32[96,128]{1,0:T(8,128)S(1)} %add_add_fusion.1), channel_id=1, source_target_pairs={{0,128},{32,160},{64,192},{96,224},{128,0},{160,32},{192,64},{224,... | collective-permute-start | bytes 147464 | tf_op jit(solution)/shard_map/ppermute | solution.py:301
  56.1 1.2 %collective-permute-start.16 = (f32[96,128]{1,0:T(8,128)S(1)}, f32[96,128]{1,0:T(8,128)S(1)}, u32[]{:S(2)}, u32[]{:S(2)}) collective-permute-start(f32[96,128]{1,0:T(8,128)S(1)} %add_add_fusion.1), channel_id=1, source_target_pairs={{0,64},{32,96},{64,0},{96,32},{128,192},{160,224},{192,128},{224,1... | collective-permute-start | bytes 147464 | tf_op jit(solution)/shard_map/ppermute | solution.py:301
  57.2 0.3 collective-permute-done.18
  57.5 3.6 %collective-permute-done.17 = f32[96,128]{1,0:T(8,128)S(1)} collective-permute-done((f32[96,128]{1,0:T(8,128)S(1)}, f32[96,128]{1,0:T(8,128)S(1)}, u32[]{:S(2)}, u32[]{:S(2)}) %collective-permute-start.17) | collective-permute-done | bytes 49184 | tf_op jit(solution)/shard_map/ppermute | solution.py:301
  61.2 0.8 collective-permute-start.19
  61.9 2.3 %collective-permute-done.19.other_ref = f32[96,128]{1,0:T(8,128)S(1)} collective-permute-done((f32[96,128]{1,0:T(8,128)S(1)}, f32[96,128]{1,0:T(8,128)S(1)}, u32[]{:S(2)}, u32[]{:S(2)}) %collective-permute-start.19) | collective-permute-done | bytes 49184 | tf_op jit(solution)/shard_map/ppermute | solution.py:302
  64.2 2.5 %interval_rows.1 = (f32[16,128]{1,0:T(8,128)S(1)}, f32[64,64]{1,0:T(8,128)S(1)}) custom-call(s32[3]{0:T(128)S(1)} %pad_add_fusion.place, f32[96,128]{1,0:T(8,128)S(1)} %add_add_fusion.total_ref, f32[96,128]{1,0:T(8,128)S(1)} %collective-permute-done.19.other_ref, f32[64,64]{1,0:T(8,128)S(1)} %get-tuple-element.48.gram_day_ref, ...), custom_call_target="tpu_custom_call" | custom-call | flops 1048576 | bytes 65536 | tf_op jit(solution)/shard_map/interval_rows/pallas_call | solution.py:224
  66.7 4.6 %collective-permute-start.20 = (f32[16,128]{1,0:T(8,128)S(1)}, f32[16,128]{1,0:T(8,128)S(1)}, u32[]{:S(2)}, u32[]{:S(2)}) collective-permute-start(f32[16,128]{1,0:T(8,128)S(1)} %get-tuple-element.49), channel_id=1, source_target_pairs={{0,1},{1,0},{2,3},{3,2},{4,5},{5,4},{6,7},{7,6},{8,9},{9,8},{10,11... | collective-permute-start | bytes 24584 | tf_op jit(solution)/shard_map/ppermute | solution.py:246
  71.4 0.8 collective-permute-done.20
  72.2 10.2 %all_to_all.5.recv_ref = f32[16,16,128]{2,1,0:T(8,128)S(1)} all-to-all(f32[16,16,128]{2,1,0:T(8,128)S(1)} %broadcast_in_dim.2), channel_id=1, replica_groups=mesh['z'=8,'x'=4,'y'=4,'core'=2] {'x','y'}, dimensions={0} | all-to-all | bytes 262144 | tf_op jit(solution)/shard_map/all_to_all | solution.py:311
  82.4 3.0 %day_rows.1 = (f32[32,64]{1,0:T(8,128)}, f32[16,64]{1,0:T(8,128)}) custom-call(s32[3]{0:T(128)S(1)} %pad_add_fusion.place, f32[16,16,128]{2,1,0:T(8,128)S(1)} %all_to_all.5.recv_ref, f32[64,64]{1,0:T(8,128)S(1)} %get-tuple-element.50.gram_ref), custom_call_target="tpu_custom_call" | custom-call | flops 1048576 | bytes 65536 | tf_op jit(solution)/shard_map/day_rows/pallas_call | solution.py:224
  (10 shorter events, 0.1 us)
Async XLA Ops:
  4.3 6.4 %collective-permute-start = (f32[264,1024]{1,0:T(8,128)S(1)}, f32[264,1024]{1,0:T(8,128)S(1)}, u32[]{:S(2)}, u32[]{:S(2)}) collective-permute-start(f32[264,1024]{1,0:T(8,128)S(1)} %get-tuple-element.30.sent_ref), channel_id=1, source_target_pairs={{0,1},{1,0},{2,3},{3,2},{4,5},{5,4},{6,7},{7,6},{8,9},{9,8},{10,11... | collective-permute-start | bytes 3244040 | tf_op jit(solution)/shard_map/ppermute | solution.py:246
  10.8 13.7 %collective-permute-start.1 = (f32[72,1024]{1,0:T(8,128)S(1)}, f32[72,1024]{1,0:T(8,128)S(1)}, u32[]{:S(2)}, u32[]{:S(2)}) collective-permute-start(f32[72,1024]{1,0:T(8,128)S(1)} %get-tuple-element.32), channel_id=1, source_target_pairs={{0,4},{2,6},{4,0},{6,2},{1,5},{3,7},{5,1},{7,3},{8,12},{10,14},{12... | collective-permute-start | bytes 884744 | tf_op jit(solution)/shard_map/ppermute | solution.py:249
  12.1 10.7 %collective-permute-start.2 = (f32[72,512]{1,0:T(8,128)S(1)}, f32[72,512]{1,0:T(8,128)S(1)}, u32[]{:S(2)}, u32[]{:S(2)}) collective-permute-start(f32[72,512]{1,0:T(8,128)S(1)} %get-tuple-element.33), channel_id=1, source_target_pairs={{0,2},{2,0},{4,6},{6,4},{1,3},{3,1},{5,7},{7,5},{8,10},{10,8},{12,... | collective-permute-start | bytes 442376 | tf_op jit(solution)/shard_map/ppermute | solution.py:249
  12.5 12.0 %collective-permute-start.3 = (f32[72,512]{1,0:T(8,128)S(1)}, f32[72,512]{1,0:T(8,128)S(1)}, u32[]{:S(2)}, u32[]{:S(2)}) collective-permute-start(f32[72,512]{1,0:T(8,128)S(1)} %get-tuple-element.34), channel_id=1, source_target_pairs={{0,6},{2,4},{4,2},{6,0},{1,7},{3,5},{5,3},{7,1},{8,14},{10,12},{12... | collective-permute-start | bytes 442376 | tf_op jit(solution)/shard_map/ppermute | solution.py:249
  14.2 12.2 %collective-permute-start.4 = (f32[64,512]{1,0:T(8,128)S(1)}, f32[64,512]{1,0:T(8,128)S(1)}, u32[]{:S(2)}, u32[]{:S(2)}) collective-permute-start(f32[64,512]{1,0:T(8,128)S(1)} %get-tuple-element.35), channel_id=1, source_target_pairs={{0,2},{2,0},{4,6},{6,4},{1,3},{3,1},{5,7},{7,5},{8,10},{10,8},{12,... | collective-permute-start | bytes 393224 | tf_op jit(solution)/shard_map/ppermute | solution.py:249
  14.2 13.1 %collective-permute-start.5 = (f32[64,512]{1,0:T(8,128)S(1)}, f32[64,512]{1,0:T(8,128)S(1)}, u32[]{:S(2)}, u32[]{:S(2)}) collective-permute-start(f32[64,512]{1,0:T(8,128)S(1)} %get-tuple-element.36), channel_id=1, source_target_pairs={{0,6},{2,4},{4,2},{6,0},{1,7},{3,5},{5,3},{7,1},{8,14},{10,12},{12... | collective-permute-start | bytes 393224 | tf_op jit(solution)/shard_map/ppermute | solution.py:249
  28.4 3.8 %collective-permute-start.7 = (bf16[64,1024]{1,0:T(8,128)(2,1)S(1)}, bf16[64,1024]{1,0:T(8,128)(2,1)S(1)}, u32[]{:S(2)}, u32[]{:S(2)}) collective-permute-start(bf16[64,1024]{1,0:T(8,128)(2,1)S(1)} %get-tuple-element.40.low), channel_id=1, source_target_pairs={{0,1},{1,0},{2,3},{3,2},{4,5},{5,4},{6,7},{7,6},{8,9},{9,8},{10,11... | collective-permute-start | bytes 393224 | tf_op jit(solution)/shard_map/ppermute | solution.py:246
  28.9 6.6 %collective-permute-start.6 = (bf16[64,1024]{1,0:T(8,128)(2,1)S(1)}, bf16[64,1024]{1,0:T(8,128)(2,1)S(1)}, u32[]{:S(2)}, u32[]{:S(2)}) collective-permute-start(bf16[64,1024]{1,0:T(8,128)(2,1)S(1)} %get-tuple-element.40.low), channel_id=1, source_target_pairs={{0,4},{2,6},{4,0},{6,2},{1,5},{3,7},{5,1},{7,3},{8,12},{10,14},{12... | collective-permute-start | bytes 393224 | tf_op jit(solution)/shard_map/ppermute | solution.py:249
  30.1 6.8 %collective-permute-start.11 = (bf16[64,1024]{1,0:T(8,128)(2,1)S(1)}, bf16[64,1024]{1,0:T(8,128)(2,1)S(1)}, u32[]{:S(2)}, u32[]{:S(2)}) collective-permute-start(bf16[64,1024]{1,0:T(8,128)(2,1)S(1)} %get-tuple-element.40.low), channel_id=1, source_target_pairs={{0,2},{2,0},{4,6},{6,4},{1,3},{3,1},{5,7},{7,5},{8,10},{10,8},{12,... | collective-permute-start | bytes 393224 | tf_op jit(solution)/shard_map/ppermute | solution.py:249
  30.5 8.2 %collective-permute-start.9 = (bf16[64,1024]{1,0:T(8,128)(2,1)S(1)}, bf16[64,1024]{1,0:T(8,128)(2,1)S(1)}, u32[]{:S(2)}, u32[]{:S(2)}) collective-permute-start(bf16[64,1024]{1,0:T(8,128)(2,1)S(1)} %get-tuple-element.40.low), channel_id=1, source_target_pairs={{0,6},{2,4},{4,2},{6,0},{1,7},{3,5},{5,3},{7,1},{8,14},{10,12},{12... | collective-permute-start | bytes 393224 | tf_op jit(solution)/shard_map/ppermute | solution.py:249
  37.0 3.3 %collective-permute-start.12 = (bf16[64,1024]{1,0:T(8,128)(2,1)S(1)}, bf16[64,1024]{1,0:T(8,128)(2,1)S(1)}, u32[]{:S(2)}, u32[]{:S(2)}) collective-permute-start(bf16[64,1024]{1,0:T(8,128)(2,1)S(1)} %collective-permute-done.11.low2), channel_id=1, source_target_pairs={{0,1},{1,0},{2,3},{3,2},{4,5},{5,4},{6,7},{7,6},{8,9},{9,8},{10,11... | collective-permute-start | bytes 393224 | tf_op jit(solution)/shard_map/ppermute | solution.py:246
  38.7 1.6 %collective-permute-start.10 = (bf16[64,1024]{1,0:T(8,128)(2,1)S(1)}, bf16[64,1024]{1,0:T(8,128)(2,1)S(1)}, u32[]{:S(2)}, u32[]{:S(2)}) collective-permute-start(bf16[64,1024]{1,0:T(8,128)(2,1)S(1)} %collective-permute-done.9.low1), channel_id=1, source_target_pairs={{0,1},{1,0},{2,3},{3,2},{4,5},{5,4},{6,7},{7,6},{8,9},{9,8},{10,11... | collective-permute-start | bytes 393224 | tf_op jit(solution)/shard_map/ppermute | solution.py:246
  39.2 1.3 %collective-permute-start.8 = (bf16[64,1024]{1,0:T(8,128)(2,1)S(1)}, bf16[64,1024]{1,0:T(8,128)(2,1)S(1)}, u32[]{:S(2)}, u32[]{:S(2)}) collective-permute-start(bf16[64,1024]{1,0:T(8,128)(2,1)S(1)} %collective-permute-done.6.low0), channel_id=1, source_target_pairs={{0,1},{1,0},{2,3},{3,2},{4,5},{5,4},{6,7},{7,6},{8,9},{9,8},{10,11... | collective-permute-start | bytes 393224 | tf_op jit(solution)/shard_map/ppermute | solution.py:246
  42.2 3.9 %collective-permute-start.13 = (f32[96,128]{1,0:T(8,128)S(1)}, f32[96,128]{1,0:T(8,128)S(1)}, u32[]{:S(2)}, u32[]{:S(2)}) collective-permute-start(f32[96,128]{1,0:T(8,128)S(1)} %get-tuple-element.45), channel_id=1, source_target_pairs={{0,8},{8,0},{16,24},{24,16},{1,9},{9,1},{17,25},{25,17},{2,10},{10... | collective-permute-start | bytes 147464 | tf_op jit(solution)/shard_map/ppermute | solution.py:300
  42.4 4.8 %collective-permute-start.14 = (f32[96,128]{1,0:T(8,128)S(1)}, f32[96,128]{1,0:T(8,128)S(1)}, u32[]{:S(2)}, u32[]{:S(2)}) collective-permute-start(f32[96,128]{1,0:T(8,128)S(1)} %get-tuple-element.46), channel_id=1, source_target_pairs={{0,16},{8,24},{16,0},{24,8},{1,17},{9,25},{17,1},{25,9},{2,18},{10... | collective-permute-start | bytes 147464 | tf_op jit(solution)/shard_map/ppermute | solution.py:300
  44.9 4.2 %collective-permute-start.15 = (f32[96,128]{1,0:T(8,128)S(1)}, f32[96,128]{1,0:T(8,128)S(1)}, u32[]{:S(2)}, u32[]{:S(2)}) collective-permute-start(f32[96,128]{1,0:T(8,128)S(1)} %get-tuple-element.47), channel_id=1, source_target_pairs={{0,24},{8,16},{16,8},{24,0},{1,25},{9,17},{17,9},{25,1},{2,26},{10... | collective-permute-start | bytes 147464 | tf_op jit(solution)/shard_map/ppermute | solution.py:300
  49.0 8.5 %collective-permute-start.18 = (f32[96,128]{1,0:T(8,128)S(1)}, f32[96,128]{1,0:T(8,128)S(1)}, u32[]{:S(2)}, u32[]{:S(2)}) collective-permute-start(f32[96,128]{1,0:T(8,128)S(1)} %add_add_fusion.1), channel_id=1, source_target_pairs={{0,128},{32,160},{64,192},{96,224},{128,0},{160,32},{192,64},{224,... | collective-permute-start | bytes 147464 | tf_op jit(solution)/shard_map/ppermute | solution.py:301
  56.0 5.1 %collective-permute-start.17 = (f32[96,128]{1,0:T(8,128)S(1)}, f32[96,128]{1,0:T(8,128)S(1)}, u32[]{:S(2)}, u32[]{:S(2)}) collective-permute-start(f32[96,128]{1,0:T(8,128)S(1)} %add_add_fusion.1), channel_id=1, source_target_pairs={{0,192},{32,224},{64,128},{96,160},{128,64},{160,96},{192,0},{224,... | collective-permute-start | bytes 147464 | tf_op jit(solution)/shard_map/ppermute | solution.py:301
  56.1 5.1 %collective-permute-start.16 = (f32[96,128]{1,0:T(8,128)S(1)}, f32[96,128]{1,0:T(8,128)S(1)}, u32[]{:S(2)}, u32[]{:S(2)}) collective-permute-start(f32[96,128]{1,0:T(8,128)S(1)} %add_add_fusion.1), channel_id=1, source_target_pairs={{0,64},{32,96},{64,0},{96,32},{128,192},{160,224},{192,128},{224,1... | collective-permute-start | bytes 147464 | tf_op jit(solution)/shard_map/ppermute | solution.py:301
  61.2 3.0 %collective-permute-start.19 = (f32[96,128]{1,0:T(8,128)S(1)}, f32[96,128]{1,0:T(8,128)S(1)}, u32[]{:S(2)}, u32[]{:S(2)}) collective-permute-start(f32[96,128]{1,0:T(8,128)S(1)} %add_add_fusion.total_ref), channel_id=1, source_target_pairs={{0,32},{32,0},{64,96},{96,64},{128,160},{160,128},{192,224},{224,1... | collective-permute-start | bytes 147464 | tf_op jit(solution)/shard_map/ppermute | solution.py:302
  66.7 5.4 %collective-permute-start.20 = (f32[16,128]{1,0:T(8,128)S(1)}, f32[16,128]{1,0:T(8,128)S(1)}, u32[]{:S(2)}, u32[]{:S(2)}) collective-permute-start(f32[16,128]{1,0:T(8,128)S(1)} %get-tuple-element.49), channel_id=1, source_target_pairs={{0,1},{1,0},{2,3},{3,2},{4,5},{5,4},{6,7},{7,6},{8,9},{9,8},{10,11... | collective-permute-start | bytes 24584 | tf_op jit(solution)/shard_map/ppermute | solution.py:246

commit v6 on v5

--- a/solution.py
+++ b/solution.py
@@ -9,7 +9,6 @@
 
 RANK = 64
 HALF = 512
-ORDER = (2, 3, 1)
 HIGH = lax.Precision.HIGHEST
 F32 = jnp.float32
 BF16 = jnp.bfloat16
@@ -65,17 +64,16 @@
     return jnp.concatenate([wide[:, at : at + RANK] for at in range(0, wide.shape[1], RANK)], axis=0)
 
 
-def load_blocks(place, slab_ref, held_ref, sems, core):
+def load_blocks(slab_ref, held_ref, sems, core):
     copies = []
     for d in range(4):
-        at = pl.multiple_of((2 * (place[1] ^ d) + core) * 1024, 1024)
+        at = pl.multiple_of((2 * (lax.axis_index("y") ^ d) + core) * 1024, 1024)
         copies.append(pltpu.make_async_copy(slab_ref.at[:, pl.ds(at, 1024)], held_ref.at[d], sems.at[d]))
         copies[-1].start()
     return copies
 
 
-def send_kernel(
-    place, slab_ref, interval_ref, day_ref, sums_ref, held_ref, khatri_ref, day_twice_ref, sems, *own
+def send_kernel(slab_ref, interval_ref, day_ref, sums_ref, held_ref, khatri_ref, day_twice_ref, sems, *own
 ):
     factor, day, small_sems = own
     small = [
@@ -84,7 +82,7 @@
     ]
     for copy in small:
         copy.start()
-    copies = load_blocks(place, slab_ref, held_ref, sems, 1 - place[0])
+    copies = load_blocks(slab_ref, held_ref, sems, 1 - lax.axis_index("core"))
     for copy in small:
         copy.wait()
     product = factor[...][:, None, :] * day[...][None, :, :]
@@ -98,15 +96,11 @@
         sums_ref[d * RANK : (d + 1) * RANK] = dot(khatri, held_ref[d], precision=None)
 
 
-def keep_kernel(place, slab_ref, khatri_ref, sums_ref, held_ref, sems):
-    copies = load_blocks(place, slab_ref, held_ref, sems, place[0])
+def keep_kernel(slab_ref, khatri_ref, sums_ref, held_ref, sems):
+    copies = load_blocks(slab_ref, held_ref, sems, lax.axis_index("core"))
     for d in range(4):
         copies[d].wait()
         sums_ref[d] = dot(khatri_ref[...], held_ref[d], precision=None)
-
-
-def pack(gram):
-    return jnp.concatenate([gram[: RANK // 2], gram[RANK // 2 :]], axis=1)
 
 
 def unpack(packed):
@@ -150,8 +144,13 @@
     total = None
     for low, i in zip(lows, blocks):
         rows = low[...]
-        term = dot(jnp.concatenate([held_ref[i], rows], axis=0), rows, ((1,), (1,)), None)
-        total = term if total is None else total + term
+        none = jnp.zeros_like(rows)
+        for side in range(2):
+            starts = range(side * RANK, 512, 2 * RANK)
+            left = [held_ref[i, at : at + RANK] for at in starts] + [rows[side * 32 : side * 32 + 32]]
+            right = jnp.concatenate([none, rows] if side else [rows, none], axis=0)
+            term = dot(jnp.concatenate(left, axis=0), right, ((1,), (1,)), None)
+            total = term if total is None else total + term
     return total
 
 
@@ -159,18 +158,23 @@
     acc[...] = times_blocks((low,), keep_ref, (0,)) + times_blocks((low_other,), send_ref, (0,))
 
 
-def second_partial_kernel(low0, low1, low2, keep_ref, before, acc):
-    acc[...] = before[...] + times_blocks((low0, low1, low2), keep_ref, ORDER)
-
-
-def last_partial_kernel(place, low0, low1, low2, send_ref, before, *refs):
+def one_partial_kernel(block, low, keep_ref, before, acc):
+    acc[...] = before[...] + times_blocks((low,), keep_ref, (block,))
+
+
+def mixed_partial_kernel(low3, other2, other1, keep_ref, send_ref, before, acc):
+    acc[...] = (
+        before[...] + times_blocks((low3,), keep_ref, (3,)) + times_blocks((other2, other1), send_ref, (2, 1))
+    )
+
+
+def last_partial_kernel(low, send_ref, before, *refs):
     outs, acc = refs[:4], refs[4]
-    acc[...] = before[...] + times_blocks((low0, low1, low2), send_ref, ORDER)
-    packed = pack(acc[512:])
+    acc[...] = before[...] + times_blocks((low,), send_ref, (3,))
     for d, out in enumerate(outs):
-        at = pl.multiple_of((place[2] ^ d) * 128, 128)
-        out[:RANK] = jnp.concatenate([acc[pl.ds(at, RANK)], acc[pl.ds(at + RANK, RANK)]], axis=1)
-        out[RANK:] = packed
+        at = pl.multiple_of((lax.axis_index("x") ^ d) * RANK, RANK)
+        out[:RANK] = acc[pl.ds(at, RANK)]
+        out[RANK:] = acc[4 * RANK :]
 
 
 def inverse_of(system):
@@ -185,7 +189,7 @@
     return jnp.transpose(eliminate(shifted(system), rhs))[RANK : RANK + count]
 
 
-def interval_kernel(place, total_ref, other_ref, gram_day_ref, day_ref, out_ref, gram_ref):
+def interval_kernel(total_ref, other_ref, gram_day_ref, day_ref, out_ref, gram_ref):
     gram = unpack(total_ref[RANK:] + other_ref[RANK:])
     gram_ref[...] = gram
     partial = (total_ref[:RANK] + other_ref[:RANK]).reshape(4, 16, 2 * RANK)
@@ -196,11 +200,11 @@
     none = jnp.zeros((8, RANK), F32)
     out_ref[:8] = jnp.concatenate([day_part[:8], day_part[8:]], axis=1)
     out_ref[8:] = jnp.where(
-        place[0] == 0, jnp.concatenate([rows, none], axis=1), jnp.concatenate([none, rows], axis=1)
-    )
-
-
-def day_kernel(place, recv_ref, gram_ref, interval_ref, day_ref):
+        lax.axis_index("core") == 0, jnp.concatenate([rows, none], axis=1), jnp.concatenate([none, rows], axis=1)
+    )
+
+
+def day_kernel(recv_ref, gram_ref, interval_ref, day_ref):
     rows = recv_ref[:, 8:].reshape(8 * recv_ref.shape[0], 2 * RANK)
     gram_new = dot(rows, rows, ((0,), (0,)))
     gram_new = gram_new[:RANK, :RANK] + gram_new[RANK:, RANK:]
@@ -208,8 +212,8 @@
     for i in range(1, recv_ref.shape[0]):
         total = total + recv_ref[i, :8]
     for i in range(4):
-        both = recv_ref[i * 4 + place[1], 8:]
-        interval_ref[i * 8 : i * 8 + 8] = jnp.where(place[0] == 0, both[:, :RANK], both[:, RANK:])
+        both = recv_ref[i * 4 + lax.axis_index("y"), 8:]
+        interval_ref[i * 8 : i * 8 + 8] = jnp.where(lax.axis_index("core") == 0, both[:, :RANK], both[:, RANK:])
     day_ref[...] = solve_rows(
         gram_ref[...] * gram_new, jnp.concatenate([total[:, :RANK], total[:, RANK:]], axis=0)
     )
@@ -238,9 +242,7 @@
     flat = pltpu.with_memory_space_constraint(slab.reshape(intervals * days, links), pltpu.HBM)
     interval_factor = pltpu.with_memory_space_constraint(interval_factor, pltpu.HBM)
     day_factor = pltpu.with_memory_space_constraint(day_factor, pltpu.HBM)
-    place = jnp.stack([lax.axis_index(axis) for axis in ("core", "y", "x")]).astype(jnp.int32)
     held = shape((4, 512, 1024), BF16)
-    smem = {0: pltpu.SMEM}
 
     def other_core(a):
         return lax.ppermute(a, "core", partners(2, 1))
@@ -251,9 +253,9 @@
     send, held_send, khatri, day_twice = call(
         send_kernel,
         (shape((264, 1024)), held, shape((RANK, 512), BF16), shape((16, 2 * RANK))),
-        (place, flat, interval_factor, day_factor),
+        (flat, interval_factor, day_factor),
         "sums_to_send",
-        {0: pltpu.SMEM, 1: pl.ANY, 2: pl.ANY, 3: pl.ANY},
+        {0: pl.ANY, 1: pl.ANY, 2: pl.ANY},
         [
             pltpu.SemaphoreType.DMA((4,)),
             pltpu.VMEM((32, RANK), F32),
@@ -265,9 +267,9 @@
     keep, held_keep = call(
         keep_kernel,
         (shape((4, RANK, 1024)), held),
-        (place, flat, khatri),
+        (flat, khatri),
         "sums_to_keep",
-        {0: pltpu.SMEM, 1: pl.ANY},
+        {0: pl.ANY},
         [pltpu.SemaphoreType.DMA((4,))],
     )
     sums = call(
@@ -283,34 +285,43 @@
     link, low = call(
         link_kernel, (shape((RANK, 1024)), shape((RANK, 1024), BF16)), (*parts, inverse), "link_rows"
     )
-    lows = [along_y(low, d) for d in ORDER]
-    low_other = other_core(low)
-    acc = call(first_partial_kernel, shape((576, RANK)), (low, low_other, held_keep, held_send), "partial_own")
-    lows[0] = lax.optimization_barrier((lows[0], acc))[0]
-    others = [other_core(one) for one in lows]
-    acc = call(second_partial_kernel, shape((576, RANK)), (*lows, held_keep, acc), "partial_own_core")
+    low2, low3, low1 = [along_y(low, d) for d in (2, 3, 1)]
+    total = shape((288, 2 * RANK))
+
+    def after(one, acc):
+        return lax.optimization_barrier((one, acc))[0]
+
+    acc = call(first_partial_kernel, total, (low, other_core(low), held_keep, held_send), "partial_own")
+    low2 = after(low2, acc)
+    other2 = other_core(low2)
+    acc = call(functools.partial(one_partial_kernel, 2), total, (low2, held_keep, acc), "partial_two")
+    low1 = after(low1, acc)
+    other1 = other_core(low1)
+    acc = call(functools.partial(one_partial_kernel, 1), total, (low1, held_keep, acc), "partial_one")
+    low3 = after(low3, acc)
+    other3 = other_core(low3)
+    acc = call(mixed_partial_kernel, total, (low3, other2, other1, held_keep, held_send, acc), "partial_mixed")
     outgoing = call(
         last_partial_kernel,
         (shape((96, 128)),) * 4,
-        (place, *others, held_send, acc),
-        "partial_other_core",
-        smem,
-        [pltpu.VMEM((576, RANK), F32)],
+        (other3, held_send, acc),
+        "partial_last",
+        None,
+        [pltpu.VMEM((288, 2 * RANK), F32)],
     )
     over_x = sum([lax.ppermute(outgoing[d], "x", partners(4, d)) for d in (1, 2, 3)], outgoing[0])
-    over_z = sum([lax.ppermute(over_x, "z", partners(8, d)) for d in (2, 6, 4)], over_x)
-    z_other = lax.ppermute(over_z, "z", partners(8, 1))
+    over_z = sum([lax.ppermute(over_x, "z", partners(8, d)) for d in (1, 2, 3)], over_x)
+    z_other = lax.ppermute(over_z, "z", partners(8, 6))
     found, gram_link = call(
         interval_kernel,
         (shape((16, 128)), shape((RANK, RANK))),
-        (place, over_z, z_other, gram_day, day_twice),
+        (over_z, z_other, gram_day, day_twice),
         "interval_rows",
-        smem,
     )
     found = found + other_core(found)
     everyone = lax.all_to_all(jnp.broadcast_to(found[None], (16, 16, 128)), ("x", "y"), 0, 0)
     interval_new, day_new = call(
-        day_kernel, (shape((32, RANK)), shape((16, RANK))), (place, everyone, gram_link), "day_rows", smem
+        day_kernel, (shape((32, RANK)), shape((16, RANK))), (everyone, gram_link), "day_rows"
     )
     return link.T, interval_new, day_new
 

time: 85.6 us -> 80.5 us (0.940)
  Pallas kernels: 18.8 us -> 16.3 us
  waiting for transfers between devices: 24.8 us -> 23.2 us
    ppermute x3, starting transfers between devices: 8.2 us -> 4.81 us  [body(): lax.ppermute(over_x, 'z', partners(8, d))]
    ppermute x1, starting transfers between devices: 0.76 us -> 3.58 us  [body(): z_other = lax.ppermute(over_z, 'z', partners(8, 6))]
    pallas_call x10 -> x12, Pallas kernels: 18.8 us -> 16.3 us  [call(): pl.pallas_call(kernel, out_shape=out_shape, in_specs=[pl.BlockSpec(memory...]
    ppermute x8, waiting for transfers between devices: 14.7 us -> 12.8 us  [along_y(): return lax.ppermute(a, 'y', partners(4, d))]
  transfers between devices with their start and end apart: 21 -> 21, of which waited for: 13 -> 11; matrix products, arithmetic and copies ran while one was open for 0% -> 0% of each run, Pallas kernels for 8% -> 9%
where the time goes in v6:
time: 80.5 us; the launch traced here: 80.3 us
  starting transfers between devices  30.4 us (38%)
  waiting for transfers between devices  23.2 us (29%)
  Pallas kernels  16.3 us (20%)
  blocking collectives  9.62 us (12%)
    pallas_call x12, Pallas kernels, call(): pl.pallas_call(kernel, out_shape=out_shape, in_specs=[pl.BlockSpec(memory...  16.3 us
    ppermute x8, waiting for transfers between devices, along_y(): return lax.ppermute(a, 'y', partners(4, d))  12.8 us
    ppermute x6, starting transfers between devices, other_core(): return lax.ppermute(a, 'core', partners(2, 1))  9.94 us
    all_to_all x1, blocking collectives, body(): lax.all_to_all(jnp.broadcast_to(found[None], (16, 16, 128)), ('x', 'y'),...  9.62 us
    ppermute x8, starting transfers between devices, along_y(): return lax.ppermute(a, 'y', partners(4, d))  8.08 us
    ppermute x3, starting transfers between devices, body(): lax.ppermute(over_x, 'z', partners(8, d))  4.81 us
    ppermute x3, starting transfers between devices, body(): lax.ppermute(outgoing[d], 'x', partners(4, d))  3.95 us
    ppermute x3, waiting for transfers between devices, body(): lax.ppermute(over_x, 'z', partners(8, d))  3.84 us
  transfers between devices with their start and end apart: 21, of which 11 were waited for; matrix products, arithmetic and copies ran while one was open for 0% of the time, Pallas kernels for 9%

profile of v6, /device:TPU:1, one launch (start us, length us, event | category | flops | bytes accessed | tf_op | source)
XLA Modules:
  0.0 80.3 jit_solution(12228814500932207640)
XLA Ops:
  0.6 3.1 %sums_to_send.1 = (f32[264,1024]{1,0:T(8,128)S(1)}, bf16[4,512,1024]{2,1,0:T(8,128)(2,1)S(1)}, bf16[64,512]{1,0:T(8,128)(2,1)S(1)}, f32[16,128]{1,0:T(8,128)S(1)}) custom-call(bf16[512,8192]{1,0:T(8,128)(2,1)} %bitcast.2, f32[32,64]{1,0:T(8,128)} %interval_ref.1, f32[16,64]{1,0:T(8,128)} %day_ref.1), custom_call_target="tpu_custom_call" | custom-call | flops 1048576 | bytes 65536 | tf_op jit(solution)/shard_map/sums_to_send/pallas_call | solution.py:228
  3.7 3.3 %collective-permute-start = (f32[264,1024]{1,0:T(8,128)S(1)}, f32[264,1024]{1,0:T(8,128)S(1)}, u32[]{:S(2)}, u32[]{:S(2)}) collective-permute-start(f32[264,1024]{1,0:T(8,128)S(1)} %get-tuple-element.32.sent_ref), channel_id=1, source_target_pairs={{0,1},{1,0},{2,3},{3,2},{4,5},{5,4},{6,7},{7,6},{8,9},{9,8},{10,11... | collective-permute-start | bytes 3244040 | tf_op jit(solution)/shard_map/ppermute | solution.py:248
  7.0 2.5 %sums_to_keep.1 = (f32[4,64,1024]{2,1,0:T(8,128)S(1)}, bf16[4,512,1024]{2,1,0:T(8,128)(2,1)S(1)}) custom-call(bf16[512,8192]{1,0:T(8,128)(2,1)} %bitcast.3, bf16[64,512]{1,0:T(8,128)(2,1)S(1)} %get-tuple-element.30.khatri_ref), custom_call_target="tpu_custom_call" | custom-call | flops 1048576 | bytes 65536 | tf_op jit(solution)/shard_map/sums_to_keep/pallas_call | solution.py:228
  9.6 0.1 add_cores.1
  9.7 1.3 %collective-permute-start.1 = (f32[72,1024]{1,0:T(8,128)S(1)}, f32[72,1024]{1,0:T(8,128)S(1)}, u32[]{:S(2)}, u32[]{:S(2)}) collective-permute-start(f32[72,1024]{1,0:T(8,128)S(1)} %get-tuple-element.34), channel_id=1, source_target_pairs={{0,4},{2,6},{4,0},{6,2},{1,5},{3,7},{5,1},{7,3},{8,12},{10,14},{12... | collective-permute-start | bytes 884744 | tf_op jit(solution)/shard_map/ppermute | solution.py:251
  11.0 0.4 collective-permute-start.2
  11.3 1.7 %collective-permute-start.3 = (f32[72,512]{1,0:T(8,128)S(1)}, f32[72,512]{1,0:T(8,128)S(1)}, u32[]{:S(2)}, u32[]{:S(2)}) collective-permute-start(f32[72,512]{1,0:T(8,128)S(1)} %get-tuple-element.36), channel_id=1, source_target_pairs={{0,6},{2,4},{4,2},{6,0},{1,7},{3,5},{5,3},{7,1},{8,14},{10,12},{12... | collective-permute-start | bytes 442376 | tf_op jit(solution)/shard_map/ppermute | solution.py:251
  13.0 1.5 %collective-permute-start.5 = (f32[64,512]{1,0:T(8,128)S(1)}, f32[64,512]{1,0:T(8,128)S(1)}, u32[]{:S(2)}, u32[]{:S(2)}) collective-permute-start(f32[64,512]{1,0:T(8,128)S(1)} %get-tuple-element.38), channel_id=1, source_target_pairs={{0,6},{2,4},{4,2},{6,0},{1,7},{3,5},{5,3},{7,1},{8,14},{10,12},{12... | collective-permute-start | bytes 393224 | tf_op jit(solution)/shard_map/ppermute | solution.py:251
  14.5 7.0 %collective-permute-done.2.one.one_a = f32[72,512]{1,0:T(8,128)S(1)} collective-permute-done((f32[72,512]{1,0:T(8,128)S(1)}, f32[72,512]{1,0:T(8,128)S(1)}, u32[]{:S(2)}, u32[]{:S(2)}) %collective-permute-start.2) | collective-permute-done | bytes 147488 | tf_op jit(solution)/shard_map/ppermute | solution.py:251
  21.5 1.8 %collective-permute-done.3.three.three_a = f32[72,512]{1,0:T(8,128)S(1)} collective-permute-done((f32[72,512]{1,0:T(8,128)S(1)}, f32[72,512]{1,0:T(8,128)S(1)}, u32[]{:S(2)}, u32[]{:S(2)}) %collective-permute-start.3) | collective-permute-done | bytes 147488 | tf_op jit(solution)/shard_map/ppermute | solution.py:251
  23.4 1.8 %link_inverse.1 = (f32[64,64]{1,0:T(8,128)S(1)}, f32[64,64]{1,0:T(8,128)S(1)}) custom-call(f32[72,1024]{1,0:T(8,128)S(1)} %get-tuple-element.33.own, f32[72,1024]{1,0:T(8,128)S(1)} %collective-permute-done.1.two, f32[72,512]{1,0:T(8,128)S(1)} %collective-permute-done.2.one.one_a, f32[72,512]{1,0:T(8,128)S(1)} %collective-permute-done.3.three.three_a, ...), custom_call_target="tpu_custom_call" | custom-call | flops 1048576 | bytes 65536 | tf_op jit(solution)/shard_map/link_inverse/pallas_call | solution.py:228
  25.2 0.0 collective-permute-done.4.one_b
  25.2 1.0 %collective-permute-done.5.three_b = f32[64,512]{1,0:T(8,128)S(1)} collective-permute-done((f32[64,512]{1,0:T(8,128)S(1)}, f32[64,512]{1,0:T(8,128)S(1)}, u32[]{:S(2)}, u32[]{:S(2)}) %collective-permute-start.5) | collective-permute-done | bytes 131104 | tf_op jit(solution)/shard_map/ppermute | solution.py:251
  26.2 1.1 %link_rows.1 = (f32[64,1024]{1,0:T(8,128)}, bf16[64,1024]{1,0:T(8,128)(2,1)S(1)}) custom-call(f32[72,1024]{1,0:T(8,128)S(1)} %get-tuple-element.33.own, f32[72,1024]{1,0:T(8,128)S(1)} %collective-permute-done.1.two, f32[72,512]{1,0:T(8,128)S(1)} %collective-permute-done.2.one.one_a, f32[72,512]{1,0:T(8,128)S(1)} %collective-permute-done.3.three.three_a, ...), custom_call_target="tpu_custom_call" | custom-call | flops 1048576 | bytes 65536 | tf_op jit(solution)/shard_map/link_rows/pallas_call | solution.py:228
  27.3 0.5 collective-permute-start.9
  27.8 1.2 %collective-permute-start.8 = (bf16[64,1024]{1,0:T(8,128)(2,1)S(1)}, bf16[64,1024]{1,0:T(8,128)(2,1)S(1)}, u32[]{:S(2)}, u32[]{:S(2)}) collective-permute-start(bf16[64,1024]{1,0:T(8,128)(2,1)S(1)} %get-tuple-element.42.low), channel_id=1, source_target_pairs={{0,4},{2,6},{4,0},{6,2},{1,5},{3,7},{5,1},{7,3},{8,12},{10,14},{12... | collective-permute-start | bytes 393224 | tf_op jit(solution)/shard_map/ppermute | solution.py:251
  29.0 0.4 collective-permute-start.7
  29.3 1.7 %collective-permute-start.6 = (bf16[64,1024]{1,0:T(8,128)(2,1)S(1)}, bf16[64,1024]{1,0:T(8,128)(2,1)S(1)}, u32[]{:S(2)}, u32[]{:S(2)}) collective-permute-start(bf16[64,1024]{1,0:T(8,128)(2,1)S(1)} %get-tuple-element.42.low), channel_id=1, source_target_pairs={{0,6},{2,4},{4,2},{6,0},{1,7},{3,5},{5,3},{7,1},{8,14},{10,12},{12... | collective-permute-start | bytes 393224 | tf_op jit(solution)/shard_map/ppermute | solution.py:251
  31.0 0.8 partial_own.1.before
  31.8 2.6 %collective-permute-done.8.low = bf16[64,1024]{1,0:T(8,128)(2,1)S(1)} collective-permute-done((bf16[64,1024]{1,0:T(8,128)(2,1)S(1)}, bf16[64,1024]{1,0:T(8,128)(2,1)S(1)}, u32[]{:S(2)}, u32[]{:S(2)}) %collective-permute-start.8) | collective-permute-done | bytes 131104 | tf_op jit(solution)/shard_map/ppermute | solution.py:251
  34.4 1.2 %collective-permute-start.11 = (bf16[64,1024]{1,0:T(8,128)(2,1)S(1)}, bf16[64,1024]{1,0:T(8,128)(2,1)S(1)}, u32[]{:S(2)}, u32[]{:S(2)}) collective-permute-start(bf16[64,1024]{1,0:T(8,128)(2,1)S(1)} %collective-permute-done.8.low), channel_id=1, source_target_pairs={{0,1},{1,0},{2,3},{3,2},{4,5},{5,4},{6,7},{7,6},{8,9},{9,8},{10,11... | collective-permute-start | bytes 393224 | tf_op jit(solution)/shard_map/ppermute | solution.py:248
  35.6 0.5 partial_two.1.before
  36.1 0.5 collective-permute-start.12
  36.6 0.5 partial_one.1.before
  37.1 0.4 collective-permute-done.6.low3
  37.5 0.5 collective-permute-start.10
  38.0 1.1 %partial_mixed.1.before = f32[288,128]{1,0:T(8,128)S(1)} custom-call(bf16[64,1024]{1,0:T(8,128)(2,1)S(1)} %collective-permute-done.6.low3, bf16[64,1024]{1,0:T(8,128)(2,1)S(1)} %collective-permute-done.11.other2, bf16[64,1024]{1,0:T(8,128)(2,1)S(1)} %collective-permute-done.12.other1, bf16[4,512,1024]{2,1,0:T(8,128)(2,1)S(1)} %get-tuple-element.43.keep_ref, ...), custom_call_target="tpu_custom_call" | custom-call | flops 1048576 | bytes 65536 | tf_op jit(solution)/shard_map/partial_mixed/pallas_call | solution.py:228
  39.1 0.0 collective-permute-done.10.low
  39.1 0.5 partial_last.1
  39.6 0.9 %collective-permute-start.13 = (f32[96,128]{1,0:T(8,128)S(1)}, f32[96,128]{1,0:T(8,128)S(1)}, u32[]{:S(2)}, u32[]{:S(2)}) collective-permute-start(f32[96,128]{1,0:T(8,128)S(1)} %get-tuple-element.49), channel_id=1, source_target_pairs={{0,8},{8,0},{16,24},{24,16},{1,9},{9,1},{17,25},{25,17},{2,10},{10... | collective-permute-start | bytes 147464 | tf_op jit(solution)/shard_map/ppermute | solution.py:312
  40.5 2.5 %collective-permute-start.14 = (f32[96,128]{1,0:T(8,128)S(1)}, f32[96,128]{1,0:T(8,128)S(1)}, u32[]{:S(2)}, u32[]{:S(2)}) collective-permute-start(f32[96,128]{1,0:T(8,128)S(1)} %get-tuple-element.50), channel_id=1, source_target_pairs={{0,16},{8,24},{16,0},{24,8},{1,17},{9,25},{17,1},{25,9},{2,18},{10... | collective-permute-start | bytes 147464 | tf_op jit(solution)/shard_map/ppermute | solution.py:312
  42.9 0.6 collective-permute-start.15
  43.5 0.0 collective-permute-done.13
  43.5 1.7 %collective-permute-done.14 = f32[96,128]{1,0:T(8,128)S(1)} collective-permute-done((f32[96,128]{1,0:T(8,128)S(1)}, f32[96,128]{1,0:T(8,128)S(1)}, u32[]{:S(2)}, u32[]{:S(2)}) %collective-permute-start.14) | collective-permute-done | bytes 49184 | tf_op jit(solution)/shard_map/ppermute | solution.py:312
  45.2 1.9 %collective-permute-done.15 = f32[96,128]{1,0:T(8,128)S(1)} collective-permute-done((f32[96,128]{1,0:T(8,128)S(1)}, f32[96,128]{1,0:T(8,128)S(1)}, u32[]{:S(2)}, u32[]{:S(2)}) %collective-permute-start.15) | collective-permute-done | bytes 49184 | tf_op jit(solution)/shard_map/ppermute | solution.py:312
  47.1 4.4 %collective-permute-start.18 = (f32[96,128]{1,0:T(8,128)S(1)}, f32[96,128]{1,0:T(8,128)S(1)}, u32[]{:S(2)}, u32[]{:S(2)}) collective-permute-start(f32[96,128]{1,0:T(8,128)S(1)} %add_add_fusion.1), channel_id=1, source_target_pairs={{0,96},{32,64},{64,32},{96,0},{128,224},{160,192},{192,160},{224,1... | collective-permute-start | bytes 147464 | tf_op jit(solution)/shard_map/ppermute | solution.py:313
  51.5 0.0 collective-permute-start.17
  51.5 0.4 collective-permute-start.16
  51.9 1.1 %collective-permute-done.18 = f32[96,128]{1,0:T(8,128)S(1)} collective-permute-done((f32[96,128]{1,0:T(8,128)S(1)}, f32[96,128]{1,0:T(8,128)S(1)}, u32[]{:S(2)}, u32[]{:S(2)}) %collective-permute-start.18) | collective-permute-done | bytes 49184 | tf_op jit(solution)/shard_map/ppermute | solution.py:313
  53.0 2.7 %collective-permute-done.17 = f32[96,128]{1,0:T(8,128)S(1)} collective-permute-done((f32[96,128]{1,0:T(8,128)S(1)}, f32[96,128]{1,0:T(8,128)S(1)}, u32[]{:S(2)}, u32[]{:S(2)}) %collective-permute-start.17) | collective-permute-done | bytes 49184 | tf_op jit(solution)/shard_map/ppermute | solution.py:313
  55.8 0.0 collective-permute-done.16
  55.8 3.6 %collective-permute-start.19 = (f32[96,128]{1,0:T(8,128)S(1)}, f32[96,128]{1,0:T(8,128)S(1)}, u32[]{:S(2)}, u32[]{:S(2)}) collective-permute-start(f32[96,128]{1,0:T(8,128)S(1)} %add_add_fusion.total_ref), channel_id=1, source_target_pairs={{0,192},{32,224},{64,128},{96,160},{128,64},{160,96},{192,0},{224,... | collective-permute-start | bytes 147464 | tf_op jit(solution)/shard_map/ppermute | solution.py:314
  59.4 2.1 %collective-permute-done.19.other_ref = f32[96,128]{1,0:T(8,128)S(1)} collective-permute-done((f32[96,128]{1,0:T(8,128)S(1)}, f32[96,128]{1,0:T(8,128)S(1)}, u32[]{:S(2)}, u32[]{:S(2)}) %collective-permute-start.19) | collective-permute-done | bytes 49184 | tf_op jit(solution)/shard_map/ppermute | solution.py:314
  61.5 2.0 %interval_rows.1 = (f32[16,128]{1,0:T(8,128)S(1)}, f32[64,64]{1,0:T(8,128)S(1)}) custom-call(f32[96,128]{1,0:T(8,128)S(1)} %add_add_fusion.total_ref, f32[96,128]{1,0:T(8,128)S(1)} %collective-permute-done.19.other_ref, f32[64,64]{1,0:T(8,128)S(1)} %get-tuple-element.52.gram_day_ref, f32[16,128]{1,0:T(8,128)S(1)} %get-tuple-element.39.day_ref), custom_call_target="tpu_custom_call" | custom-call | flops 1048576 | bytes 65536 | tf_op jit(solution)/shard_map/interval_rows/pallas_call | solution.py:228
  63.5 3.9 %collective-permute-start.20 = (f32[16,128]{1,0:T(8,128)S(1)}, f32[16,128]{1,0:T(8,128)S(1)}, u32[]{:S(2)}, u32[]{:S(2)}) collective-permute-start(f32[16,128]{1,0:T(8,128)S(1)} %get-tuple-element.53), channel_id=1, source_target_pairs={{0,1},{1,0},{2,3},{3,2},{4,5},{5,4},{6,7},{7,6},{8,9},{9,8},{10,11... | collective-permute-start | bytes 24584 | tf_op jit(solution)/shard_map/ppermute | solution.py:248
  67.4 0.8 %collective-permute-done.20 = f32[16,128]{1,0:T(8,128)S(1)} collective-permute-done((f32[16,128]{1,0:T(8,128)S(1)}, f32[16,128]{1,0:T(8,128)S(1)}, u32[]{:S(2)}, u32[]{:S(2)}) %collective-permute-start.20) | collective-permute-done | bytes 8224 | tf_op jit(solution)/shard_map/ppermute | solution.py:248
  68.2 9.6 %all_to_all.5.recv_ref = f32[16,16,128]{2,1,0:T(8,128)S(1)} all-to-all(f32[16,16,128]{2,1,0:T(8,128)S(1)} %broadcast_in_dim.2), channel_id=1, replica_groups=mesh['z'=8,'x'=4,'y'=4,'core'=2] {'x','y'}, dimensions={0} | all-to-all | bytes 262144 | tf_op jit(solution)/shard_map/all_to_all | solution.py:322
  77.8 2.4 %day_rows.1 = (f32[32,64]{1,0:T(8,128)}, f32[16,64]{1,0:T(8,128)}) custom-call(f32[16,16,128]{2,1,0:T(8,128)S(1)} %all_to_all.5.recv_ref, f32[64,64]{1,0:T(8,128)S(1)} %get-tuple-element.54.gram_ref), custom_call_target="tpu_custom_call" | custom-call | flops 1048576 | bytes 65536 | tf_op jit(solution)/shard_map/day_rows/pallas_call | solution.py:228
  (11 shorter events, 0.1 us)
Async XLA Ops:
  3.7 5.9 %collective-permute-start = (f32[264,1024]{1,0:T(8,128)S(1)}, f32[264,1024]{1,0:T(8,128)S(1)}, u32[]{:S(2)}, u32[]{:S(2)}) collective-permute-start(f32[264,1024]{1,0:T(8,128)S(1)} %get-tuple-element.32.sent_ref), channel_id=1, source_target_pairs={{0,1},{1,0},{2,3},{3,2},{4,5},{5,4},{6,7},{7,6},{8,9},{9,8},{10,11... | collective-permute-start | bytes 3244040 | tf_op jit(solution)/shard_map/ppermute | solution.py:248
  9.7 13.7 %collective-permute-start.1 = (f32[72,1024]{1,0:T(8,128)S(1)}, f32[72,1024]{1,0:T(8,128)S(1)}, u32[]{:S(2)}, u32[]{:S(2)}) collective-permute-start(f32[72,1024]{1,0:T(8,128)S(1)} %get-tuple-element.34), channel_id=1, source_target_pairs={{0,4},{2,6},{4,0},{6,2},{1,5},{3,7},{5,1},{7,3},{8,12},{10,14},{12... | collective-permute-start | bytes 884744 | tf_op jit(solution)/shard_map/ppermute | solution.py:251
  11.0 10.6 %collective-permute-start.2 = (f32[72,512]{1,0:T(8,128)S(1)}, f32[72,512]{1,0:T(8,128)S(1)}, u32[]{:S(2)}, u32[]{:S(2)}) collective-permute-start(f32[72,512]{1,0:T(8,128)S(1)} %get-tuple-element.35), channel_id=1, source_target_pairs={{0,2},{2,0},{4,6},{6,4},{1,3},{3,1},{5,7},{7,5},{8,10},{10,8},{12,... | collective-permute-start | bytes 442376 | tf_op jit(solution)/shard_map/ppermute | solution.py:251
  11.3 12.0 %collective-permute-start.3 = (f32[72,512]{1,0:T(8,128)S(1)}, f32[72,512]{1,0:T(8,128)S(1)}, u32[]{:S(2)}, u32[]{:S(2)}) collective-permute-start(f32[72,512]{1,0:T(8,128)S(1)} %get-tuple-element.36), channel_id=1, source_target_pairs={{0,6},{2,4},{4,2},{6,0},{1,7},{3,5},{5,3},{7,1},{8,14},{10,12},{12... | collective-permute-start | bytes 442376 | tf_op jit(solution)/shard_map/ppermute | solution.py:251
  13.0 12.2 %collective-permute-start.4 = (f32[64,512]{1,0:T(8,128)S(1)}, f32[64,512]{1,0:T(8,128)S(1)}, u32[]{:S(2)}, u32[]{:S(2)}) collective-permute-start(f32[64,512]{1,0:T(8,128)S(1)} %get-tuple-element.37), channel_id=1, source_target_pairs={{0,2},{2,0},{4,6},{6,4},{1,3},{3,1},{5,7},{7,5},{8,10},{10,8},{12,... | collective-permute-start | bytes 393224 | tf_op jit(solution)/shard_map/ppermute | solution.py:251
  13.0 13.1 %collective-permute-start.5 = (f32[64,512]{1,0:T(8,128)S(1)}, f32[64,512]{1,0:T(8,128)S(1)}, u32[]{:S(2)}, u32[]{:S(2)}) collective-permute-start(f32[64,512]{1,0:T(8,128)S(1)} %get-tuple-element.38), channel_id=1, source_target_pairs={{0,6},{2,4},{4,2},{6,0},{1,7},{3,5},{5,3},{7,1},{8,14},{10,12},{12... | collective-permute-start | bytes 393224 | tf_op jit(solution)/shard_map/ppermute | solution.py:251
  27.3 3.8 %collective-permute-start.9 = (bf16[64,1024]{1,0:T(8,128)(2,1)S(1)}, bf16[64,1024]{1,0:T(8,128)(2,1)S(1)}, u32[]{:S(2)}, u32[]{:S(2)}) collective-permute-start(bf16[64,1024]{1,0:T(8,128)(2,1)S(1)} %get-tuple-element.42.low), channel_id=1, source_target_pairs={{0,1},{1,0},{2,3},{3,2},{4,5},{5,4},{6,7},{7,6},{8,9},{9,8},{10,11... | collective-permute-start | bytes 393224 | tf_op jit(solution)/shard_map/ppermute | solution.py:248
  27.8 6.6 %collective-permute-start.8 = (bf16[64,1024]{1,0:T(8,128)(2,1)S(1)}, bf16[64,1024]{1,0:T(8,128)(2,1)S(1)}, u32[]{:S(2)}, u32[]{:S(2)}) collective-permute-start(bf16[64,1024]{1,0:T(8,128)(2,1)S(1)} %get-tuple-element.42.low), channel_id=1, source_target_pairs={{0,4},{2,6},{4,0},{6,2},{1,5},{3,7},{5,1},{7,3},{8,12},{10,14},{12... | collective-permute-start | bytes 393224 | tf_op jit(solution)/shard_map/ppermute | solution.py:251
  29.0 7.1 %collective-permute-start.7 = (bf16[64,1024]{1,0:T(8,128)(2,1)S(1)}, bf16[64,1024]{1,0:T(8,128)(2,1)S(1)}, u32[]{:S(2)}, u32[]{:S(2)}) collective-permute-start(bf16[64,1024]{1,0:T(8,128)(2,1)S(1)} %get-tuple-element.42.low), channel_id=1, source_target_pairs={{0,2},{2,0},{4,6},{6,4},{1,3},{3,1},{5,7},{7,5},{8,10},{10,8},{12,... | collective-permute-start | bytes 393224 | tf_op jit(solution)/shard_map/ppermute | solution.py:251
  29.3 8.2 %collective-permute-start.6 = (bf16[64,1024]{1,0:T(8,128)(2,1)S(1)}, bf16[64,1024]{1,0:T(8,128)(2,1)S(1)}, u32[]{:S(2)}, u32[]{:S(2)}) collective-permute-start(bf16[64,1024]{1,0:T(8,128)(2,1)S(1)} %get-tuple-element.42.low), channel_id=1, source_target_pairs={{0,6},{2,4},{4,2},{6,0},{1,7},{3,5},{5,3},{7,1},{8,14},{10,12},{12... | collective-permute-start | bytes 393224 | tf_op jit(solution)/shard_map/ppermute | solution.py:251
  34.4 3.6 %collective-permute-start.11 = (bf16[64,1024]{1,0:T(8,128)(2,1)S(1)}, bf16[64,1024]{1,0:T(8,128)(2,1)S(1)}, u32[]{:S(2)}, u32[]{:S(2)}) collective-permute-start(bf16[64,1024]{1,0:T(8,128)(2,1)S(1)} %collective-permute-done.8.low), channel_id=1, source_target_pairs={{0,1},{1,0},{2,3},{3,2},{4,5},{5,4},{6,7},{7,6},{8,9},{9,8},{10,11... | collective-permute-start | bytes 393224 | tf_op jit(solution)/shard_map/ppermute | solution.py:248
  36.1 1.9 %collective-permute-start.12 = (bf16[64,1024]{1,0:T(8,128)(2,1)S(1)}, bf16[64,1024]{1,0:T(8,128)(2,1)S(1)}, u32[]{:S(2)}, u32[]{:S(2)}) collective-permute-start(bf16[64,1024]{1,0:T(8,128)(2,1)S(1)} %collective-permute-done.7.low), channel_id=1, source_target_pairs={{0,1},{1,0},{2,3},{3,2},{4,5},{5,4},{6,7},{7,6},{8,9},{9,8},{10,11... | collective-permute-start | bytes 393224 | tf_op jit(solution)/shard_map/ppermute | solution.py:248
  37.5 1.6 %collective-permute-start.10 = (bf16[64,1024]{1,0:T(8,128)(2,1)S(1)}, bf16[64,1024]{1,0:T(8,128)(2,1)S(1)}, u32[]{:S(2)}, u32[]{:S(2)}) collective-permute-start(bf16[64,1024]{1,0:T(8,128)(2,1)S(1)} %collective-permute-done.6.low3), channel_id=1, source_target_pairs={{0,1},{1,0},{2,3},{3,2},{4,5},{5,4},{6,7},{7,6},{8,9},{9,8},{10,11... | collective-permute-start | bytes 393224 | tf_op jit(solution)/shard_map/ppermute | solution.py:248
  39.6 3.9 %collective-permute-start.13 = (f32[96,128]{1,0:T(8,128)S(1)}, f32[96,128]{1,0:T(8,128)S(1)}, u32[]{:S(2)}, u32[]{:S(2)}) collective-permute-start(f32[96,128]{1,0:T(8,128)S(1)} %get-tuple-element.49), channel_id=1, source_target_pairs={{0,8},{8,0},{16,24},{24,16},{1,9},{9,1},{17,25},{25,17},{2,10},{10... | collective-permute-start | bytes 147464 | tf_op jit(solution)/shard_map/ppermute | solution.py:312
  40.5 4.8 %collective-permute-start.14 = (f32[96,128]{1,0:T(8,128)S(1)}, f32[96,128]{1,0:T(8,128)S(1)}, u32[]{:S(2)}, u32[]{:S(2)}) collective-permute-start(f32[96,128]{1,0:T(8,128)S(1)} %get-tuple-element.50), channel_id=1, source_target_pairs={{0,16},{8,24},{16,0},{24,8},{1,17},{9,25},{17,1},{25,9},{2,18},{10... | collective-permute-start | bytes 147464 | tf_op jit(solution)/shard_map/ppermute | solution.py:312
  42.9 4.2 %collective-permute-start.15 = (f32[96,128]{1,0:T(8,128)S(1)}, f32[96,128]{1,0:T(8,128)S(1)}, u32[]{:S(2)}, u32[]{:S(2)}) collective-permute-start(f32[96,128]{1,0:T(8,128)S(1)} %get-tuple-element.51), channel_id=1, source_target_pairs={{0,24},{8,16},{16,8},{24,0},{1,25},{9,17},{17,9},{25,1},{2,26},{10... | collective-permute-start | bytes 147464 | tf_op jit(solution)/shard_map/ppermute | solution.py:312
  47.1 5.9 %collective-permute-start.18 = (f32[96,128]{1,0:T(8,128)S(1)}, f32[96,128]{1,0:T(8,128)S(1)}, u32[]{:S(2)}, u32[]{:S(2)}) collective-permute-start(f32[96,128]{1,0:T(8,128)S(1)} %add_add_fusion.1), channel_id=1, source_target_pairs={{0,96},{32,64},{64,32},{96,0},{128,224},{160,192},{192,160},{224,1... | collective-permute-start | bytes 147464 | tf_op jit(solution)/shard_map/ppermute | solution.py:313
  51.5 4.2 %collective-permute-start.17 = (f32[96,128]{1,0:T(8,128)S(1)}, f32[96,128]{1,0:T(8,128)S(1)}, u32[]{:S(2)}, u32[]{:S(2)}) collective-permute-start(f32[96,128]{1,0:T(8,128)S(1)} %add_add_fusion.1), channel_id=1, source_target_pairs={{0,64},{32,96},{64,0},{96,32},{128,192},{160,224},{192,128},{224,1... | collective-permute-start | bytes 147464 | tf_op jit(solution)/shard_map/ppermute | solution.py:313
  51.5 4.2 %collective-permute-start.16 = (f32[96,128]{1,0:T(8,128)S(1)}, f32[96,128]{1,0:T(8,128)S(1)}, u32[]{:S(2)}, u32[]{:S(2)}) collective-permute-start(f32[96,128]{1,0:T(8,128)S(1)} %add_add_fusion.1), channel_id=1, source_target_pairs={{0,32},{32,0},{64,96},{96,64},{128,160},{160,128},{192,224},{224,1... | collective-permute-start | bytes 147464 | tf_op jit(solution)/shard_map/ppermute | solution.py:313
  55.8 5.7 %collective-permute-start.19 = (f32[96,128]{1,0:T(8,128)S(1)}, f32[96,128]{1,0:T(8,128)S(1)}, u32[]{:S(2)}, u32[]{:S(2)}) collective-permute-start(f32[96,128]{1,0:T(8,128)S(1)} %add_add_fusion.total_ref), channel_id=1, source_target_pairs={{0,192},{32,224},{64,128},{96,160},{128,64},{160,96},{192,0},{224,... | collective-permute-start | bytes 147464 | tf_op jit(solution)/shard_map/ppermute | solution.py:314
  63.5 4.7 %collective-permute-start.20 = (f32[16,128]{1,0:T(8,128)S(1)}, f32[16,128]{1,0:T(8,128)S(1)}, u32[]{:S(2)}, u32[]{:S(2)}) collective-permute-start(f32[16,128]{1,0:T(8,128)S(1)} %get-tuple-element.53), channel_id=1, source_target_pairs={{0,1},{1,0},{2,3},{3,2},{4,5},{5,4},{6,7},{7,6},{8,9},{9,8},{10,11... | collective-permute-start | bytes 24584 | tf_op jit(solution)/shard_map/ppermute | solution.py:248

commit v7 on v6

--- a/solution.py
+++ b/solution.py
@@ -107,16 +107,18 @@
     return jnp.concatenate([packed[:, :RANK], packed[:, RANK:]], axis=0)
 
 
-def add_kernel(keep_ref, sent_ref, got_ref, own, two, one_a, three_a, one_b, three_b):
-    factor = jnp.concatenate([sent_ref[4 * RANK :, : 4 * RANK], got_ref[4 * RANK :, : 4 * RANK]], axis=1)
+def add_kernel(keep_ref, sent_ref, got_ref, own, factor_ref, two, one_a, three_a, one_b, three_b):
+    factors = [ref[4 * RANK :, : 4 * RANK] for ref in (sent_ref, got_ref)]
+    factor = jnp.concatenate(factors, axis=1)
+    factor_ref[...] = factor
 
     def total(d, lanes):
         return keep_ref[d, :, lanes] + got_ref[d * RANK : (d + 1) * RANK, lanes]
 
-    for d, out in ((0, own), (2, two)):
-        out[:RANK] = total(d, slice(0, 1024))
-        out[RANK:, : 8 * RANK] = factor
-        out[RANK:, 8 * RANK :] = jnp.zeros((8, 1024 - 8 * RANK), F32)
+    own[...] = total(0, slice(0, 1024))
+    for i in range(8):
+        two[i * RANK : (i + 1) * RANK] = total(2, slice(i * 128, (i + 1) * 128))
+    two[8 * RANK :] = jnp.concatenate([from_lanes(rows) for rows in factors], axis=1)
     for d, first, second in ((1, one_a, one_b), (3, three_a, three_b)):
         first[:RANK] = total(d, slice(0, HALF))
         first[RANK:] = factor
@@ -127,17 +129,25 @@
     day = day_ref[:, :RANK]
     gram_day = dot(day, day, ((0,), (0,)))
     gram_day_ref[...] = gram_day
-    wide = (own[RANK:, :HALF], two[RANK:, :HALF], one[RANK:], three[RANK:])
-    factor = jnp.concatenate([from_lanes(rows) for rows in wide], axis=0)
+    wide = (own[...], one[RANK:], three[RANK:])
+    factor = jnp.concatenate([unpack(two[8 * RANK :])] + [from_lanes(rows) for rows in wide], axis=0)
     inverse_ref[...] = inverse_of(dot(factor, factor, ((0,), (0,))) * gram_day)
 
 
-def link_kernel(own, two, one_a, three_a, one_b, three_b, inverse_ref, link_ref, low_ref):
-    first = (own[:RANK, :HALF] + two[:RANK, :HALF]) + (one_a[:RANK] + three_a[:RANK])
-    second = (own[:RANK, HALF:] + two[:RANK, HALF:]) + (one_b[...] + three_b[...])
-    link = dot(inverse_ref[...], jnp.concatenate([first, second], axis=1))
-    link_ref[...] = link
-    low_ref[...] = link.astype(BF16)
+def link_kernel(own, two, one_a, three_a, one_b, inverse_ref, link_ref):
+    lanes = jnp.concatenate([two[at : at + RANK] for at in range(0, 8 * RANK, RANK)], axis=1)
+    first = (own[:, :HALF] + lanes[:, :HALF]) + (one_a[:RANK] + three_a[:RANK])
+    second = (own[:, HALF:] + lanes[:, HALF:]) + one_b[...]
+    link_ref[...] = dot(inverse_ref[...], jnp.concatenate([first, second], axis=1))
+
+
+def last_link_kernel(before, three_b, inverse_ref, link_ref, low_ref):
+    first = before[:, :HALF]
+    second = before[:, HALF:] + dot(inverse_ref[...], three_b[...])
+    link_ref[:, :HALF] = first
+    link_ref[:, HALF:] = second
+    low_ref[:, :HALF] = first.astype(BF16)
+    low_ref[:, HALF:] = second.astype(BF16)
 
 
 def times_blocks(lows, held_ref, blocks):
@@ -154,7 +164,8 @@
     return total
 
 
-def first_partial_kernel(low, low_other, keep_ref, send_ref, acc):
+def first_partial_kernel(low, low_other, keep_ref, send_ref, link_ref, acc, link_out):
+    link_out[...] = link_ref[...]
     acc[...] = times_blocks((low,), keep_ref, (0,)) + times_blocks((low_other,), send_ref, (0,))
 
 
@@ -272,18 +283,30 @@
         {0: pl.ANY},
         [pltpu.SemaphoreType.DMA((4,))],
     )
-    sums = call(
+    own, factor, two, one_a, three_a, one_b, three_b = call(
         add_kernel,
-        (shape((72, 1024)),) * 2 + (shape((72, HALF)),) * 2 + (shape((RANK, HALF)),) * 2,
+        (
+            shape((RANK, 1024)),
+            shape((8, HALF)),
+            shape((8 * RANK + 32, 128)),
+            shape((72, HALF)),
+            shape((72, HALF)),
+            shape((RANK, HALF)),
+            shape((RANK, HALF)),
+        ),
         (keep, send, got),
         "add_cores",
     )
-    parts = [sums[0]] + [along_y(one, d) for one, d in zip(sums[1:], (2, 1, 3, 1, 3))]
+    two, one_a, three_a = along_y(two, 2), along_y(one_a, 1), along_y(three_a, 3)
+    one_b, three_b = along_y(one_b, 1), along_y(three_b, 3)
     inverse, gram_day = call(
-        inverse_kernel, (shape((RANK, RANK)),) * 2, (*parts[:4], day_twice), "link_inverse"
+        inverse_kernel, (shape((RANK, RANK)),) * 2, (factor, two, one_a, three_a, day_twice), "link_inverse"
+    )
+    link = call(
+        link_kernel, shape((RANK, 1024)), (own, two, one_a, three_a, one_b, inverse), "most_of_link_rows"
     )
     link, low = call(
-        link_kernel, (shape((RANK, 1024)), shape((RANK, 1024), BF16)), (*parts, inverse), "link_rows"
+        last_link_kernel, (shape((RANK, 1024)), shape((RANK, 1024), BF16)), (link, three_b, inverse), "link_rows"
     )
     low2, low3, low1 = [along_y(low, d) for d in (2, 3, 1)]
     total = shape((288, 2 * RANK))
@@ -291,7 +314,12 @@
     def after(one, acc):
         return lax.optimization_barrier((one, acc))[0]
 
-    acc = call(first_partial_kernel, total, (low, other_core(low), held_keep, held_send), "partial_own")
+    acc, link = call(
+        first_partial_kernel,
+        (total, shape((RANK, 1024))),
+        (low, other_core(low), held_keep, held_send, link),
+        "partial_own",
+    )
     low2 = after(low2, acc)
     other2 = other_core(low2)
     acc = call(functools.partial(one_partial_kernel, 2), total, (low2, held_keep, acc), "partial_two")

time: 80.5 us -> 79.8 us (level)
  waiting for transfers between devices: 23.2 us -> 21.7 us
    ppermute x8, waiting for transfers between devices: 12.8 us -> 11.4 us  [along_y(): return lax.ppermute(a, 'y', partners(4, d))]
    pallas_call x12 -> x13, Pallas kernels: 16.3 us -> 16.6 us  [call(): pl.pallas_call(kernel, out_shape=out_shape, in_specs=[pl.BlockSpec(memory...]
  transfers between devices with their start and end apart: 21 -> 21, of which waited for: 11 -> 11; matrix products, arithmetic and copies ran while one was open for 0% -> 0% of each run, Pallas kernels for 9% -> 10%
where the time goes in v7:
time: 79.8 us; the launch traced here: 79.6 us
  starting transfers between devices  30.5 us (38%)
  waiting for transfers between devices  21.7 us (27%)
  Pallas kernels  16.6 us (21%)
  blocking collectives  10 us (13%)
    pallas_call x13, Pallas kernels, call(): pl.pallas_call(kernel, out_shape=out_shape, in_specs=[pl.BlockSpec(memory...  16.6 us
    ppermute x8, waiting for transfers between devices, along_y(): return lax.ppermute(a, 'y', partners(4, d))  11.4 us
    ppermute x6, starting transfers between devices, other_core(): return lax.ppermute(a, 'core', partners(2, 1))  10.1 us
    all_to_all x1, blocking collectives, body(): lax.all_to_all(jnp.broadcast_to(found[None], (16, 16, 128)), ('x', 'y'),...  10 us
    ppermute x8, starting transfers between devices, along_y(): return lax.ppermute(a, 'y', partners(4, d))  8.1 us
    ppermute x3, starting transfers between devices, body(): lax.ppermute(over_x, 'z', partners(8, d))  4.81 us
    ppermute x3, starting transfers between devices, body(): lax.ppermute(outgoing[d], 'x', partners(4, d))  3.95 us
    ppermute x3, waiting for transfers between devices, body(): lax.ppermute(over_x, 'z', partners(8, d))  3.84 us
  transfers between devices with their start and end apart: 21, of which 11 were waited for; matrix products, arithmetic and copies ran while one was open for 0% of the time, Pallas kernels for 10%

profile of v7, /device:TPU:1, one launch (start us, length us, event | category | flops | bytes accessed | tf_op | source)
XLA Modules:
  0.0 79.6 jit_solution(13985076475674530540)
XLA Ops:
  0.6 3.1 %sums_to_send.1 = (f32[264,1024]{1,0:T(8,128)S(1)}, bf16[4,512,1024]{2,1,0:T(8,128)(2,1)S(1)}, bf16[64,512]{1,0:T(8,128)(2,1)S(1)}, f32[16,128]{1,0:T(8,128)S(1)}) custom-call(bf16[512,8192]{1,0:T(8,128)(2,1)} %bitcast.2, f32[32,64]{1,0:T(8,128)} %interval_ref.1, f32[16,64]{1,0:T(8,128)} %day_ref.1), custom_call_target="tpu_custom_call" | custom-call | flops 1048576 | bytes 65536 | tf_op jit(solution)/shard_map/sums_to_send/pallas_call | solution.py:239
  3.7 3.3 %collective-permute-start = (f32[264,1024]{1,0:T(8,128)S(1)}, f32[264,1024]{1,0:T(8,128)S(1)}, u32[]{:S(2)}, u32[]{:S(2)}) collective-permute-start(f32[264,1024]{1,0:T(8,128)S(1)} %get-tuple-element.35.sent_ref), channel_id=1, source_target_pairs={{0,1},{1,0},{2,3},{3,2},{4,5},{5,4},{6,7},{7,6},{8,9},{9,8},{10,11... | collective-permute-start | bytes 3244040 | tf_op jit(solution)/shard_map/ppermute | solution.py:259
  7.0 2.5 %sums_to_keep.1 = (f32[4,64,1024]{2,1,0:T(8,128)S(1)}, bf16[4,512,1024]{2,1,0:T(8,128)(2,1)S(1)}) custom-call(bf16[512,8192]{1,0:T(8,128)(2,1)} %bitcast.3, bf16[64,512]{1,0:T(8,128)(2,1)S(1)} %get-tuple-element.33.khatri_ref), custom_call_target="tpu_custom_call" | custom-call | flops 1048576 | bytes 65536 | tf_op jit(solution)/shard_map/sums_to_keep/pallas_call | solution.py:239
  9.6 0.2 add_cores.1
  9.7 1.3 %collective-permute-start.1 = (f32[544,128]{1,0:T(8,128)S(1)}, f32[544,128]{1,0:T(8,128)S(1)}, u32[]{:S(2)}, u32[]{:S(2)}) collective-permute-start(f32[544,128]{1,0:T(8,128)S(1)} %get-tuple-element.37), channel_id=1, source_target_pairs={{0,4},{2,6},{4,0},{6,2},{1,5},{3,7},{5,1},{7,3},{8,12},{10,14},{12... | collective-permute-start | bytes 835592 | tf_op jit(solution)/shard_map/ppermute | solution.py:262
  11.0 0.4 collective-permute-start.2
  11.4 1.7 %collective-permute-start.3 = (f32[72,512]{1,0:T(8,128)S(1)}, f32[72,512]{1,0:T(8,128)S(1)}, u32[]{:S(2)}, u32[]{:S(2)}) collective-permute-start(f32[72,512]{1,0:T(8,128)S(1)} %get-tuple-element.39), channel_id=1, source_target_pairs={{0,6},{2,4},{4,2},{6,0},{1,7},{3,5},{5,3},{7,1},{8,14},{10,12},{12... | collective-permute-start | bytes 442376 | tf_op jit(solution)/shard_map/ppermute | solution.py:262
  13.1 0.0 collective-permute-start.4
  13.1 1.5 %collective-permute-start.5 = (f32[64,512]{1,0:T(8,128)S(1)}, f32[64,512]{1,0:T(8,128)S(1)}, u32[]{:S(2)}, u32[]{:S(2)}) collective-permute-start(f32[64,512]{1,0:T(8,128)S(1)} %get-tuple-element.44), channel_id=1, source_target_pairs={{0,6},{2,4},{4,2},{6,0},{1,7},{3,5},{5,3},{7,1},{8,14},{10,12},{12... | collective-permute-start | bytes 393224 | tf_op jit(solution)/shard_map/ppermute | solution.py:262
  14.6 6.7 %collective-permute-done.2.one.one_a = f32[72,512]{1,0:T(8,128)S(1)} collective-permute-done((f32[72,512]{1,0:T(8,128)S(1)}, f32[72,512]{1,0:T(8,128)S(1)}, u32[]{:S(2)}, u32[]{:S(2)}) %collective-permute-start.2) | collective-permute-done | bytes 147488 | tf_op jit(solution)/shard_map/ppermute | solution.py:262
  21.2 1.8 %collective-permute-done.3.three.three_a = f32[72,512]{1,0:T(8,128)S(1)} collective-permute-done((f32[72,512]{1,0:T(8,128)S(1)}, f32[72,512]{1,0:T(8,128)S(1)}, u32[]{:S(2)}, u32[]{:S(2)}) %collective-permute-start.3) | collective-permute-done | bytes 147488 | tf_op jit(solution)/shard_map/ppermute | solution.py:262
  23.1 1.8 %link_inverse.1 = (f32[64,64]{1,0:T(8,128)S(1)}, f32[64,64]{1,0:T(8,128)S(1)}) custom-call(f32[8,512]{1,0:T(8,128)S(1)} %get-tuple-element.41.own, f32[544,128]{1,0:T(8,128)S(1)} %collective-permute-done.1.two, f32[72,512]{1,0:T(8,128)S(1)} %collective-permute-done.2.one.one_a, f32[72,512]{1,0:T(8,128)S(1)} %collective-permute-done.3.three.three_a, ...), custom_call_target="tpu_custom_call" | custom-call | flops 1048576 | bytes 65536 | tf_op jit(solution)/shard_map/link_inverse/pallas_call | solution.py:239
  24.9 0.0 collective-permute-done.4.one_b
  24.9 0.4 most_of_link_rows.1.before
  25.3 0.6 collective-permute-done.5.three_b
  25.9 0.3 link_rows.1
  26.1 0.6 collective-permute-start.6
  26.7 1.2 %collective-permute-start.9 = (bf16[64,1024]{1,0:T(8,128)(2,1)S(1)}, bf16[64,1024]{1,0:T(8,128)(2,1)S(1)}, u32[]{:S(2)}, u32[]{:S(2)}) collective-permute-start(bf16[64,1024]{1,0:T(8,128)(2,1)S(1)} %get-tuple-element.45.low), channel_id=1, source_target_pairs={{0,4},{2,6},{4,0},{6,2},{1,5},{3,7},{5,1},{7,3},{8,12},{10,14},{12... | collective-permute-start | bytes 393224 | tf_op jit(solution)/shard_map/ppermute | solution.py:262
  27.9 0.4 collective-permute-start.8
  28.3 1.7 %collective-permute-start.7 = (bf16[64,1024]{1,0:T(8,128)(2,1)S(1)}, bf16[64,1024]{1,0:T(8,128)(2,1)S(1)}, u32[]{:S(2)}, u32[]{:S(2)}) collective-permute-start(bf16[64,1024]{1,0:T(8,128)(2,1)S(1)} %get-tuple-element.45.low), channel_id=1, source_target_pairs={{0,6},{2,4},{4,2},{6,0},{1,7},{3,5},{5,3},{7,1},{8,14},{10,12},{12... | collective-permute-start | bytes 393224 | tf_op jit(solution)/shard_map/ppermute | solution.py:262
  30.0 0.0 collective-permute-done.6.low_other
  30.0 1.4 %partial_own.1 = (f32[288,128]{1,0:T(8,128)S(1)}, f32[64,1024]{1,0:T(8,128)}) custom-call(bf16[64,1024]{1,0:T(8,128)(2,1)S(1)} %get-tuple-element.45.low, bf16[64,1024]{1,0:T(8,128)(2,1)S(1)} %collective-permute-done.6.low_other, bf16[4,512,1024]{2,1,0:T(8,128)(2,1)S(1)} %get-tuple-element.46.keep_ref, bf16[4,512,1024]{2,1,0:T(8,128)(2,1)S(1)} %get-tuple-element.47.send_ref, ...), custom_call_target="tpu_custom_call" | custom-call | flops 1048576 | bytes 65536 | tf_op jit(solution)/shard_map/partial_own/pallas_call | solution.py:239
  31.4 1.9 %collective-permute-done.9.low = bf16[64,1024]{1,0:T(8,128)(2,1)S(1)} collective-permute-done((bf16[64,1024]{1,0:T(8,128)(2,1)S(1)}, bf16[64,1024]{1,0:T(8,128)(2,1)S(1)}, u32[]{:S(2)}, u32[]{:S(2)}) %collective-permute-start.9) | collective-permute-done | bytes 131104 | tf_op jit(solution)/shard_map/ppermute | solution.py:262
  33.3 1.3 %collective-permute-start.11 = (bf16[64,1024]{1,0:T(8,128)(2,1)S(1)}, bf16[64,1024]{1,0:T(8,128)(2,1)S(1)}, u32[]{:S(2)}, u32[]{:S(2)}) collective-permute-start(bf16[64,1024]{1,0:T(8,128)(2,1)S(1)} %collective-permute-done.9.low), channel_id=1, source_target_pairs={{0,1},{1,0},{2,3},{3,2},{4,5},{5,4},{6,7},{7,6},{8,9},{9,8},{10,11... | collective-permute-start | bytes 393224 | tf_op jit(solution)/shard_map/ppermute | solution.py:259
  34.6 0.5 partial_two.1.before
  35.1 0.5 collective-permute-start.12
  35.6 0.5 partial_one.1.before
  36.0 0.4 collective-permute-done.7.low3
  36.5 0.5 collective-permute-start.10
  37.0 0.0 collective-permute-done.12.other1
  37.0 1.1 %partial_mixed.1.before = f32[288,128]{1,0:T(8,128)S(1)} custom-call(bf16[64,1024]{1,0:T(8,128)(2,1)S(1)} %collective-permute-done.7.low3, bf16[64,1024]{1,0:T(8,128)(2,1)S(1)} %collective-permute-done.11.other2, bf16[64,1024]{1,0:T(8,128)(2,1)S(1)} %collective-permute-done.12.other1, bf16[4,512,1024]{2,1,0:T(8,128)(2,1)S(1)} %get-tuple-element.46.keep_ref, ...), custom_call_target="tpu_custom_call" | custom-call | flops 1048576 | bytes 65536 | tf_op jit(solution)/shard_map/partial_mixed/pallas_call | solution.py:239
  38.0 0.5 partial_last.1
  38.5 0.9 %collective-permute-start.13 = (f32[96,128]{1,0:T(8,128)S(1)}, f32[96,128]{1,0:T(8,128)S(1)}, u32[]{:S(2)}, u32[]{:S(2)}) collective-permute-start(f32[96,128]{1,0:T(8,128)S(1)} %get-tuple-element.55), channel_id=1, source_target_pairs={{0,8},{8,0},{16,24},{24,16},{1,9},{9,1},{17,25},{25,17},{2,10},{10... | collective-permute-start | bytes 147464 | tf_op jit(solution)/shard_map/ppermute | solution.py:340
  39.4 2.5 %collective-permute-start.14 = (f32[96,128]{1,0:T(8,128)S(1)}, f32[96,128]{1,0:T(8,128)S(1)}, u32[]{:S(2)}, u32[]{:S(2)}) collective-permute-start(f32[96,128]{1,0:T(8,128)S(1)} %get-tuple-element.56), channel_id=1, source_target_pairs={{0,16},{8,24},{16,0},{24,8},{1,17},{9,25},{17,1},{25,9},{2,18},{10... | collective-permute-start | bytes 147464 | tf_op jit(solution)/shard_map/ppermute | solution.py:340
  41.9 0.6 collective-permute-start.15
  42.5 1.7 %collective-permute-done.14 = f32[96,128]{1,0:T(8,128)S(1)} collective-permute-done((f32[96,128]{1,0:T(8,128)S(1)}, f32[96,128]{1,0:T(8,128)S(1)}, u32[]{:S(2)}, u32[]{:S(2)}) %collective-permute-start.14) | collective-permute-done | bytes 49184 | tf_op jit(solution)/shard_map/ppermute | solution.py:340
  44.2 1.9 %collective-permute-done.15 = f32[96,128]{1,0:T(8,128)S(1)} collective-permute-done((f32[96,128]{1,0:T(8,128)S(1)}, f32[96,128]{1,0:T(8,128)S(1)}, u32[]{:S(2)}, u32[]{:S(2)}) %collective-permute-start.15) | collective-permute-done | bytes 49184 | tf_op jit(solution)/shard_map/ppermute | solution.py:340
  46.1 4.4 %collective-permute-start.18 = (f32[96,128]{1,0:T(8,128)S(1)}, f32[96,128]{1,0:T(8,128)S(1)}, u32[]{:S(2)}, u32[]{:S(2)}) collective-permute-start(f32[96,128]{1,0:T(8,128)S(1)} %add_add_fusion.1), channel_id=1, source_target_pairs={{0,96},{32,64},{64,32},{96,0},{128,224},{160,192},{192,160},{224,1... | collective-permute-start | bytes 147464 | tf_op jit(solution)/shard_map/ppermute | solution.py:341
  50.5 0.4 collective-permute-start.16
  50.9 1.1 %collective-permute-done.18 = f32[96,128]{1,0:T(8,128)S(1)} collective-permute-done((f32[96,128]{1,0:T(8,128)S(1)}, f32[96,128]{1,0:T(8,128)S(1)}, u32[]{:S(2)}, u32[]{:S(2)}) %collective-permute-start.18) | collective-permute-done | bytes 49184 | tf_op jit(solution)/shard_map/ppermute | solution.py:341
  52.0 2.7 %collective-permute-done.17 = f32[96,128]{1,0:T(8,128)S(1)} collective-permute-done((f32[96,128]{1,0:T(8,128)S(1)}, f32[96,128]{1,0:T(8,128)S(1)}, u32[]{:S(2)}, u32[]{:S(2)}) %collective-permute-start.17) | collective-permute-done | bytes 49184 | tf_op jit(solution)/shard_map/ppermute | solution.py:341
  54.7 3.6 %collective-permute-start.19 = (f32[96,128]{1,0:T(8,128)S(1)}, f32[96,128]{1,0:T(8,128)S(1)}, u32[]{:S(2)}, u32[]{:S(2)}) collective-permute-start(f32[96,128]{1,0:T(8,128)S(1)} %add_add_fusion.total_ref), channel_id=1, source_target_pairs={{0,192},{32,224},{64,128},{96,160},{128,64},{160,96},{192,0},{224,... | collective-permute-start | bytes 147464 | tf_op jit(solution)/shard_map/ppermute | solution.py:342
  58.3 2.1 %collective-permute-done.19.other_ref = f32[96,128]{1,0:T(8,128)S(1)} collective-permute-done((f32[96,128]{1,0:T(8,128)S(1)}, f32[96,128]{1,0:T(8,128)S(1)}, u32[]{:S(2)}, u32[]{:S(2)}) %collective-permute-start.19) | collective-permute-done | bytes 49184 | tf_op jit(solution)/shard_map/ppermute | solution.py:342
  60.4 2.0 %interval_rows.1 = (f32[16,128]{1,0:T(8,128)S(1)}, f32[64,64]{1,0:T(8,128)S(1)}) custom-call(f32[96,128]{1,0:T(8,128)S(1)} %add_add_fusion.total_ref, f32[96,128]{1,0:T(8,128)S(1)} %collective-permute-done.19.other_ref, f32[64,64]{1,0:T(8,128)S(1)} %get-tuple-element.58.gram_day_ref, f32[16,128]{1,0:T(8,128)S(1)} %get-tuple-element.42.day_ref), custom_call_target="tpu_custom_call" | custom-call | flops 1048576 | bytes 65536 | tf_op jit(solution)/shard_map/interval_rows/pallas_call | solution.py:239
  62.4 3.9 %collective-permute-start.20 = (f32[16,128]{1,0:T(8,128)S(1)}, f32[16,128]{1,0:T(8,128)S(1)}, u32[]{:S(2)}, u32[]{:S(2)}) collective-permute-start(f32[16,128]{1,0:T(8,128)S(1)} %get-tuple-element.59), channel_id=1, source_target_pairs={{0,1},{1,0},{2,3},{3,2},{4,5},{5,4},{6,7},{7,6},{8,9},{9,8},{10,11... | collective-permute-start | bytes 24584 | tf_op jit(solution)/shard_map/ppermute | solution.py:259
  66.3 0.8 %collective-permute-done.20 = f32[16,128]{1,0:T(8,128)S(1)} collective-permute-done((f32[16,128]{1,0:T(8,128)S(1)}, f32[16,128]{1,0:T(8,128)S(1)}, u32[]{:S(2)}, u32[]{:S(2)}) %collective-permute-start.20) | collective-permute-done | bytes 8224 | tf_op jit(solution)/shard_map/ppermute | solution.py:259
  67.2 10.0 %all_to_all.5.recv_ref = f32[16,16,128]{2,1,0:T(8,128)S(1)} all-to-all(f32[16,16,128]{2,1,0:T(8,128)S(1)} %broadcast_in_dim.2), channel_id=1, replica_groups=mesh['z'=8,'x'=4,'y'=4,'core'=2] {'x','y'}, dimensions={0} | all-to-all | bytes 262144 | tf_op jit(solution)/shard_map/all_to_all | solution.py:350
  77.2 2.4 %day_rows.1 = (f32[32,64]{1,0:T(8,128)}, f32[16,64]{1,0:T(8,128)}) custom-call(f32[16,16,128]{2,1,0:T(8,128)S(1)} %all_to_all.5.recv_ref, f32[64,64]{1,0:T(8,128)S(1)} %get-tuple-element.60.gram_ref), custom_call_target="tpu_custom_call" | custom-call | flops 1048576 | bytes 65536 | tf_op jit(solution)/shard_map/day_rows/pallas_call | solution.py:239
  (12 shorter events, 0.1 us)
Async XLA Ops:
  3.7 5.9 %collective-permute-start = (f32[264,1024]{1,0:T(8,128)S(1)}, f32[264,1024]{1,0:T(8,128)S(1)}, u32[]{:S(2)}, u32[]{:S(2)}) collective-permute-start(f32[264,1024]{1,0:T(8,128)S(1)} %get-tuple-element.35.sent_ref), channel_id=1, source_target_pairs={{0,1},{1,0},{2,3},{3,2},{4,5},{5,4},{6,7},{7,6},{8,9},{9,8},{10,11... | collective-permute-start | bytes 3244040 | tf_op jit(solution)/shard_map/ppermute | solution.py:259
  9.7 13.3 %collective-permute-start.1 = (f32[544,128]{1,0:T(8,128)S(1)}, f32[544,128]{1,0:T(8,128)S(1)}, u32[]{:S(2)}, u32[]{:S(2)}) collective-permute-start(f32[544,128]{1,0:T(8,128)S(1)} %get-tuple-element.37), channel_id=1, source_target_pairs={{0,4},{2,6},{4,0},{6,2},{1,5},{3,7},{5,1},{7,3},{8,12},{10,14},{12... | collective-permute-start | bytes 835592 | tf_op jit(solution)/shard_map/ppermute | solution.py:262
  11.0 10.2 %collective-permute-start.2 = (f32[72,512]{1,0:T(8,128)S(1)}, f32[72,512]{1,0:T(8,128)S(1)}, u32[]{:S(2)}, u32[]{:S(2)}) collective-permute-start(f32[72,512]{1,0:T(8,128)S(1)} %get-tuple-element.38), channel_id=1, source_target_pairs={{0,2},{2,0},{4,6},{6,4},{1,3},{3,1},{5,7},{7,5},{8,10},{10,8},{12,... | collective-permute-start | bytes 442376 | tf_op jit(solution)/shard_map/ppermute | solution.py:262
  11.4 11.7 %collective-permute-start.3 = (f32[72,512]{1,0:T(8,128)S(1)}, f32[72,512]{1,0:T(8,128)S(1)}, u32[]{:S(2)}, u32[]{:S(2)}) collective-permute-start(f32[72,512]{1,0:T(8,128)S(1)} %get-tuple-element.39), channel_id=1, source_target_pairs={{0,6},{2,4},{4,2},{6,0},{1,7},{3,5},{5,3},{7,1},{8,14},{10,12},{12... | collective-permute-start | bytes 442376 | tf_op jit(solution)/shard_map/ppermute | solution.py:262
  13.1 11.8 %collective-permute-start.4 = (f32[64,512]{1,0:T(8,128)S(1)}, f32[64,512]{1,0:T(8,128)S(1)}, u32[]{:S(2)}, u32[]{:S(2)}) collective-permute-start(f32[64,512]{1,0:T(8,128)S(1)} %get-tuple-element.40), channel_id=1, source_target_pairs={{0,2},{2,0},{4,6},{6,4},{1,3},{3,1},{5,7},{7,5},{8,10},{10,8},{12,... | collective-permute-start | bytes 393224 | tf_op jit(solution)/shard_map/ppermute | solution.py:262
  13.1 12.8 %collective-permute-start.5 = (f32[64,512]{1,0:T(8,128)S(1)}, f32[64,512]{1,0:T(8,128)S(1)}, u32[]{:S(2)}, u32[]{:S(2)}) collective-permute-start(f32[64,512]{1,0:T(8,128)S(1)} %get-tuple-element.44), channel_id=1, source_target_pairs={{0,6},{2,4},{4,2},{6,0},{1,7},{3,5},{5,3},{7,1},{8,14},{10,12},{12... | collective-permute-start | bytes 393224 | tf_op jit(solution)/shard_map/ppermute | solution.py:262
  26.1 3.9 %collective-permute-start.6 = (bf16[64,1024]{1,0:T(8,128)(2,1)S(1)}, bf16[64,1024]{1,0:T(8,128)(2,1)S(1)}, u32[]{:S(2)}, u32[]{:S(2)}) collective-permute-start(bf16[64,1024]{1,0:T(8,128)(2,1)S(1)} %get-tuple-element.45.low), channel_id=1, source_target_pairs={{0,1},{1,0},{2,3},{3,2},{4,5},{5,4},{6,7},{7,6},{8,9},{9,8},{10,11... | collective-permute-start | bytes 393224 | tf_op jit(solution)/shard_map/ppermute | solution.py:259
  26.7 6.6 %collective-permute-start.9 = (bf16[64,1024]{1,0:T(8,128)(2,1)S(1)}, bf16[64,1024]{1,0:T(8,128)(2,1)S(1)}, u32[]{:S(2)}, u32[]{:S(2)}) collective-permute-start(bf16[64,1024]{1,0:T(8,128)(2,1)S(1)} %get-tuple-element.45.low), channel_id=1, source_target_pairs={{0,4},{2,6},{4,0},{6,2},{1,5},{3,7},{5,1},{7,3},{8,12},{10,14},{12... | collective-permute-start | bytes 393224 | tf_op jit(solution)/shard_map/ppermute | solution.py:262
  27.9 7.2 %collective-permute-start.8 = (bf16[64,1024]{1,0:T(8,128)(2,1)S(1)}, bf16[64,1024]{1,0:T(8,128)(2,1)S(1)}, u32[]{:S(2)}, u32[]{:S(2)}) collective-permute-start(bf16[64,1024]{1,0:T(8,128)(2,1)S(1)} %get-tuple-element.45.low), channel_id=1, source_target_pairs={{0,2},{2,0},{4,6},{6,4},{1,3},{3,1},{5,7},{7,5},{8,10},{10,8},{12,... | collective-permute-start | bytes 393224 | tf_op jit(solution)/shard_map/ppermute | solution.py:262
  28.3 8.2 %collective-permute-start.7 = (bf16[64,1024]{1,0:T(8,128)(2,1)S(1)}, bf16[64,1024]{1,0:T(8,128)(2,1)S(1)}, u32[]{:S(2)}, u32[]{:S(2)}) collective-permute-start(bf16[64,1024]{1,0:T(8,128)(2,1)S(1)} %get-tuple-element.45.low), channel_id=1, source_target_pairs={{0,6},{2,4},{4,2},{6,0},{1,7},{3,5},{5,3},{7,1},{8,14},{10,12},{12... | collective-permute-start | bytes 393224 | tf_op jit(solution)/shard_map/ppermute | solution.py:262
  33.3 3.7 %collective-permute-start.11 = (bf16[64,1024]{1,0:T(8,128)(2,1)S(1)}, bf16[64,1024]{1,0:T(8,128)(2,1)S(1)}, u32[]{:S(2)}, u32[]{:S(2)}) collective-permute-start(bf16[64,1024]{1,0:T(8,128)(2,1)S(1)} %collective-permute-done.9.low), channel_id=1, source_target_pairs={{0,1},{1,0},{2,3},{3,2},{4,5},{5,4},{6,7},{7,6},{8,9},{9,8},{10,11... | collective-permute-start | bytes 393224 | tf_op jit(solution)/shard_map/ppermute | solution.py:259
  35.1 1.9 %collective-permute-start.12 = (bf16[64,1024]{1,0:T(8,128)(2,1)S(1)}, bf16[64,1024]{1,0:T(8,128)(2,1)S(1)}, u32[]{:S(2)}, u32[]{:S(2)}) collective-permute-start(bf16[64,1024]{1,0:T(8,128)(2,1)S(1)} %collective-permute-done.8.low), channel_id=1, source_target_pairs={{0,1},{1,0},{2,3},{3,2},{4,5},{5,4},{6,7},{7,6},{8,9},{9,8},{10,11... | collective-permute-start | bytes 393224 | tf_op jit(solution)/shard_map/ppermute | solution.py:259
  36.5 1.6 %collective-permute-start.10 = (bf16[64,1024]{1,0:T(8,128)(2,1)S(1)}, bf16[64,1024]{1,0:T(8,128)(2,1)S(1)}, u32[]{:S(2)}, u32[]{:S(2)}) collective-permute-start(bf16[64,1024]{1,0:T(8,128)(2,1)S(1)} %collective-permute-done.7.low3), channel_id=1, source_target_pairs={{0,1},{1,0},{2,3},{3,2},{4,5},{5,4},{6,7},{7,6},{8,9},{9,8},{10,11... | collective-permute-start | bytes 393224 | tf_op jit(solution)/shard_map/ppermute | solution.py:259
  38.5 3.9 %collective-permute-start.13 = (f32[96,128]{1,0:T(8,128)S(1)}, f32[96,128]{1,0:T(8,128)S(1)}, u32[]{:S(2)}, u32[]{:S(2)}) collective-permute-start(f32[96,128]{1,0:T(8,128)S(1)} %get-tuple-element.55), channel_id=1, source_target_pairs={{0,8},{8,0},{16,24},{24,16},{1,9},{9,1},{17,25},{25,17},{2,10},{10... | collective-permute-start | bytes 147464 | tf_op jit(solution)/shard_map/ppermute | solution.py:340
  39.4 4.7 %collective-permute-start.14 = (f32[96,128]{1,0:T(8,128)S(1)}, f32[96,128]{1,0:T(8,128)S(1)}, u32[]{:S(2)}, u32[]{:S(2)}) collective-permute-start(f32[96,128]{1,0:T(8,128)S(1)} %get-tuple-element.56), channel_id=1, source_target_pairs={{0,16},{8,24},{16,0},{24,8},{1,17},{9,25},{17,1},{25,9},{2,18},{10... | collective-permute-start | bytes 147464 | tf_op jit(solution)/shard_map/ppermute | solution.py:340
  41.9 4.2 %collective-permute-start.15 = (f32[96,128]{1,0:T(8,128)S(1)}, f32[96,128]{1,0:T(8,128)S(1)}, u32[]{:S(2)}, u32[]{:S(2)}) collective-permute-start(f32[96,128]{1,0:T(8,128)S(1)} %get-tuple-element.57), channel_id=1, source_target_pairs={{0,24},{8,16},{16,8},{24,0},{1,25},{9,17},{17,9},{25,1},{2,26},{10... | collective-permute-start | bytes 147464 | tf_op jit(solution)/shard_map/ppermute | solution.py:340
  46.1 5.9 %collective-permute-start.18 = (f32[96,128]{1,0:T(8,128)S(1)}, f32[96,128]{1,0:T(8,128)S(1)}, u32[]{:S(2)}, u32[]{:S(2)}) collective-permute-start(f32[96,128]{1,0:T(8,128)S(1)} %add_add_fusion.1), channel_id=1, source_target_pairs={{0,96},{32,64},{64,32},{96,0},{128,224},{160,192},{192,160},{224,1... | collective-permute-start | bytes 147464 | tf_op jit(solution)/shard_map/ppermute | solution.py:341
  50.5 4.2 %collective-permute-start.17 = (f32[96,128]{1,0:T(8,128)S(1)}, f32[96,128]{1,0:T(8,128)S(1)}, u32[]{:S(2)}, u32[]{:S(2)}) collective-permute-start(f32[96,128]{1,0:T(8,128)S(1)} %add_add_fusion.1), channel_id=1, source_target_pairs={{0,64},{32,96},{64,0},{96,32},{128,192},{160,224},{192,128},{224,1... | collective-permute-start | bytes 147464 | tf_op jit(solution)/shard_map/ppermute | solution.py:341
  50.5 4.2 %collective-permute-start.16 = (f32[96,128]{1,0:T(8,128)S(1)}, f32[96,128]{1,0:T(8,128)S(1)}, u32[]{:S(2)}, u32[]{:S(2)}) collective-permute-start(f32[96,128]{1,0:T(8,128)S(1)} %add_add_fusion.1), channel_id=1, source_target_pairs={{0,32},{32,0},{64,96},{96,64},{128,160},{160,128},{192,224},{224,1... | collective-permute-start | bytes 147464 | tf_op jit(solution)/shard_map/ppermute | solution.py:341
  54.7 5.7 %collective-permute-start.19 = (f32[96,128]{1,0:T(8,128)S(1)}, f32[96,128]{1,0:T(8,128)S(1)}, u32[]{:S(2)}, u32[]{:S(2)}) collective-permute-start(f32[96,128]{1,0:T(8,128)S(1)} %add_add_fusion.total_ref), channel_id=1, source_target_pairs={{0,192},{32,224},{64,128},{96,160},{128,64},{160,96},{192,0},{224,... | collective-permute-start | bytes 147464 | tf_op jit(solution)/shard_map/ppermute | solution.py:342
  62.4 4.7 %collective-permute-start.20 = (f32[16,128]{1,0:T(8,128)S(1)}, f32[16,128]{1,0:T(8,128)S(1)}, u32[]{:S(2)}, u32[]{:S(2)}) collective-permute-start(f32[16,128]{1,0:T(8,128)S(1)} %get-tuple-element.59), channel_id=1, source_target_pairs={{0,1},{1,0},{2,3},{3,2},{4,5},{5,4},{6,7},{7,6},{8,9},{9,8},{10,11... | collective-permute-start | bytes 24584 | tf_op jit(solution)/shard_map/ppermute | solution.py:259

commit v8 on v7

--- a/solution.py
+++ b/solution.py
@@ -164,9 +164,13 @@
     return total
 
 
-def first_partial_kernel(low, low_other, keep_ref, send_ref, link_ref, acc, link_out):
+def first_partial_kernel(low, keep_ref, link_ref, acc, link_out):
     link_out[...] = link_ref[...]
-    acc[...] = times_blocks((low,), keep_ref, (0,)) + times_blocks((low_other,), send_ref, (0,))
+    acc[...] = times_blocks((low,), keep_ref, (0,))
+
+
+def second_partial_kernel(low2, low_other, keep_ref, send_ref, before, acc):
+    acc[...] = before[...] + times_blocks((low2,), keep_ref, (2,)) + times_blocks((low_other,), send_ref, (0,))
 
 
 def one_partial_kernel(block, low, keep_ref, before, acc):
@@ -200,10 +204,11 @@
     return jnp.transpose(eliminate(shifted(system), rhs))[RANK : RANK + count]
 
 
-def interval_kernel(total_ref, other_ref, gram_day_ref, day_ref, out_ref, gram_ref):
-    gram = unpack(total_ref[RANK:] + other_ref[RANK:])
+def interval_kernel(part0, part1, part2, part3, gram_day_ref, day_ref, out_ref, gram_ref):
+    total = (part0[...] + part1[...]) + (part2[...] + part3[...])
+    gram = unpack(total[RANK:])
     gram_ref[...] = gram
-    partial = (total_ref[:RANK] + other_ref[:RANK]).reshape(4, 16, 2 * RANK)
+    partial = total[:RANK].reshape(4, 16, 2 * RANK)
     sums = jnp.sum(partial * day_ref[...][None], axis=1)
     rows = solve_rows(gram * gram_day_ref[...], jnp.concatenate([sums[:, :RANK], sums[:, RANK:]], axis=0))
     day_part = jnp.sum(partial * jnp.concatenate([rows[:4], rows[4:]], axis=1)[:, None, :], axis=0)
@@ -317,12 +322,13 @@
     acc, link = call(
         first_partial_kernel,
         (total, shape((RANK, 1024))),
-        (low, other_core(low), held_keep, held_send, link),
+        (low, held_keep, link),
         "partial_own",
     )
+    low_other = other_core(after(low, acc))
     low2 = after(low2, acc)
     other2 = other_core(low2)
-    acc = call(functools.partial(one_partial_kernel, 2), total, (low2, held_keep, acc), "partial_two")
+    acc = call(second_partial_kernel, total, (low2, low_other, held_keep, held_send, acc), "partial_two")
     low1 = after(low1, acc)
     other1 = other_core(low1)
     acc = call(functools.partial(one_partial_kernel, 1), total, (low1, held_keep, acc), "partial_one")
@@ -338,12 +344,12 @@
         [pltpu.VMEM((288, 2 * RANK), F32)],
     )
     over_x = sum([lax.ppermute(outgoing[d], "x", partners(4, d)) for d in (1, 2, 3)], outgoing[0])
-    over_z = sum([lax.ppermute(over_x, "z", partners(8, d)) for d in (1, 2, 3)], over_x)
-    z_other = lax.ppermute(over_z, "z", partners(8, 6))
+    over_pair = over_x + lax.ppermute(over_x, "z", partners(8, 6))
+    over_z = [over_pair] + [lax.ppermute(over_pair, "z", partners(8, d)) for d in (1, 2, 3)]
     found, gram_link = call(
         interval_kernel,
         (shape((16, 128)), shape((RANK, RANK))),
-        (over_z, z_other, gram_day, day_twice),
+        (*over_z, gram_day, day_twice),
         "interval_rows",
     )
     found = found + other_core(found)

time: 79.8 us -> 79.2 us (level)
  starting transfers between devices: 30.5 us -> 33.7 us
  waiting for transfers between devices: 21.7 us -> 18.6 us
    ppermute x4, waiting for transfers between devices: 5.92 us -> 3.81 us  [the longest x3 2.24 us: body(): lax.ppermute(over_pair, 'z', partners(8, d))]
    ppermute x6, starting transfers between devices: 10.1 us -> 11.8 us  [other_core(): return lax.ppermute(a, 'core', partners(2, 1))]
    ppermute x8, waiting for transfers between devices: 11.4 us -> 10 us  [along_y(): return lax.ppermute(a, 'y', partners(4, d))]
    ppermute x4, starting transfers between devices: 8.41 us -> 9.73 us  [the longest x1 6.1 us: body(): over_pair = over_x + lax.ppermute(over_x, 'z', partners(8, 6))]
  transfers between devices with their start and end apart: 21 -> 21, of which waited for: 11 -> 10; matrix products, arithmetic and copies ran while one was open for 0% -> 0% of each run, Pallas kernels for 10% -> 10%
where the time goes in v8:
time: 79.2 us; the launch traced here: 79 us
  starting transfers between devices  33.7 us (43%)
  waiting for transfers between devices  18.6 us (23%)
  Pallas kernels  16.6 us (21%)
  blocking collectives  9.34 us (12%)
    pallas_call x13, Pallas kernels, call(): pl.pallas_call(kernel, out_shape=out_shape, in_specs=[pl.BlockSpec(memory...  16.6 us
    ppermute x6, starting transfers between devices, other_core(): return lax.ppermute(a, 'core', partners(2, 1))  11.8 us
    ppermute x8, waiting for transfers between devices, along_y(): return lax.ppermute(a, 'y', partners(4, d))  10 us
    all_to_all x1, blocking collectives, body(): lax.all_to_all(jnp.broadcast_to(found[None], (16, 16, 128)), ('x', 'y'),...  9.34 us
    ppermute x8, starting transfers between devices, along_y(): return lax.ppermute(a, 'y', partners(4, d))  8.17 us
    ppermute x1, starting transfers between devices, body(): over_pair = over_x + lax.ppermute(over_x, 'z', partners(8, 6))  6.1 us
    ppermute x3, waiting for transfers between devices, body(): lax.ppermute(outgoing[d], 'x', partners(4, d))  3.96 us
    ppermute x3, starting transfers between devices, body(): lax.ppermute(outgoing[d], 'x', partners(4, d))  3.95 us
  transfers between devices with their start and end apart: 21, of which 10 were waited for; matrix products, arithmetic and copies ran while one was open for 0% of the time, Pallas kernels for 10%

profile of v8, /device:TPU:1, one launch (start us, length us, event | category | flops | bytes accessed | tf_op | source)
XLA Modules:
  0.0 79.0 jit_solution(5213135654423387813)
XLA Ops:
  0.6 3.1 %sums_to_send.1 = (f32[264,1024]{1,0:T(8,128)S(1)}, bf16[4,512,1024]{2,1,0:T(8,128)(2,1)S(1)}, bf16[64,512]{1,0:T(8,128)(2,1)S(1)}, f32[16,128]{1,0:T(8,128)S(1)}) custom-call(bf16[512,8192]{1,0:T(8,128)(2,1)} %bitcast.2, f32[32,64]{1,0:T(8,128)} %interval_ref.1, f32[16,64]{1,0:T(8,128)} %day_ref.1), custom_call_target="tpu_custom_call" | custom-call | flops 1048576 | bytes 65536 | tf_op jit(solution)/shard_map/sums_to_send/pallas_call | solution.py:244
  3.7 3.3 %collective-permute-start = (f32[264,1024]{1,0:T(8,128)S(1)}, f32[264,1024]{1,0:T(8,128)S(1)}, u32[]{:S(2)}, u32[]{:S(2)}) collective-permute-start(f32[264,1024]{1,0:T(8,128)S(1)} %get-tuple-element.36.sent_ref), channel_id=1, source_target_pairs={{0,1},{1,0},{2,3},{3,2},{4,5},{5,4},{6,7},{7,6},{8,9},{9,8},{10,11... | collective-permute-start | bytes 3244040 | tf_op jit(solution)/shard_map/ppermute | solution.py:264
  7.0 2.5 %sums_to_keep.1 = (f32[4,64,1024]{2,1,0:T(8,128)S(1)}, bf16[4,512,1024]{2,1,0:T(8,128)(2,1)S(1)}) custom-call(bf16[512,8192]{1,0:T(8,128)(2,1)} %bitcast.3, bf16[64,512]{1,0:T(8,128)(2,1)S(1)} %get-tuple-element.34.khatri_ref), custom_call_target="tpu_custom_call" | custom-call | flops 1048576 | bytes 65536 | tf_op jit(solution)/shard_map/sums_to_keep/pallas_call | solution.py:244
  9.6 0.2 add_cores.1
  9.7 1.3 %collective-permute-start.1 = (f32[544,128]{1,0:T(8,128)S(1)}, f32[544,128]{1,0:T(8,128)S(1)}, u32[]{:S(2)}, u32[]{:S(2)}) collective-permute-start(f32[544,128]{1,0:T(8,128)S(1)} %get-tuple-element.38), channel_id=1, source_target_pairs={{0,4},{2,6},{4,0},{6,2},{1,5},{3,7},{5,1},{7,3},{8,12},{10,14},{12... | collective-permute-start | bytes 835592 | tf_op jit(solution)/shard_map/ppermute | solution.py:267
  11.0 0.4 collective-permute-start.2
  11.4 1.7 %collective-permute-start.3 = (f32[72,512]{1,0:T(8,128)S(1)}, f32[72,512]{1,0:T(8,128)S(1)}, u32[]{:S(2)}, u32[]{:S(2)}) collective-permute-start(f32[72,512]{1,0:T(8,128)S(1)} %get-tuple-element.40), channel_id=1, source_target_pairs={{0,6},{2,4},{4,2},{6,0},{1,7},{3,5},{5,3},{7,1},{8,14},{10,12},{12... | collective-permute-start | bytes 442376 | tf_op jit(solution)/shard_map/ppermute | solution.py:267
  13.1 0.0 collective-permute-start.4
  13.1 1.5 %collective-permute-start.5 = (f32[64,512]{1,0:T(8,128)S(1)}, f32[64,512]{1,0:T(8,128)S(1)}, u32[]{:S(2)}, u32[]{:S(2)}) collective-permute-start(f32[64,512]{1,0:T(8,128)S(1)} %get-tuple-element.45), channel_id=1, source_target_pairs={{0,6},{2,4},{4,2},{6,0},{1,7},{3,5},{5,3},{7,1},{8,14},{10,12},{12... | collective-permute-start | bytes 393224 | tf_op jit(solution)/shard_map/ppermute | solution.py:267
  14.6 6.7 %collective-permute-done.2.one.one_a = f32[72,512]{1,0:T(8,128)S(1)} collective-permute-done((f32[72,512]{1,0:T(8,128)S(1)}, f32[72,512]{1,0:T(8,128)S(1)}, u32[]{:S(2)}, u32[]{:S(2)}) %collective-permute-start.2) | collective-permute-done | bytes 147488 | tf_op jit(solution)/shard_map/ppermute | solution.py:267
  21.2 1.8 %collective-permute-done.3.three.three_a = f32[72,512]{1,0:T(8,128)S(1)} collective-permute-done((f32[72,512]{1,0:T(8,128)S(1)}, f32[72,512]{1,0:T(8,128)S(1)}, u32[]{:S(2)}, u32[]{:S(2)}) %collective-permute-start.3) | collective-permute-done | bytes 147488 | tf_op jit(solution)/shard_map/ppermute | solution.py:267
  23.1 1.8 %link_inverse.1 = (f32[64,64]{1,0:T(8,128)S(1)}, f32[64,64]{1,0:T(8,128)S(1)}) custom-call(f32[8,512]{1,0:T(8,128)S(1)} %get-tuple-element.42.own, f32[544,128]{1,0:T(8,128)S(1)} %collective-permute-done.1.two, f32[72,512]{1,0:T(8,128)S(1)} %collective-permute-done.2.one.one_a, f32[72,512]{1,0:T(8,128)S(1)} %collective-permute-done.3.three.three_a, ...), custom_call_target="tpu_custom_call" | custom-call | flops 1048576 | bytes 65536 | tf_op jit(solution)/shard_map/link_inverse/pallas_call | solution.py:244
  24.9 0.0 collective-permute-done.4.one_b
  24.9 0.4 most_of_link_rows.1.before
  25.3 0.6 collective-permute-done.5.three_b
  25.9 0.3 link_rows.1
  26.1 1.3 %collective-permute-start.8 = (bf16[64,1024]{1,0:T(8,128)(2,1)S(1)}, bf16[64,1024]{1,0:T(8,128)(2,1)S(1)}, u32[]{:S(2)}, u32[]{:S(2)}) collective-permute-start(bf16[64,1024]{1,0:T(8,128)(2,1)S(1)} %get-tuple-element.52.low), channel_id=1, source_target_pairs={{0,4},{2,6},{4,0},{6,2},{1,5},{3,7},{5,1},{7,3},{8,12},{10,14},{12... | collective-permute-start | bytes 393224 | tf_op jit(solution)/shard_map/ppermute | solution.py:267
  27.4 1.1 %partial_own.1 = (f32[288,128]{1,0:T(8,128)S(1)}, f32[64,1024]{1,0:T(8,128)}) custom-call(bf16[64,1024]{1,0:T(8,128)(2,1)S(1)} %get-tuple-element.52.low, bf16[4,512,1024]{2,1,0:T(8,128)(2,1)S(1)} %get-tuple-element.47.keep_ref, f32[64,1024]{1,0:T(8,128)S(1)} %get-tuple-element.48.link_ref), custom_call_target="tpu_custom_call" | custom-call | flops 1048576 | bytes 65536 | tf_op jit(solution)/shard_map/partial_own/pallas_call | solution.py:244
  28.5 0.8 collective-permute-start.9
  29.3 0.4 collective-permute-start.7
  29.7 1.7 %collective-permute-start.6 = (bf16[64,1024]{1,0:T(8,128)(2,1)S(1)}, bf16[64,1024]{1,0:T(8,128)(2,1)S(1)}, u32[]{:S(2)}, u32[]{:S(2)}) collective-permute-start(bf16[64,1024]{1,0:T(8,128)(2,1)S(1)} %get-tuple-element.52.low), channel_id=1, source_target_pairs={{0,6},{2,4},{4,2},{6,0},{1,7},{3,5},{5,3},{7,1},{8,14},{10,12},{12... | collective-permute-start | bytes 393224 | tf_op jit(solution)/shard_map/ppermute | solution.py:267
  31.3 0.9 %collective-permute-done.8.low2 = bf16[64,1024]{1,0:T(8,128)(2,1)S(1)} collective-permute-done((bf16[64,1024]{1,0:T(8,128)(2,1)S(1)}, bf16[64,1024]{1,0:T(8,128)(2,1)S(1)}, u32[]{:S(2)}, u32[]{:S(2)}) %collective-permute-start.8) | collective-permute-done | bytes 131104 | tf_op jit(solution)/shard_map/ppermute | solution.py:267
  32.3 1.4 %collective-permute-start.11 = (bf16[64,1024]{1,0:T(8,128)(2,1)S(1)}, bf16[64,1024]{1,0:T(8,128)(2,1)S(1)}, u32[]{:S(2)}, u32[]{:S(2)}) collective-permute-start(bf16[64,1024]{1,0:T(8,128)(2,1)S(1)} %collective-permute-done.8.low2), channel_id=1, source_target_pairs={{0,1},{1,0},{2,3},{3,2},{4,5},{5,4},{6,7},{7,6},{8,9},{9,8},{10,11... | collective-permute-start | bytes 393224 | tf_op jit(solution)/shard_map/ppermute | solution.py:264
  33.7 0.8 partial_two.1.before
  34.5 0.0 collective-permute-done.7.low
  34.5 0.7 collective-permute-start.12
  35.2 0.5 partial_one.1.before
  35.7 0.0 collective-permute-done.6.low3
  35.7 1.1 %collective-permute-start.10 = (bf16[64,1024]{1,0:T(8,128)(2,1)S(1)}, bf16[64,1024]{1,0:T(8,128)(2,1)S(1)}, u32[]{:S(2)}, u32[]{:S(2)}) collective-permute-start(bf16[64,1024]{1,0:T(8,128)(2,1)S(1)} %collective-permute-done.6.low3), channel_id=1, source_target_pairs={{0,1},{1,0},{2,3},{3,2},{4,5},{5,4},{6,7},{7,6},{8,9},{9,8},{10,11... | collective-permute-start | bytes 393224 | tf_op jit(solution)/shard_map/ppermute | solution.py:264
  36.8 1.1 %partial_mixed.1.before = f32[288,128]{1,0:T(8,128)S(1)} custom-call(bf16[64,1024]{1,0:T(8,128)(2,1)S(1)} %collective-permute-done.6.low3, bf16[64,1024]{1,0:T(8,128)(2,1)S(1)} %collective-permute-done.11.other2, bf16[64,1024]{1,0:T(8,128)(2,1)S(1)} %collective-permute-done.12.other1, bf16[4,512,1024]{2,1,0:T(8,128)(2,1)S(1)} %get-tuple-element.47.keep_ref, ...), custom_call_target="tpu_custom_call" | custom-call | flops 1048576 | bytes 65536 | tf_op jit(solution)/shard_map/partial_mixed/pallas_call | solution.py:244
  37.9 0.5 partial_last.1
  38.4 1.3 %collective-permute-start.13 = (f32[96,128]{1,0:T(8,128)S(1)}, f32[96,128]{1,0:T(8,128)S(1)}, u32[]{:S(2)}, u32[]{:S(2)}) collective-permute-start(f32[96,128]{1,0:T(8,128)S(1)} %get-tuple-element.57), channel_id=1, source_target_pairs={{0,8},{8,0},{16,24},{24,16},{1,9},{9,1},{17,25},{25,17},{2,10},{10... | collective-permute-start | bytes 147464 | tf_op jit(solution)/shard_map/ppermute | solution.py:346
  39.7 2.5 %collective-permute-start.14 = (f32[96,128]{1,0:T(8,128)S(1)}, f32[96,128]{1,0:T(8,128)S(1)}, u32[]{:S(2)}, u32[]{:S(2)}) collective-permute-start(f32[96,128]{1,0:T(8,128)S(1)} %get-tuple-element.58), channel_id=1, source_target_pairs={{0,16},{8,24},{16,0},{24,8},{1,17},{9,25},{17,1},{25,9},{2,18},{10... | collective-permute-start | bytes 147464 | tf_op jit(solution)/shard_map/ppermute | solution.py:346
  42.1 0.2 collective-permute-start.15
  42.3 2.2 %collective-permute-done.14 = f32[96,128]{1,0:T(8,128)S(1)} collective-permute-done((f32[96,128]{1,0:T(8,128)S(1)}, f32[96,128]{1,0:T(8,128)S(1)}, u32[]{:S(2)}, u32[]{:S(2)}) %collective-permute-start.14) | collective-permute-done | bytes 49184 | tf_op jit(solution)/shard_map/ppermute | solution.py:346
  44.5 1.8 %collective-permute-done.15 = f32[96,128]{1,0:T(8,128)S(1)} collective-permute-done((f32[96,128]{1,0:T(8,128)S(1)}, f32[96,128]{1,0:T(8,128)S(1)}, u32[]{:S(2)}, u32[]{:S(2)}) %collective-permute-start.15) | collective-permute-done | bytes 49184 | tf_op jit(solution)/shard_map/ppermute | solution.py:346
  46.3 6.1 %collective-permute-start.16 = (f32[96,128]{1,0:T(8,128)S(1)}, f32[96,128]{1,0:T(8,128)S(1)}, u32[]{:S(2)}, u32[]{:S(2)}) collective-permute-start(f32[96,128]{1,0:T(8,128)S(1)} %add_add_fusion), channel_id=1, source_target_pairs={{0,192},{32,224},{64,128},{96,160},{128,64},{160,96},{192,0},{224,... | collective-permute-start | bytes 147464 | tf_op jit(solution)/shard_map/ppermute | solution.py:347
  52.4 1.6 %collective-permute-done.16 = f32[96,128]{1,0:T(8,128)S(1)} collective-permute-done((f32[96,128]{1,0:T(8,128)S(1)}, f32[96,128]{1,0:T(8,128)S(1)}, u32[]{:S(2)}, u32[]{:S(2)}) %collective-permute-start.16) | collective-permute-done | bytes 49184 | tf_op jit(solution)/shard_map/ppermute | solution.py:347
  54.0 1.9 %collective-permute-start.19 = (f32[96,128]{1,0:T(8,128)S(1)}, f32[96,128]{1,0:T(8,128)S(1)}, u32[]{:S(2)}, u32[]{:S(2)}) collective-permute-start(f32[96,128]{1,0:T(8,128)S(1)} %add.18.part0), channel_id=1, source_target_pairs={{0,96},{32,64},{64,32},{96,0},{128,224},{160,192},{192,160},{224,1... | collective-permute-start | bytes 147464 | tf_op jit(solution)/shard_map/ppermute | solution.py:348
  55.9 0.0 collective-permute-start.18
  55.9 1.7 %collective-permute-start.17 = (f32[96,128]{1,0:T(8,128)S(1)}, f32[96,128]{1,0:T(8,128)S(1)}, u32[]{:S(2)}, u32[]{:S(2)}) collective-permute-start(f32[96,128]{1,0:T(8,128)S(1)} %add.18.part0), channel_id=1, source_target_pairs={{0,32},{32,0},{64,96},{96,64},{128,160},{160,128},{192,224},{224,1... | collective-permute-start | bytes 147464 | tf_op jit(solution)/shard_map/ppermute | solution.py:348
  57.6 1.2 %collective-permute-done.19.part3 = f32[96,128]{1,0:T(8,128)S(1)} collective-permute-done((f32[96,128]{1,0:T(8,128)S(1)}, f32[96,128]{1,0:T(8,128)S(1)}, u32[]{:S(2)}, u32[]{:S(2)}) %collective-permute-start.19) | collective-permute-done | bytes 49184 | tf_op jit(solution)/shard_map/ppermute | solution.py:348
  58.8 1.0 %collective-permute-done.18.part2 = f32[96,128]{1,0:T(8,128)S(1)} collective-permute-done((f32[96,128]{1,0:T(8,128)S(1)}, f32[96,128]{1,0:T(8,128)S(1)}, u32[]{:S(2)}, u32[]{:S(2)}) %collective-permute-start.18) | collective-permute-done | bytes 49184 | tf_op jit(solution)/shard_map/ppermute | solution.py:348
  59.8 2.0 %interval_rows.1 = (f32[16,128]{1,0:T(8,128)S(1)}, f32[64,64]{1,0:T(8,128)S(1)}) custom-call(f32[96,128]{1,0:T(8,128)S(1)} %add.18.part0, f32[96,128]{1,0:T(8,128)S(1)} %collective-permute-done.17.part1, f32[96,128]{1,0:T(8,128)S(1)} %collective-permute-done.18.part2, f32[96,128]{1,0:T(8,128)S(1)} %collective-permute-done.19.part3, ...), custom_call_target="tpu_custom_call" | custom-call | flops 1048576 | bytes 65536 | tf_op jit(solution)/shard_map/interval_rows/pallas_call | solution.py:244
  61.9 4.5 %collective-permute-start.20 = (f32[16,128]{1,0:T(8,128)S(1)}, f32[16,128]{1,0:T(8,128)S(1)}, u32[]{:S(2)}, u32[]{:S(2)}) collective-permute-start(f32[16,128]{1,0:T(8,128)S(1)} %get-tuple-element.61), channel_id=1, source_target_pairs={{0,1},{1,0},{2,3},{3,2},{4,5},{5,4},{6,7},{7,6},{8,9},{9,8},{10,11... | collective-permute-start | bytes 24584 | tf_op jit(solution)/shard_map/ppermute | solution.py:264
  66.3 0.8 %collective-permute-done.20 = f32[16,128]{1,0:T(8,128)S(1)} collective-permute-done((f32[16,128]{1,0:T(8,128)S(1)}, f32[16,128]{1,0:T(8,128)S(1)}, u32[]{:S(2)}, u32[]{:S(2)}) %collective-permute-start.20) | collective-permute-done | bytes 8224 | tf_op jit(solution)/shard_map/ppermute | solution.py:264
  67.2 9.3 %all_to_all.5.recv_ref = f32[16,16,128]{2,1,0:T(8,128)S(1)} all-to-all(f32[16,16,128]{2,1,0:T(8,128)S(1)} %broadcast_in_dim.2), channel_id=1, replica_groups=mesh['z'=8,'x'=4,'y'=4,'core'=2] {'x','y'}, dimensions={0} | all-to-all | bytes 262144 | tf_op jit(solution)/shard_map/all_to_all | solution.py:356
  76.5 2.4 %day_rows.1 = (f32[32,64]{1,0:T(8,128)}, f32[16,64]{1,0:T(8,128)}) custom-call(f32[16,16,128]{2,1,0:T(8,128)S(1)} %all_to_all.5.recv_ref, f32[64,64]{1,0:T(8,128)S(1)} %get-tuple-element.62.gram_ref), custom_call_target="tpu_custom_call" | custom-call | flops 1048576 | bytes 65536 | tf_op jit(solution)/shard_map/day_rows/pallas_call | solution.py:244
  (12 shorter events, 0.1 us)
Async XLA Ops:
  3.7 5.9 %collective-permute-start = (f32[264,1024]{1,0:T(8,128)S(1)}, f32[264,1024]{1,0:T(8,128)S(1)}, u32[]{:S(2)}, u32[]{:S(2)}) collective-permute-start(f32[264,1024]{1,0:T(8,128)S(1)} %get-tuple-element.36.sent_ref), channel_id=1, source_target_pairs={{0,1},{1,0},{2,3},{3,2},{4,5},{5,4},{6,7},{7,6},{8,9},{9,8},{10,11... | collective-permute-start | bytes 3244040 | tf_op jit(solution)/shard_map/ppermute | solution.py:264
  9.7 13.3 %collective-permute-start.1 = (f32[544,128]{1,0:T(8,128)S(1)}, f32[544,128]{1,0:T(8,128)S(1)}, u32[]{:S(2)}, u32[]{:S(2)}) collective-permute-start(f32[544,128]{1,0:T(8,128)S(1)} %get-tuple-element.38), channel_id=1, source_target_pairs={{0,4},{2,6},{4,0},{6,2},{1,5},{3,7},{5,1},{7,3},{8,12},{10,14},{12... | collective-permute-start | bytes 835592 | tf_op jit(solution)/shard_map/ppermute | solution.py:267
  11.0 10.2 %collective-permute-start.2 = (f32[72,512]{1,0:T(8,128)S(1)}, f32[72,512]{1,0:T(8,128)S(1)}, u32[]{:S(2)}, u32[]{:S(2)}) collective-permute-start(f32[72,512]{1,0:T(8,128)S(1)} %get-tuple-element.39), channel_id=1, source_target_pairs={{0,2},{2,0},{4,6},{6,4},{1,3},{3,1},{5,7},{7,5},{8,10},{10,8},{12,... | collective-permute-start | bytes 442376 | tf_op jit(solution)/shard_map/ppermute | solution.py:267
  11.4 11.7 %collective-permute-start.3 = (f32[72,512]{1,0:T(8,128)S(1)}, f32[72,512]{1,0:T(8,128)S(1)}, u32[]{:S(2)}, u32[]{:S(2)}) collective-permute-start(f32[72,512]{1,0:T(8,128)S(1)} %get-tuple-element.40), channel_id=1, source_target_pairs={{0,6},{2,4},{4,2},{6,0},{1,7},{3,5},{5,3},{7,1},{8,14},{10,12},{12... | collective-permute-start | bytes 442376 | tf_op jit(solution)/shard_map/ppermute | solution.py:267
  13.1 11.8 %collective-permute-start.4 = (f32[64,512]{1,0:T(8,128)S(1)}, f32[64,512]{1,0:T(8,128)S(1)}, u32[]{:S(2)}, u32[]{:S(2)}) collective-permute-start(f32[64,512]{1,0:T(8,128)S(1)} %get-tuple-element.41), channel_id=1, source_target_pairs={{0,2},{2,0},{4,6},{6,4},{1,3},{3,1},{5,7},{7,5},{8,10},{10,8},{12,... | collective-permute-start | bytes 393224 | tf_op jit(solution)/shard_map/ppermute | solution.py:267
  13.1 12.8 %collective-permute-start.5 = (f32[64,512]{1,0:T(8,128)S(1)}, f32[64,512]{1,0:T(8,128)S(1)}, u32[]{:S(2)}, u32[]{:S(2)}) collective-permute-start(f32[64,512]{1,0:T(8,128)S(1)} %get-tuple-element.45), channel_id=1, source_target_pairs={{0,6},{2,4},{4,2},{6,0},{1,7},{3,5},{5,3},{7,1},{8,14},{10,12},{12... | collective-permute-start | bytes 393224 | tf_op jit(solution)/shard_map/ppermute | solution.py:267
  26.1 6.2 %collective-permute-start.8 = (bf16[64,1024]{1,0:T(8,128)(2,1)S(1)}, bf16[64,1024]{1,0:T(8,128)(2,1)S(1)}, u32[]{:S(2)}, u32[]{:S(2)}) collective-permute-start(bf16[64,1024]{1,0:T(8,128)(2,1)S(1)} %get-tuple-element.52.low), channel_id=1, source_target_pairs={{0,4},{2,6},{4,0},{6,2},{1,5},{3,7},{5,1},{7,3},{8,12},{10,14},{12... | collective-permute-start | bytes 393224 | tf_op jit(solution)/shard_map/ppermute | solution.py:267
  28.5 5.2 %collective-permute-start.9 = (bf16[64,1024]{1,0:T(8,128)(2,1)S(1)}, bf16[64,1024]{1,0:T(8,128)(2,1)S(1)}, u32[]{:S(2)}, u32[]{:S(2)}) collective-permute-start(bf16[64,1024]{1,0:T(8,128)(2,1)S(1)} %get-tuple-element.52.low), channel_id=1, source_target_pairs={{0,1},{1,0},{2,3},{3,2},{4,5},{5,4},{6,7},{7,6},{8,9},{9,8},{10,11... | collective-permute-start | bytes 393224 | tf_op jit(solution)/shard_map/ppermute | solution.py:264
  29.3 5.2 %collective-permute-start.7 = (bf16[64,1024]{1,0:T(8,128)(2,1)S(1)}, bf16[64,1024]{1,0:T(8,128)(2,1)S(1)}, u32[]{:S(2)}, u32[]{:S(2)}) collective-permute-start(bf16[64,1024]{1,0:T(8,128)(2,1)S(1)} %get-tuple-element.52.low), channel_id=1, source_target_pairs={{0,2},{2,0},{4,6},{6,4},{1,3},{3,1},{5,7},{7,5},{8,10},{10,8},{12,... | collective-permute-start | bytes 393224 | tf_op jit(solution)/shard_map/ppermute | solution.py:267
  29.7 6.0 %collective-permute-start.6 = (bf16[64,1024]{1,0:T(8,128)(2,1)S(1)}, bf16[64,1024]{1,0:T(8,128)(2,1)S(1)}, u32[]{:S(2)}, u32[]{:S(2)}) collective-permute-start(bf16[64,1024]{1,0:T(8,128)(2,1)S(1)} %get-tuple-element.52.low), channel_id=1, source_target_pairs={{0,6},{2,4},{4,2},{6,0},{1,7},{3,5},{5,3},{7,1},{8,14},{10,12},{12... | collective-permute-start | bytes 393224 | tf_op jit(solution)/shard_map/ppermute | solution.py:267
  32.3 4.5 %collective-permute-start.11 = (bf16[64,1024]{1,0:T(8,128)(2,1)S(1)}, bf16[64,1024]{1,0:T(8,128)(2,1)S(1)}, u32[]{:S(2)}, u32[]{:S(2)}) collective-permute-start(bf16[64,1024]{1,0:T(8,128)(2,1)S(1)} %collective-permute-done.8.low2), channel_id=1, source_target_pairs={{0,1},{1,0},{2,3},{3,2},{4,5},{5,4},{6,7},{7,6},{8,9},{9,8},{10,11... | collective-permute-start | bytes 393224 | tf_op jit(solution)/shard_map/ppermute | solution.py:264
  34.5 2.3 %collective-permute-start.12 = (bf16[64,1024]{1,0:T(8,128)(2,1)S(1)}, bf16[64,1024]{1,0:T(8,128)(2,1)S(1)}, u32[]{:S(2)}, u32[]{:S(2)}) collective-permute-start(bf16[64,1024]{1,0:T(8,128)(2,1)S(1)} %collective-permute-done.7.low), channel_id=1, source_target_pairs={{0,1},{1,0},{2,3},{3,2},{4,5},{5,4},{6,7},{7,6},{8,9},{9,8},{10,11... | collective-permute-start | bytes 393224 | tf_op jit(solution)/shard_map/ppermute | solution.py:264
  35.7 2.2 %collective-permute-start.10 = (bf16[64,1024]{1,0:T(8,128)(2,1)S(1)}, bf16[64,1024]{1,0:T(8,128)(2,1)S(1)}, u32[]{:S(2)}, u32[]{:S(2)}) collective-permute-start(bf16[64,1024]{1,0:T(8,128)(2,1)S(1)} %collective-permute-done.6.low3), channel_id=1, source_target_pairs={{0,1},{1,0},{2,3},{3,2},{4,5},{5,4},{6,7},{7,6},{8,9},{9,8},{10,11... | collective-permute-start | bytes 393224 | tf_op jit(solution)/shard_map/ppermute | solution.py:264
  38.4 3.9 %collective-permute-start.13 = (f32[96,128]{1,0:T(8,128)S(1)}, f32[96,128]{1,0:T(8,128)S(1)}, u32[]{:S(2)}, u32[]{:S(2)}) collective-permute-start(f32[96,128]{1,0:T(8,128)S(1)} %get-tuple-element.57), channel_id=1, source_target_pairs={{0,8},{8,0},{16,24},{24,16},{1,9},{9,1},{17,25},{25,17},{2,10},{10... | collective-permute-start | bytes 147464 | tf_op jit(solution)/shard_map/ppermute | solution.py:346
  39.7 4.8 %collective-permute-start.14 = (f32[96,128]{1,0:T(8,128)S(1)}, f32[96,128]{1,0:T(8,128)S(1)}, u32[]{:S(2)}, u32[]{:S(2)}) collective-permute-start(f32[96,128]{1,0:T(8,128)S(1)} %get-tuple-element.58), channel_id=1, source_target_pairs={{0,16},{8,24},{16,0},{24,8},{1,17},{9,25},{17,1},{25,9},{2,18},{10... | collective-permute-start | bytes 147464 | tf_op jit(solution)/shard_map/ppermute | solution.py:346
  42.1 4.2 %collective-permute-start.15 = (f32[96,128]{1,0:T(8,128)S(1)}, f32[96,128]{1,0:T(8,128)S(1)}, u32[]{:S(2)}, u32[]{:S(2)}) collective-permute-start(f32[96,128]{1,0:T(8,128)S(1)} %get-tuple-element.59), channel_id=1, source_target_pairs={{0,24},{8,16},{16,8},{24,0},{1,25},{9,17},{17,9},{25,1},{2,26},{10... | collective-permute-start | bytes 147464 | tf_op jit(solution)/shard_map/ppermute | solution.py:346
  46.3 7.7 %collective-permute-start.16 = (f32[96,128]{1,0:T(8,128)S(1)}, f32[96,128]{1,0:T(8,128)S(1)}, u32[]{:S(2)}, u32[]{:S(2)}) collective-permute-start(f32[96,128]{1,0:T(8,128)S(1)} %add_add_fusion), channel_id=1, source_target_pairs={{0,192},{32,224},{64,128},{96,160},{128,64},{160,96},{192,0},{224,... | collective-permute-start | bytes 147464 | tf_op jit(solution)/shard_map/ppermute | solution.py:347
  54.0 4.8 %collective-permute-start.19 = (f32[96,128]{1,0:T(8,128)S(1)}, f32[96,128]{1,0:T(8,128)S(1)}, u32[]{:S(2)}, u32[]{:S(2)}) collective-permute-start(f32[96,128]{1,0:T(8,128)S(1)} %add.18.part0), channel_id=1, source_target_pairs={{0,96},{32,64},{64,32},{96,0},{128,224},{160,192},{192,160},{224,1... | collective-permute-start | bytes 147464 | tf_op jit(solution)/shard_map/ppermute | solution.py:348
  55.9 4.0 %collective-permute-start.18 = (f32[96,128]{1,0:T(8,128)S(1)}, f32[96,128]{1,0:T(8,128)S(1)}, u32[]{:S(2)}, u32[]{:S(2)}) collective-permute-start(f32[96,128]{1,0:T(8,128)S(1)} %add.18.part0), channel_id=1, source_target_pairs={{0,64},{32,96},{64,0},{96,32},{128,192},{160,224},{192,128},{224,1... | collective-permute-start | bytes 147464 | tf_op jit(solution)/shard_map/ppermute | solution.py:348
  55.9 3.9 %collective-permute-start.17 = (f32[96,128]{1,0:T(8,128)S(1)}, f32[96,128]{1,0:T(8,128)S(1)}, u32[]{:S(2)}, u32[]{:S(2)}) collective-permute-start(f32[96,128]{1,0:T(8,128)S(1)} %add.18.part0), channel_id=1, source_target_pairs={{0,32},{32,0},{64,96},{96,64},{128,160},{160,128},{192,224},{224,1... | collective-permute-start | bytes 147464 | tf_op jit(solution)/shard_map/ppermute | solution.py:348
  61.9 5.3 %collective-permute-start.20 = (f32[16,128]{1,0:T(8,128)S(1)}, f32[16,128]{1,0:T(8,128)S(1)}, u32[]{:S(2)}, u32[]{:S(2)}) collective-permute-start(f32[16,128]{1,0:T(8,128)S(1)} %get-tuple-element.61), channel_id=1, source_target_pairs={{0,1},{1,0},{2,3},{3,2},{4,5},{5,4},{6,7},{7,6},{8,9},{9,8},{10,11... | collective-permute-start | bytes 24584 | tf_op jit(solution)/shard_map/ppermute | solution.py:264

commit v9 on v8

--- a/solution.py
+++ b/solution.py
@@ -164,12 +164,12 @@
     return total
 
 
-def first_partial_kernel(low, keep_ref, link_ref, acc, link_out):
+def first_partial_kernel(low, keep_ref, acc):
+    acc[...] = times_blocks((low,), keep_ref, (0,))
+
+
+def second_partial_kernel(low2, low_other, keep_ref, send_ref, before, link_ref, acc, link_out):
     link_out[...] = link_ref[...]
-    acc[...] = times_blocks((low,), keep_ref, (0,))
-
-
-def second_partial_kernel(low2, low_other, keep_ref, send_ref, before, acc):
     acc[...] = before[...] + times_blocks((low2,), keep_ref, (2,)) + times_blocks((low_other,), send_ref, (0,))
 
 
@@ -319,16 +319,16 @@
     def after(one, acc):
         return lax.optimization_barrier((one, acc))[0]
 
-    acc, link = call(
-        first_partial_kernel,
-        (total, shape((RANK, 1024))),
-        (low, held_keep, link),
-        "partial_own",
-    )
+    acc = call(first_partial_kernel, total, (low, held_keep), "partial_own")
     low_other = other_core(after(low, acc))
     low2 = after(low2, acc)
     other2 = other_core(low2)
-    acc = call(second_partial_kernel, total, (low2, low_other, held_keep, held_send, acc), "partial_two")
+    acc, link = call(
+        second_partial_kernel,
+        (total, shape((RANK, 1024))),
+        (low2, low_other, held_keep, held_send, acc, link),
+        "partial_two",
+    )
     low1 = after(low1, acc)
     other1 = other_core(low1)
     acc = call(functools.partial(one_partial_kernel, 1), total, (low1, held_keep, acc), "partial_one")

time: 79.2 us -> 79.4 us (level)
    ppermute x3, waiting for transfers between devices: 3.96 us -> 3.13 us  [body(): lax.ppermute(outgoing[d], 'x', partners(4, d))]
    all_to_all x1, blocking collectives: 9.34 us -> 10.1 us  [body(): lax.all_to_all(jnp.broadcast_to(found[None], (16, 16, 128)), ('x', 'y'),...]
  transfers between devices with their start and end apart: 21 -> 21, of which waited for: 10 -> 11; matrix products, arithmetic and copies ran while one was open for 0% -> 0% of each run, Pallas kernels for 10% -> 10%
where the time goes in v9:
time: 79.4 us; the launch traced here: 79.2 us
  starting transfers between devices  33.3 us (42%)
  waiting for transfers between devices  18.4 us (23%)
  Pallas kernels  16.6 us (21%)
  blocking collectives  10.1 us (13%)
    pallas_call x13, Pallas kernels, call(): pl.pallas_call(kernel, out_shape=out_shape, in_specs=[pl.BlockSpec(memory...  16.6 us
    ppermute x6, starting transfers between devices, other_core(): return lax.ppermute(a, 'core', partners(2, 1))  11.5 us
    ppermute x8, waiting for transfers between devices, along_y(): return lax.ppermute(a, 'y', partners(4, d))  10.6 us
    all_to_all x1, blocking collectives, body(): lax.all_to_all(jnp.broadcast_to(found[None], (16, 16, 128)), ('x', 'y'),...  10.1 us
    ppermute x8, starting transfers between devices, along_y(): return lax.ppermute(a, 'y', partners(4, d))  8.19 us
    ppermute x1, starting transfers between devices, body(): over_pair = over_x + lax.ppermute(over_x, 'z', partners(8, 6))  6.1 us
    ppermute x3, starting transfers between devices, body(): lax.ppermute(outgoing[d], 'x', partners(4, d))  3.95 us
    ppermute x3, starting transfers between devices, body(): lax.ppermute(over_pair, 'z', partners(8, d))  3.63 us
  transfers between devices with their start and end apart: 21, of which 11 were waited for; matrix products, arithmetic and copies ran while one was open for 0% of the time, Pallas kernels for 10%

profile of v9, /device:TPU:1, one launch (start us, length us, event | category | flops | bytes accessed | tf_op | source)
XLA Modules:
  0.0 79.2 jit_solution(15203049710623126602)
XLA Ops:
  0.6 3.1 %sums_to_send.1 = (f32[264,1024]{1,0:T(8,128)S(1)}, bf16[4,512,1024]{2,1,0:T(8,128)(2,1)S(1)}, bf16[64,512]{1,0:T(8,128)(2,1)S(1)}, f32[16,128]{1,0:T(8,128)S(1)}) custom-call(bf16[512,8192]{1,0:T(8,128)(2,1)} %bitcast.2, f32[32,64]{1,0:T(8,128)} %interval_ref.1, f32[16,64]{1,0:T(8,128)} %day_ref.1), custom_call_target="tpu_custom_call" | custom-call | flops 1048576 | bytes 65536 | tf_op jit(solution)/shard_map/sums_to_send/pallas_call | solution.py:244
  3.7 3.3 %collective-permute-start = (f32[264,1024]{1,0:T(8,128)S(1)}, f32[264,1024]{1,0:T(8,128)S(1)}, u32[]{:S(2)}, u32[]{:S(2)}) collective-permute-start(f32[264,1024]{1,0:T(8,128)S(1)} %get-tuple-element.36.sent_ref), channel_id=1, source_target_pairs={{0,1},{1,0},{2,3},{3,2},{4,5},{5,4},{6,7},{7,6},{8,9},{9,8},{10,11... | collective-permute-start | bytes 3244040 | tf_op jit(solution)/shard_map/ppermute | solution.py:264
  7.0 2.5 %sums_to_keep.1 = (f32[4,64,1024]{2,1,0:T(8,128)S(1)}, bf16[4,512,1024]{2,1,0:T(8,128)(2,1)S(1)}) custom-call(bf16[512,8192]{1,0:T(8,128)(2,1)} %bitcast.3, bf16[64,512]{1,0:T(8,128)(2,1)S(1)} %get-tuple-element.34.khatri_ref), custom_call_target="tpu_custom_call" | custom-call | flops 1048576 | bytes 65536 | tf_op jit(solution)/shard_map/sums_to_keep/pallas_call | solution.py:244
  9.6 0.2 add_cores.1
  9.7 1.3 %collective-permute-start.1 = (f32[544,128]{1,0:T(8,128)S(1)}, f32[544,128]{1,0:T(8,128)S(1)}, u32[]{:S(2)}, u32[]{:S(2)}) collective-permute-start(f32[544,128]{1,0:T(8,128)S(1)} %get-tuple-element.38), channel_id=1, source_target_pairs={{0,4},{2,6},{4,0},{6,2},{1,5},{3,7},{5,1},{7,3},{8,12},{10,14},{12... | collective-permute-start | bytes 835592 | tf_op jit(solution)/shard_map/ppermute | solution.py:267
  11.0 0.4 collective-permute-start.2
  11.4 1.7 %collective-permute-start.3 = (f32[72,512]{1,0:T(8,128)S(1)}, f32[72,512]{1,0:T(8,128)S(1)}, u32[]{:S(2)}, u32[]{:S(2)}) collective-permute-start(f32[72,512]{1,0:T(8,128)S(1)} %get-tuple-element.40), channel_id=1, source_target_pairs={{0,6},{2,4},{4,2},{6,0},{1,7},{3,5},{5,3},{7,1},{8,14},{10,12},{12... | collective-permute-start | bytes 442376 | tf_op jit(solution)/shard_map/ppermute | solution.py:267
  13.1 0.0 collective-permute-start.4
  13.1 1.5 %collective-permute-start.5 = (f32[64,512]{1,0:T(8,128)S(1)}, f32[64,512]{1,0:T(8,128)S(1)}, u32[]{:S(2)}, u32[]{:S(2)}) collective-permute-start(f32[64,512]{1,0:T(8,128)S(1)} %get-tuple-element.45), channel_id=1, source_target_pairs={{0,6},{2,4},{4,2},{6,0},{1,7},{3,5},{5,3},{7,1},{8,14},{10,12},{12... | collective-permute-start | bytes 393224 | tf_op jit(solution)/shard_map/ppermute | solution.py:267
  14.6 6.7 %collective-permute-done.2.one.one_a = f32[72,512]{1,0:T(8,128)S(1)} collective-permute-done((f32[72,512]{1,0:T(8,128)S(1)}, f32[72,512]{1,0:T(8,128)S(1)}, u32[]{:S(2)}, u32[]{:S(2)}) %collective-permute-start.2) | collective-permute-done | bytes 147488 | tf_op jit(solution)/shard_map/ppermute | solution.py:267
  21.2 1.8 %collective-permute-done.3.three.three_a = f32[72,512]{1,0:T(8,128)S(1)} collective-permute-done((f32[72,512]{1,0:T(8,128)S(1)}, f32[72,512]{1,0:T(8,128)S(1)}, u32[]{:S(2)}, u32[]{:S(2)}) %collective-permute-start.3) | collective-permute-done | bytes 147488 | tf_op jit(solution)/shard_map/ppermute | solution.py:267
  23.1 1.8 %link_inverse.1 = (f32[64,64]{1,0:T(8,128)S(1)}, f32[64,64]{1,0:T(8,128)S(1)}) custom-call(f32[8,512]{1,0:T(8,128)S(1)} %get-tuple-element.42.own, f32[544,128]{1,0:T(8,128)S(1)} %collective-permute-done.1.two, f32[72,512]{1,0:T(8,128)S(1)} %collective-permute-done.2.one.one_a, f32[72,512]{1,0:T(8,128)S(1)} %collective-permute-done.3.three.three_a, ...), custom_call_target="tpu_custom_call" | custom-call | flops 1048576 | bytes 65536 | tf_op jit(solution)/shard_map/link_inverse/pallas_call | solution.py:244
  24.9 0.0 collective-permute-done.4.one_b
  24.9 0.4 most_of_link_rows.1.before
  25.3 0.6 collective-permute-done.5.three_b
  25.9 0.3 link_rows.1
  26.1 1.3 %collective-permute-start.6 = (bf16[64,1024]{1,0:T(8,128)(2,1)S(1)}, bf16[64,1024]{1,0:T(8,128)(2,1)S(1)}, u32[]{:S(2)}, u32[]{:S(2)}) collective-permute-start(bf16[64,1024]{1,0:T(8,128)(2,1)S(1)} %get-tuple-element.49.low), channel_id=1, source_target_pairs={{0,4},{2,6},{4,0},{6,2},{1,5},{3,7},{5,1},{7,3},{8,12},{10,14},{12... | collective-permute-start | bytes 393224 | tf_op jit(solution)/shard_map/ppermute | solution.py:267
  27.4 0.5 partial_own.1.before
  27.9 0.9 %collective-permute-start.7 = (bf16[64,1024]{1,0:T(8,128)(2,1)S(1)}, bf16[64,1024]{1,0:T(8,128)(2,1)S(1)}, u32[]{:S(2)}, u32[]{:S(2)}) collective-permute-start(bf16[64,1024]{1,0:T(8,128)(2,1)S(1)} %get-tuple-element.49.low), channel_id=1, source_target_pairs={{0,1},{1,0},{2,3},{3,2},{4,5},{5,4},{6,7},{7,6},{8,9},{9,8},{10,11... | collective-permute-start | bytes 393224 | tf_op jit(solution)/shard_map/ppermute | solution.py:264
  28.7 0.4 collective-permute-start.9
  29.1 1.7 %collective-permute-start.8 = (bf16[64,1024]{1,0:T(8,128)(2,1)S(1)}, bf16[64,1024]{1,0:T(8,128)(2,1)S(1)}, u32[]{:S(2)}, u32[]{:S(2)}) collective-permute-start(bf16[64,1024]{1,0:T(8,128)(2,1)S(1)} %get-tuple-element.49.low), channel_id=1, source_target_pairs={{0,6},{2,4},{4,2},{6,0},{1,7},{3,5},{5,3},{7,1},{8,14},{10,12},{12... | collective-permute-start | bytes 393224 | tf_op jit(solution)/shard_map/ppermute | solution.py:267
  30.8 1.5 %collective-permute-done.6.low2 = bf16[64,1024]{1,0:T(8,128)(2,1)S(1)} collective-permute-done((bf16[64,1024]{1,0:T(8,128)(2,1)S(1)}, bf16[64,1024]{1,0:T(8,128)(2,1)S(1)}, u32[]{:S(2)}, u32[]{:S(2)}) %collective-permute-start.6) | collective-permute-done | bytes 131104 | tf_op jit(solution)/shard_map/ppermute | solution.py:267
  32.3 2.0 %collective-permute-start.11 = (bf16[64,1024]{1,0:T(8,128)(2,1)S(1)}, bf16[64,1024]{1,0:T(8,128)(2,1)S(1)}, u32[]{:S(2)}, u32[]{:S(2)}) collective-permute-start(bf16[64,1024]{1,0:T(8,128)(2,1)S(1)} %collective-permute-done.6.low2), channel_id=1, source_target_pairs={{0,1},{1,0},{2,3},{3,2},{4,5},{5,4},{6,7},{7,6},{8,9},{9,8},{10,11... | collective-permute-start | bytes 393224 | tf_op jit(solution)/shard_map/ppermute | solution.py:264
  34.3 0.0 collective-permute-done.7.low_other
  34.3 1.4 %partial_two.1 = (f32[288,128]{1,0:T(8,128)S(1)}, f32[64,1024]{1,0:T(8,128)}) custom-call(bf16[64,1024]{1,0:T(8,128)(2,1)S(1)} %collective-permute-done.6.low2, bf16[64,1024]{1,0:T(8,128)(2,1)S(1)} %collective-permute-done.7.low_other, bf16[4,512,1024]{2,1,0:T(8,128)(2,1)S(1)} %get-tuple-element.47.keep_ref, ...), custom_call_target="tpu_custom_call" | custom-call | flops 1048576 | bytes 65536 | tf_op jit(solution)/shard_map/partial_two/pallas_call | solution.py:244
  35.7 0.0 collective-permute-start.12
  35.7 0.5 partial_one.1.before
  36.2 0.8 collective-permute-start.10
  37.0 0.1 collective-permute-done.12.other1
  37.1 1.1 %partial_mixed.1.before = f32[288,128]{1,0:T(8,128)S(1)} custom-call(bf16[64,1024]{1,0:T(8,128)(2,1)S(1)} %collective-permute-done.8.low3, bf16[64,1024]{1,0:T(8,128)(2,1)S(1)} %collective-permute-done.11.other2, bf16[64,1024]{1,0:T(8,128)(2,1)S(1)} %collective-permute-done.12.other1, bf16[4,512,1024]{2,1,0:T(8,128)(2,1)S(1)} %get-tuple-element.47.keep_ref, ...), custom_call_target="tpu_custom_call" | custom-call | flops 1048576 | bytes 65536 | tf_op jit(solution)/shard_map/partial_mixed/pallas_call | solution.py:244
  38.2 0.5 partial_last.1
  38.7 0.5 collective-permute-start.13
  39.1 2.5 %collective-permute-start.14 = (f32[96,128]{1,0:T(8,128)S(1)}, f32[96,128]{1,0:T(8,128)S(1)}, u32[]{:S(2)}, u32[]{:S(2)}) collective-permute-start(f32[96,128]{1,0:T(8,128)S(1)} %get-tuple-element.58), channel_id=1, source_target_pairs={{0,16},{8,24},{16,0},{24,8},{1,17},{9,25},{17,1},{25,9},{2,18},{10... | collective-permute-start | bytes 147464 | tf_op jit(solution)/shard_map/ppermute | solution.py:346
  41.6 1.0 %collective-permute-start.15 = (f32[96,128]{1,0:T(8,128)S(1)}, f32[96,128]{1,0:T(8,128)S(1)}, u32[]{:S(2)}, u32[]{:S(2)}) collective-permute-start(f32[96,128]{1,0:T(8,128)S(1)} %get-tuple-element.59), channel_id=1, source_target_pairs={{0,24},{8,16},{16,8},{24,0},{1,25},{9,17},{17,9},{25,1},{2,26},{10... | collective-permute-start | bytes 147464 | tf_op jit(solution)/shard_map/ppermute | solution.py:346
  42.6 1.4 %collective-permute-done.14 = f32[96,128]{1,0:T(8,128)S(1)} collective-permute-done((f32[96,128]{1,0:T(8,128)S(1)}, f32[96,128]{1,0:T(8,128)S(1)}, u32[]{:S(2)}, u32[]{:S(2)}) %collective-permute-start.14) | collective-permute-done | bytes 49184 | tf_op jit(solution)/shard_map/ppermute | solution.py:346
  44.0 1.8 %collective-permute-done.15 = f32[96,128]{1,0:T(8,128)S(1)} collective-permute-done((f32[96,128]{1,0:T(8,128)S(1)}, f32[96,128]{1,0:T(8,128)S(1)}, u32[]{:S(2)}, u32[]{:S(2)}) %collective-permute-start.15) | collective-permute-done | bytes 49184 | tf_op jit(solution)/shard_map/ppermute | solution.py:346
  45.7 6.1 %collective-permute-start.16 = (f32[96,128]{1,0:T(8,128)S(1)}, f32[96,128]{1,0:T(8,128)S(1)}, u32[]{:S(2)}, u32[]{:S(2)}) collective-permute-start(f32[96,128]{1,0:T(8,128)S(1)} %add_add_fusion), channel_id=1, source_target_pairs={{0,192},{32,224},{64,128},{96,160},{128,64},{160,96},{192,0},{224,... | collective-permute-start | bytes 147464 | tf_op jit(solution)/shard_map/ppermute | solution.py:347
  51.8 1.6 %collective-permute-done.16 = f32[96,128]{1,0:T(8,128)S(1)} collective-permute-done((f32[96,128]{1,0:T(8,128)S(1)}, f32[96,128]{1,0:T(8,128)S(1)}, u32[]{:S(2)}, u32[]{:S(2)}) %collective-permute-start.16) | collective-permute-done | bytes 49184 | tf_op jit(solution)/shard_map/ppermute | solution.py:347
  53.4 1.9 %collective-permute-start.19 = (f32[96,128]{1,0:T(8,128)S(1)}, f32[96,128]{1,0:T(8,128)S(1)}, u32[]{:S(2)}, u32[]{:S(2)}) collective-permute-start(f32[96,128]{1,0:T(8,128)S(1)} %add.18.part0), channel_id=1, source_target_pairs={{0,96},{32,64},{64,32},{96,0},{128,224},{160,192},{192,160},{224,1... | collective-permute-start | bytes 147464 | tf_op jit(solution)/shard_map/ppermute | solution.py:348
  55.3 0.0 collective-permute-start.18
  55.4 1.7 %collective-permute-start.17 = (f32[96,128]{1,0:T(8,128)S(1)}, f32[96,128]{1,0:T(8,128)S(1)}, u32[]{:S(2)}, u32[]{:S(2)}) collective-permute-start(f32[96,128]{1,0:T(8,128)S(1)} %add.18.part0), channel_id=1, source_target_pairs={{0,32},{32,0},{64,96},{96,64},{128,160},{160,128},{192,224},{224,1... | collective-permute-start | bytes 147464 | tf_op jit(solution)/shard_map/ppermute | solution.py:348
  57.1 1.2 %collective-permute-done.19.part3 = f32[96,128]{1,0:T(8,128)S(1)} collective-permute-done((f32[96,128]{1,0:T(8,128)S(1)}, f32[96,128]{1,0:T(8,128)S(1)}, u32[]{:S(2)}, u32[]{:S(2)}) %collective-permute-start.19) | collective-permute-done | bytes 49184 | tf_op jit(solution)/shard_map/ppermute | solution.py:348
  58.3 1.0 %collective-permute-done.18.part2 = f32[96,128]{1,0:T(8,128)S(1)} collective-permute-done((f32[96,128]{1,0:T(8,128)S(1)}, f32[96,128]{1,0:T(8,128)S(1)}, u32[]{:S(2)}, u32[]{:S(2)}) %collective-permute-start.18) | collective-permute-done | bytes 49184 | tf_op jit(solution)/shard_map/ppermute | solution.py:348
  59.3 2.0 %interval_rows.1 = (f32[16,128]{1,0:T(8,128)S(1)}, f32[64,64]{1,0:T(8,128)S(1)}) custom-call(f32[96,128]{1,0:T(8,128)S(1)} %add.18.part0, f32[96,128]{1,0:T(8,128)S(1)} %collective-permute-done.17.part1, f32[96,128]{1,0:T(8,128)S(1)} %collective-permute-done.18.part2, f32[96,128]{1,0:T(8,128)S(1)} %collective-permute-done.19.part3, ...), custom_call_target="tpu_custom_call" | custom-call | flops 1048576 | bytes 65536 | tf_op jit(solution)/shard_map/interval_rows/pallas_call | solution.py:244
  61.3 4.5 %collective-permute-start.20 = (f32[16,128]{1,0:T(8,128)S(1)}, f32[16,128]{1,0:T(8,128)S(1)}, u32[]{:S(2)}, u32[]{:S(2)}) collective-permute-start(f32[16,128]{1,0:T(8,128)S(1)} %get-tuple-element.61), channel_id=1, source_target_pairs={{0,1},{1,0},{2,3},{3,2},{4,5},{5,4},{6,7},{7,6},{8,9},{9,8},{10,11... | collective-permute-start | bytes 24584 | tf_op jit(solution)/shard_map/ppermute | solution.py:264
  65.8 0.8 %collective-permute-done.20 = f32[16,128]{1,0:T(8,128)S(1)} collective-permute-done((f32[16,128]{1,0:T(8,128)S(1)}, f32[16,128]{1,0:T(8,128)S(1)}, u32[]{:S(2)}, u32[]{:S(2)}) %collective-permute-start.20) | collective-permute-done | bytes 8224 | tf_op jit(solution)/shard_map/ppermute | solution.py:264
  66.6 10.1 %all_to_all.5.recv_ref = f32[16,16,128]{2,1,0:T(8,128)S(1)} all-to-all(f32[16,16,128]{2,1,0:T(8,128)S(1)} %broadcast_in_dim.2), channel_id=1, replica_groups=mesh['z'=8,'x'=4,'y'=4,'core'=2] {'x','y'}, dimensions={0} | all-to-all | bytes 262144 | tf_op jit(solution)/shard_map/all_to_all | solution.py:356
  76.8 2.4 %day_rows.1 = (f32[32,64]{1,0:T(8,128)}, f32[16,64]{1,0:T(8,128)}) custom-call(f32[16,16,128]{2,1,0:T(8,128)S(1)} %all_to_all.5.recv_ref, f32[64,64]{1,0:T(8,128)S(1)} %get-tuple-element.62.gram_ref), custom_call_target="tpu_custom_call" | custom-call | flops 1048576 | bytes 65536 | tf_op jit(solution)/shard_map/day_rows/pallas_call | solution.py:244
  (12 shorter events, 0.1 us)
Async XLA Ops:
  3.7 5.9 %collective-permute-start = (f32[264,1024]{1,0:T(8,128)S(1)}, f32[264,1024]{1,0:T(8,128)S(1)}, u32[]{:S(2)}, u32[]{:S(2)}) collective-permute-start(f32[264,1024]{1,0:T(8,128)S(1)} %get-tuple-element.36.sent_ref), channel_id=1, source_target_pairs={{0,1},{1,0},{2,3},{3,2},{4,5},{5,4},{6,7},{7,6},{8,9},{9,8},{10,11... | collective-permute-start | bytes 3244040 | tf_op jit(solution)/shard_map/ppermute | solution.py:264
  9.7 13.3 %collective-permute-start.1 = (f32[544,128]{1,0:T(8,128)S(1)}, f32[544,128]{1,0:T(8,128)S(1)}, u32[]{:S(2)}, u32[]{:S(2)}) collective-permute-start(f32[544,128]{1,0:T(8,128)S(1)} %get-tuple-element.38), channel_id=1, source_target_pairs={{0,4},{2,6},{4,0},{6,2},{1,5},{3,7},{5,1},{7,3},{8,12},{10,14},{12... | collective-permute-start | bytes 835592 | tf_op jit(solution)/shard_map/ppermute | solution.py:267
  11.0 10.2 %collective-permute-start.2 = (f32[72,512]{1,0:T(8,128)S(1)}, f32[72,512]{1,0:T(8,128)S(1)}, u32[]{:S(2)}, u32[]{:S(2)}) collective-permute-start(f32[72,512]{1,0:T(8,128)S(1)} %get-tuple-element.39), channel_id=1, source_target_pairs={{0,2},{2,0},{4,6},{6,4},{1,3},{3,1},{5,7},{7,5},{8,10},{10,8},{12,... | collective-permute-start | bytes 442376 | tf_op jit(solution)/shard_map/ppermute | solution.py:267
  11.4 11.7 %collective-permute-start.3 = (f32[72,512]{1,0:T(8,128)S(1)}, f32[72,512]{1,0:T(8,128)S(1)}, u32[]{:S(2)}, u32[]{:S(2)}) collective-permute-start(f32[72,512]{1,0:T(8,128)S(1)} %get-tuple-element.40), channel_id=1, source_target_pairs={{0,6},{2,4},{4,2},{6,0},{1,7},{3,5},{5,3},{7,1},{8,14},{10,12},{12... | collective-permute-start | bytes 442376 | tf_op jit(solution)/shard_map/ppermute | solution.py:267
  13.1 11.8 %collective-permute-start.4 = (f32[64,512]{1,0:T(8,128)S(1)}, f32[64,512]{1,0:T(8,128)S(1)}, u32[]{:S(2)}, u32[]{:S(2)}) collective-permute-start(f32[64,512]{1,0:T(8,128)S(1)} %get-tuple-element.41), channel_id=1, source_target_pairs={{0,2},{2,0},{4,6},{6,4},{1,3},{3,1},{5,7},{7,5},{8,10},{10,8},{12,... | collective-permute-start | bytes 393224 | tf_op jit(solution)/shard_map/ppermute | solution.py:267
  13.1 12.8 %collective-permute-start.5 = (f32[64,512]{1,0:T(8,128)S(1)}, f32[64,512]{1,0:T(8,128)S(1)}, u32[]{:S(2)}, u32[]{:S(2)}) collective-permute-start(f32[64,512]{1,0:T(8,128)S(1)} %get-tuple-element.45), channel_id=1, source_target_pairs={{0,6},{2,4},{4,2},{6,0},{1,7},{3,5},{5,3},{7,1},{8,14},{10,12},{12... | collective-permute-start | bytes 393224 | tf_op jit(solution)/shard_map/ppermute | solution.py:267
  26.1 6.2 %collective-permute-start.6 = (bf16[64,1024]{1,0:T(8,128)(2,1)S(1)}, bf16[64,1024]{1,0:T(8,128)(2,1)S(1)}, u32[]{:S(2)}, u32[]{:S(2)}) collective-permute-start(bf16[64,1024]{1,0:T(8,128)(2,1)S(1)} %get-tuple-element.49.low), channel_id=1, source_target_pairs={{0,4},{2,6},{4,0},{6,2},{1,5},{3,7},{5,1},{7,3},{8,12},{10,14},{12... | collective-permute-start | bytes 393224 | tf_op jit(solution)/shard_map/ppermute | solution.py:267
  27.9 6.4 %collective-permute-start.7 = (bf16[64,1024]{1,0:T(8,128)(2,1)S(1)}, bf16[64,1024]{1,0:T(8,128)(2,1)S(1)}, u32[]{:S(2)}, u32[]{:S(2)}) collective-permute-start(bf16[64,1024]{1,0:T(8,128)(2,1)S(1)} %get-tuple-element.49.low), channel_id=1, source_target_pairs={{0,1},{1,0},{2,3},{3,2},{4,5},{5,4},{6,7},{7,6},{8,9},{9,8},{10,11... | collective-permute-start | bytes 393224 | tf_op jit(solution)/shard_map/ppermute | solution.py:264
  28.7 7.0 %collective-permute-start.9 = (bf16[64,1024]{1,0:T(8,128)(2,1)S(1)}, bf16[64,1024]{1,0:T(8,128)(2,1)S(1)}, u32[]{:S(2)}, u32[]{:S(2)}) collective-permute-start(bf16[64,1024]{1,0:T(8,128)(2,1)S(1)} %get-tuple-element.49.low), channel_id=1, source_target_pairs={{0,2},{2,0},{4,6},{6,4},{1,3},{3,1},{5,7},{7,5},{8,10},{10,8},{12,... | collective-permute-start | bytes 393224 | tf_op jit(solution)/shard_map/ppermute | solution.py:267
  29.1 7.1 %collective-permute-start.8 = (bf16[64,1024]{1,0:T(8,128)(2,1)S(1)}, bf16[64,1024]{1,0:T(8,128)(2,1)S(1)}, u32[]{:S(2)}, u32[]{:S(2)}) collective-permute-start(bf16[64,1024]{1,0:T(8,128)(2,1)S(1)} %get-tuple-element.49.low), channel_id=1, source_target_pairs={{0,6},{2,4},{4,2},{6,0},{1,7},{3,5},{5,3},{7,1},{8,14},{10,12},{12... | collective-permute-start | bytes 393224 | tf_op jit(solution)/shard_map/ppermute | solution.py:267
  32.3 4.7 %collective-permute-start.11 = (bf16[64,1024]{1,0:T(8,128)(2,1)S(1)}, bf16[64,1024]{1,0:T(8,128)(2,1)S(1)}, u32[]{:S(2)}, u32[]{:S(2)}) collective-permute-start(bf16[64,1024]{1,0:T(8,128)(2,1)S(1)} %collective-permute-done.6.low2), channel_id=1, source_target_pairs={{0,1},{1,0},{2,3},{3,2},{4,5},{5,4},{6,7},{7,6},{8,9},{9,8},{10,11... | collective-permute-start | bytes 393224 | tf_op jit(solution)/shard_map/ppermute | solution.py:264
  35.7 1.3 %collective-permute-start.12 = (bf16[64,1024]{1,0:T(8,128)(2,1)S(1)}, bf16[64,1024]{1,0:T(8,128)(2,1)S(1)}, u32[]{:S(2)}, u32[]{:S(2)}) collective-permute-start(bf16[64,1024]{1,0:T(8,128)(2,1)S(1)} %collective-permute-done.9.low), channel_id=1, source_target_pairs={{0,1},{1,0},{2,3},{3,2},{4,5},{5,4},{6,7},{7,6},{8,9},{9,8},{10,11... | collective-permute-start | bytes 393224 | tf_op jit(solution)/shard_map/ppermute | solution.py:264
  36.2 1.9 %collective-permute-start.10 = (bf16[64,1024]{1,0:T(8,128)(2,1)S(1)}, bf16[64,1024]{1,0:T(8,128)(2,1)S(1)}, u32[]{:S(2)}, u32[]{:S(2)}) collective-permute-start(bf16[64,1024]{1,0:T(8,128)(2,1)S(1)} %collective-permute-done.8.low3), channel_id=1, source_target_pairs={{0,1},{1,0},{2,3},{3,2},{4,5},{5,4},{6,7},{7,6},{8,9},{9,8},{10,11... | collective-permute-start | bytes 393224 | tf_op jit(solution)/shard_map/ppermute | solution.py:264
  38.7 3.9 %collective-permute-start.13 = (f32[96,128]{1,0:T(8,128)S(1)}, f32[96,128]{1,0:T(8,128)S(1)}, u32[]{:S(2)}, u32[]{:S(2)}) collective-permute-start(f32[96,128]{1,0:T(8,128)S(1)} %get-tuple-element.57), channel_id=1, source_target_pairs={{0,8},{8,0},{16,24},{24,16},{1,9},{9,1},{17,25},{25,17},{2,10},{10... | collective-permute-start | bytes 147464 | tf_op jit(solution)/shard_map/ppermute | solution.py:346
  39.1 4.8 %collective-permute-start.14 = (f32[96,128]{1,0:T(8,128)S(1)}, f32[96,128]{1,0:T(8,128)S(1)}, u32[]{:S(2)}, u32[]{:S(2)}) collective-permute-start(f32[96,128]{1,0:T(8,128)S(1)} %get-tuple-element.58), channel_id=1, source_target_pairs={{0,16},{8,24},{16,0},{24,8},{1,17},{9,25},{17,1},{25,9},{2,18},{10... | collective-permute-start | bytes 147464 | tf_op jit(solution)/shard_map/ppermute | solution.py:346
  41.6 4.2 %collective-permute-start.15 = (f32[96,128]{1,0:T(8,128)S(1)}, f32[96,128]{1,0:T(8,128)S(1)}, u32[]{:S(2)}, u32[]{:S(2)}) collective-permute-start(f32[96,128]{1,0:T(8,128)S(1)} %get-tuple-element.59), channel_id=1, source_target_pairs={{0,24},{8,16},{16,8},{24,0},{1,25},{9,17},{17,9},{25,1},{2,26},{10... | collective-permute-start | bytes 147464 | tf_op jit(solution)/shard_map/ppermute | solution.py:346
  45.7 7.7 %collective-permute-start.16 = (f32[96,128]{1,0:T(8,128)S(1)}, f32[96,128]{1,0:T(8,128)S(1)}, u32[]{:S(2)}, u32[]{:S(2)}) collective-permute-start(f32[96,128]{1,0:T(8,128)S(1)} %add_add_fusion), channel_id=1, source_target_pairs={{0,192},{32,224},{64,128},{96,160},{128,64},{160,96},{192,0},{224,... | collective-permute-start | bytes 147464 | tf_op jit(solution)/shard_map/ppermute | solution.py:347
  53.4 4.8 %collective-permute-start.19 = (f32[96,128]{1,0:T(8,128)S(1)}, f32[96,128]{1,0:T(8,128)S(1)}, u32[]{:S(2)}, u32[]{:S(2)}) collective-permute-start(f32[96,128]{1,0:T(8,128)S(1)} %add.18.part0), channel_id=1, source_target_pairs={{0,96},{32,64},{64,32},{96,0},{128,224},{160,192},{192,160},{224,1... | collective-permute-start | bytes 147464 | tf_op jit(solution)/shard_map/ppermute | solution.py:348
  55.3 4.0 %collective-permute-start.18 = (f32[96,128]{1,0:T(8,128)S(1)}, f32[96,128]{1,0:T(8,128)S(1)}, u32[]{:S(2)}, u32[]{:S(2)}) collective-permute-start(f32[96,128]{1,0:T(8,128)S(1)} %add.18.part0), channel_id=1, source_target_pairs={{0,64},{32,96},{64,0},{96,32},{128,192},{160,224},{192,128},{224,1... | collective-permute-start | bytes 147464 | tf_op jit(solution)/shard_map/ppermute | solution.py:348
  55.4 3.9 %collective-permute-start.17 = (f32[96,128]{1,0:T(8,128)S(1)}, f32[96,128]{1,0:T(8,128)S(1)}, u32[]{:S(2)}, u32[]{:S(2)}) collective-permute-start(f32[96,128]{1,0:T(8,128)S(1)} %add.18.part0), channel_id=1, source_target_pairs={{0,32},{32,0},{64,96},{96,64},{128,160},{160,128},{192,224},{224,1... | collective-permute-start | bytes 147464 | tf_op jit(solution)/shard_map/ppermute | solution.py:348
  61.3 5.3 %collective-permute-start.20 = (f32[16,128]{1,0:T(8,128)S(1)}, f32[16,128]{1,0:T(8,128)S(1)}, u32[]{:S(2)}, u32[]{:S(2)}) collective-permute-start(f32[16,128]{1,0:T(8,128)S(1)} %get-tuple-element.61), channel_id=1, source_target_pairs={{0,1},{1,0},{2,3},{3,2},{4,5},{5,4},{6,7},{7,6},{8,9},{9,8},{10,11... | collective-permute-start | bytes 24584 | tf_op jit(solution)/shard_map/ppermute | solution.py:264
